TPU v7x, 128 devices: a whole 4x4x4 slice. The times are simulated.
128 devices in a mesh: ctx: 32 (over z_lo, y, x), tok: 4 (over z_hi, core).
Axes of the slice: x: 4, y: 4, z: 4 (z_hi: 2, z_lo: 2; z = z_hi * 2 + z_lo), core: 2. Of those that a mesh axis runs over, the one named last changes fastest.
Arguments:
- frames: bfloat16 [65536, 512], P('ctx'), may hold values from -128 to 128
- tokens: bfloat16 [8192, 512], P('tok'), may hold values from -12 to 12
- frame_mass: float32 [65536], P('ctx'), may hold values from 0.25 to 12
- token_mass: float32 [8192], P('tok'), may hold values from 0.25 to 12
Outputs:
- frame_map: bfloat16 [65536, 512], P('ctx')
- token_map: bfloat16 [8192, 512], P('tok')
- mass_ratio: float32 [65536], P('ctx')
All inputs are finite; a program needn't handle non-finite values.
Results may differ from a plain program's by a relative error of at most 0.0047.
Values may be sent and summed in bfloat16 or wider, within the bound.
No kernel may reach another device: no remote copies, remote signals or barrier semaphores. Data moves between devices by JAX's collectives and lax.ppermute only.
A program may use at most 128 MiB of HBM per device.

v0:
```python
import math

import jax
import jax.numpy as jnp
from jax import lax
from jax.sharding import PartitionSpec as P

ITERS = 2


def row_logsum(shifted):
    highest = lax.pmax(jnp.max(shifted, axis=1), "tok")
    summed = lax.psum(jnp.sum(jnp.exp(shifted - highest[:, None]), axis=1), "tok")
    return highest + jnp.log(summed)


def col_logsum(shifted):
    highest = lax.pmax(jnp.max(shifted, axis=0), "ctx")
    summed = lax.psum(jnp.sum(jnp.exp(shifted - highest[None, :]), axis=0), "ctx")
    return highest + jnp.log(summed)


def shards(frames, tokens, frame_mass, token_mass):
    score_scale = 1.0 / math.sqrt(frames.shape[1])
    frame_whole_mass = lax.psum(jnp.sum(frame_mass), "ctx")
    token_whole_mass = lax.psum(jnp.sum(token_mass), "tok")
    frame_share = frame_mass / frame_whole_mass
    log_frame = jnp.log(frame_share)
    log_token = jnp.log(token_mass / token_whole_mass)
    scores = (
        lax.dot_general(
            frames, tokens, (((1,), (1,)), ((), ())), preferred_element_type=jnp.float32
        )
        * score_scale
    )
    token_pot = jnp.zeros((tokens.shape[0],), jnp.float32)
    frame_pot = jnp.zeros((frames.shape[0],), jnp.float32)
    for step_index in range(ITERS):
        frame_pot = log_frame - row_logsum(scores + token_pot[None, :])
        token_pot = log_token - col_logsum(scores + frame_pot[:, None])
    weights = jnp.exp(scores + frame_pot[:, None] + token_pot[None, :])
    row_part = jnp.sum(weights, axis=1)
    col_part = jnp.sum(weights, axis=0)
    transport = weights.astype(jnp.bfloat16)
    frame_whole, row_sum = lax.psum(
        (jnp.dot(transport, tokens, preferred_element_type=jnp.float32), row_part), "tok"
    )
    frame_map = (frame_whole / row_sum[:, None]).astype(jnp.bfloat16)
    token_part = lax.dot_general(
        transport, frames, (((0,), (0,)), ((), ())), preferred_element_type=jnp.float32
    )
    token_whole, col_sum = lax.psum((token_part, col_part), "ctx")
    token_map = (token_whole / col_sum[:, None]).astype(jnp.bfloat16)
    mass_ratio = row_sum / frame_share
    return (frame_map, token_map, mass_ratio)


def solution(mesh):
    return jax.shard_map(
        shards,
        mesh=mesh,
        in_specs=(P("ctx", None), P("tok", None), P("ctx"), P("tok")),
        out_specs=(P("ctx", None), P("tok", None), P("ctx")),
        check_vma=False,
    )
```

profile of v0, /device:TPU:0, one launch (start us, length us, event | category | flops | bytes accessed | tf_op | source)
XLA Modules:
  0.0 949.3 jit_solution(17012778144841033214)
XLA Ops:
  7.2 0.0 copy-start
  7.2 0.0 all-reduce.4.cloned.1.call-start
  7.2 1.4 reduce_sum.72
  8.7 84.1 %psum.70 = f32[]{:T(128)} all-reduce(f32[]{:T(128)} %reduce_sum.72), channel_id=1, replica_groups=mesh['ctx'=32,'tok'=4] {'ctx'}, use_global_device_ids=true, to_apply=%region_1.0 | all-reduce | flops 1 | bytes 8 | tf_op jit(solution)/shard_map/psum | solution.py:25
  92.7 1.3 reduce_sum.73
  94.0 0.0 copy-done
  94.0 0.0 copy-start.2
  94.0 9.7 %fusion.3 = (f32[2048]{0:T(1024)S(1)}, f32[2048,2048]{1,0:T(8,128)}) fusion(bf16[2048,512]{1,0:T(8,128)(2,1)} %param.4, bf16[2048,512]{1,0:T(8,128)(2,1)S(1)} %copy-done), kind=kOutput, calls=%fused_computation.21 | convolution fusion | flops 4303353856 | bytes 20979712 | tf_op jit(solution)/shard_map/dot_general | solution.py:31
  103.7 7.2 pmax.28
  111.0 8.1 exponential_reduce_fusion.3
  119.1 11.4 %all-reduce = (f32[2048]{0:T(1024)S(1)}, f32[]{:T(128)}) all-reduce(f32[2048]{0:T(1024)S(1)} %exponential_reduce_fusion.3, f32[]{:T(128)} %reduce_sum.73), channel_id=1, replica_groups=mesh['ctx'=32,'tok'=4] {'tok'}, use_global_device_ids=true, to_apply=%region_7.0 | all-reduce | flops 2049 | bytes 16392 | tf_op jit(solution)/shard_map/psum | solution.py:13
  130.5 0.0 copy-done.2
  130.5 0.7 add_subtract_fusion.3
  131.2 0.0 copy-start.3
  131.2 6.9 add_reduce_fusion.1
  138.1 77.8 %pmax.29 = f32[2048]{0:T(1024)S(1)} all-reduce(f32[2048]{0:T(1024)S(1)} %add_reduce_fusion.1), channel_id=1, replica_groups=mesh['ctx'=32,'tok'=4] {'ctx'}, use_global_device_ids=true, to_apply=%region_9.0 | all-reduce | flops 2048 | bytes 16384 | tf_op jit(solution)/shard_map/pmax | solution.py:18
  216.0 7.6 exponential_reduce_fusion.2
  223.5 80.0 %psum.73 = f32[2048]{0:T(1024)S(1)} all-reduce(f32[2048]{0:T(1024)S(1)} %exponential_reduce_fusion.2), channel_id=1, replica_groups=mesh['ctx'=32,'tok'=4] {'ctx'}, use_global_device_ids=true, to_apply=%region_11.0 | all-reduce | flops 2048 | bytes 16384 | tf_op jit(solution)/shard_map/psum | solution.py:19
  303.5 0.0 copy-done.3
  303.5 0.7 add_subtract_fusion.2
  304.2 6.9 add_reduce_fusion
  311.1 7.4 pmax.30
  318.5 7.7 exponential_reduce_fusion.1
  326.2 7.4 psum.74
  333.6 0.7 add_subtract_fusion.1
  334.2 6.9 add_reduce_fusion.2
  341.2 78.0 %pmax.31 = f32[2048]{0:T(1024)S(1)} all-reduce(f32[2048]{0:T(1024)S(1)} %add_reduce_fusion.2), channel_id=1, replica_groups=mesh['ctx'=32,'tok'=4] {'ctx'}, use_global_device_ids=true, to_apply=%region_17.0 | all-reduce | flops 2048 | bytes 16384 | tf_op jit(solution)/shard_map/pmax | solution.py:18
  419.2 7.6 exponential_reduce_fusion
  426.8 79.8 %psum.75 = f32[2048]{0:T(1024)S(1)} all-reduce(f32[2048]{0:T(1024)S(1)} %exponential_reduce_fusion), channel_id=1, replica_groups=mesh['ctx'=32,'tok'=4] {'ctx'}, use_global_device_ids=true, to_apply=%region_19.0 | all-reduce | flops 2048 | bytes 16384 | tf_op jit(solution)/shard_map/psum | solution.py:19
  506.6 0.7 add_subtract_fusion
  507.3 8.1 fusion
  515.4 0.0 copy-start.1
  515.4 3.2 copy-done.1
  518.7 6.0 fusion.4
  524.6 0.0 all-reduce.4.cloned.1.call-update
  524.7 0.0 all-reduce.6.cloned.1.call-start
  524.7 10.5 %fusion.5 = f32[2048,512]{1,0:T(8,128)} fusion(bf16[2048,2048]{1,0:T(8,128)(2,1)} %copy-done.1, bf16[2048,512]{1,0:T(8,128)(2,1)} %param.4), kind=kOutput, calls=%fused_computation.23 | convolution fusion | flops 4294967296 | bytes 14680064 | tf_op jit(solution)/shard_map/dot_general | solution.py:49
  535.2 0.0 all-reduce.6.cloned.1.call-update
  535.2 79.0 %psum.79 = f32[2048]{0:T(1024)S(1)} all-reduce(f32[2048]{0:T(1024)S(1)} %get-tuple-element.3), channel_id=1, replica_groups=mesh['ctx'=32,'tok'=4] {'ctx'}, use_global_device_ids=true, to_apply=%region_25.0 | all-reduce | flops 2048 | bytes 16384 | tf_op jit(solution)/shard_map/psum | solution.py:52
  614.3 7.3 psum.77
  621.6 1.3 multiply_divide_fusion
  622.8 0.0 all-reduce.4.cloned.1.call-done
  622.8 3.9 divide_convert_fusion.1
  626.7 311.9 %all-reduce.6.cloned.1.call-done = f32[2048,512]{1,0:T(8,128)} async-done(((f32[2048,512]{1,0:T(8,128)}), f32[2048,512]{1,0:T(8,128)}) %all-reduce.6.cloned.1.call-update) | async-done | bytes 4194320 | tf_op jit(solution)/shard_map/psum | solution.py:52
  938.6 3.9 divide_convert_fusion
Async XLA Ops:
  7.2 86.9 %copy-start = (bf16[2048,512]{1,0:T(8,128)(2,1)S(1)}, bf16[2048,512]{1,0:T(8,128)(2,1)}, u32[]{:S(2)}) copy-start(bf16[2048,512]{1,0:T(8,128)(2,1)} %param.5) | copy-start | bytes 6291460
  7.2 615.7 %all-reduce.4.cloned.1.call-start = ((), (), s32[]{:S(2)}) async-start(), calls=%async_computation | async-start | bytes 8388608 | tf_op jit(solution)/shard_map/psum | solution.py:45
  94.0 36.5 %copy-start.2 = (f32[2048]{0:T(1024)S(1)}, f32[2048]{0:T(1024)}, u32[]{:S(2)}) copy-start(f32[2048]{0:T(1024)} %param.6) | copy-start | bytes 24580
  131.2 172.4 %copy-start.3 = (f32[2048]{0:T(1024)S(1)}, f32[2048]{0:T(1024)}, u32[]{:S(2)}) copy-start(f32[2048]{0:T(1024)} %param.7) | copy-start | bytes 24580
  515.4 3.2 copy-start.1
  524.7 414.0 %all-reduce.6.cloned.1.call-start = ((), (), s32[]{:S(2)}) async-start(), calls=%async_computation.1 | async-start | bytes 8388608 | tf_op jit(solution)/shard_map/psum | solution.py:52
Sparse Core Ops, SparseCore 0:
  524.8 90.6 all-reduce.3
  618.1 320.4 all-reduce.5
where the time goes:
time: 950 us; the launch traced here: 949 us
  blocking collectives  519 us (55%)
  waiting for transfers between devices  312 us (33%)
  other arithmetic  74.2 us (8%)
  matrix products  26.1 us (3%)
  between operations  14.2 us (1%)
    psum x1, waiting for transfers between devices, shards(): token_whole, col_sum = lax.psum((token_part, col_part), 'ctx')  312 us
    psum x2, blocking collectives, col_logsum(): lax.psum(jnp.sum(jnp.exp(shifted - highest[None, :]), axis=0), 'ctx')  160 us
    pmax x2, blocking collectives, col_logsum(): highest = lax.pmax(jnp.max(shifted, axis=0), 'ctx')  156 us
    psum x1, blocking collectives, shards(): frame_whole_mass = lax.psum(jnp.sum(frame_mass), 'ctx')  84.1 us
    psum x1, blocking collectives, shards(): token_whole, col_sum = lax.psum((token_part, col_part), 'ctx')  79 us
  transfers between devices with their start and end apart: 2, of which 1 were waited for; matrix products, arithmetic and copies ran while one was open for 2% of the time, Pallas kernels for 0%

commit v1 on v0

v1 whole, which is shorter than its diff:
```python
import functools
import math

import jax
import jax.numpy as jnp
from jax import lax
from jax.experimental import pallas as pl
from jax.experimental.pallas import tpu as pltpu
from jax.sharding import PartitionSpec as P

F32, BF16 = jnp.float32, jnp.bfloat16
TILE = 256
VMEM_BYTES = 48 * 1024 * 1024


def swap(value, axis, bit):
    size = lax.axis_size(axis)
    return lax.ppermute(value, axis, [(i, i ^ bit) for i in range(size)])


def log2(x):
    return jnp.log(x) * (1.0 / math.log(2.0))


def contract_last(a, b):
    return lax.dot_general(a, b, (((1,), (1,)), ((), ())), preferred_element_type=F32)


def column(row, out_ref):
    for start in range(0, row.shape[1], 128):
        block = jnp.broadcast_to(row[:, start : start + 128], (128, 128))
        out_ref[start : start + 128, :] = block.T


def lane_sum_row(p):
    part = p[:, 0:128]
    for start in range(128, p.shape[1], 128):
        part = part + p[:, start : start + 128]
    total = jnp.sum(part.T, axis=0, keepdims=True)
    return total


def merge_lse(parts):
    highest = jnp.max(parts, axis=0, keepdims=True)
    return highest + log2(jnp.sum(jnp.exp2(parts - highest), axis=0, keepdims=True))


def first_rows(scale, t_ref, f_ref, lse_ref, s_ref):
    s_ref[...] = contract_last(t_ref[...], f_ref[...]) * scale
    s = s_ref[...]
    highest = jnp.max(s, axis=0, keepdims=True)
    lse_ref[...] = highest + log2(jnp.sum(jnp.exp2(s - highest), axis=0, keepdims=True))


def first_cols(scale, lse_parts_ref, fm_ref, f_ref, t_ref, lse_ref, u_ref, s_ref, col_ref):
    @pl.when(pl.program_id(0) == 0)
    def _():
        u = log2(fm_ref[...]) - merge_lse(lse_parts_ref[...])
        u_ref[...] = u
        column(u, col_ref)

    s = contract_last(f_ref[...], t_ref[...]) * scale
    bias = col_ref[...]
    s_ref[...] = s + jnp.concatenate([bias] * (s.shape[1] // 128), axis=1)
    s = s_ref[...]
    highest = jnp.max(s, axis=0, keepdims=True)
    lse_ref[...] = highest + log2(jnp.sum(jnp.exp2(s - highest), axis=0, keepdims=True))


def second_rows(scale, lse_parts_ref, tm_ref, u_ref, t_ref, f_ref, sum_ref, v_ref, col_ref):
    @pl.when(pl.program_id(0) == 0)
    def _():
        v = log2(tm_ref[...]) - merge_lse(lse_parts_ref[...])
        v_ref[...] = v
        column(v, col_ref)

    s = contract_last(t_ref[...], f_ref[...]) * scale
    bias = col_ref[...]
    x = s + jnp.concatenate([bias] * (s.shape[1] // 128), axis=1) + u_ref[...]
    sum_ref[...] = jnp.sum(jnp.exp2(x), axis=0, keepdims=True)


def second_cols(scale, row_parts_ref, fm_ref, u_ref, v_ref, t_ref, f_ref, sum_ref, acc_ref, u2_ref, col_ref):
    @pl.when(pl.program_id(0) == 0)
    def _():
        u2_ref[...] = u_ref[...] + log2(fm_ref[...] / jnp.sum(row_parts_ref[...], axis=0, keepdims=True))

    column(v_ref[...], col_ref)
    s = contract_last(t_ref[...], f_ref[...]) * scale
    bias = col_ref[...]
    x = s + jnp.concatenate([bias] * (s.shape[1] // 128), axis=1) + u2_ref[...]
    p = jnp.exp2(x)
    sum_ref[...] = lane_sum_row(p)
    acc_ref[...] = jnp.dot(p.astype(BF16), f_ref[...], preferred_element_type=F32).astype(BF16)


def last_rows(scale, col_parts_ref, tm_ref, v_ref, u2_ref, shift_ref, f_ref, t_ref, sum_ref, acc_ref, total_ref, v2_ref, col_ref):
    @pl.when(pl.program_id(0) == 0)
    def _():
        total = jnp.sum(col_parts_ref[...], axis=0, keepdims=True)
        total_ref[...] = total
        v2_ref[...] = v_ref[...] + log2(tm_ref[...] / total)

    column(u2_ref[...] + shift_ref[0, 0], col_ref)
    s = contract_last(f_ref[...], t_ref[...]) * scale
    bias = col_ref[...]
    x = s + jnp.concatenate([bias] * (s.shape[1] // 128), axis=1) + v2_ref[...]
    p = jnp.exp2(x)
    sum_ref[...] = lane_sum_row(p)
    acc_ref[...] = jnp.dot(p.astype(BF16), t_ref[...], preferred_element_type=F32).astype(BF16)


def whole(shape):
    return pl.BlockSpec(shape, lambda i: (0,) * len(shape))


def lanes():
    return pl.BlockSpec((1, TILE), lambda i: (0, i))


def rows(width):
    return pl.BlockSpec((TILE, width), lambda i: (i, 0))


def row_shape(n):
    return jax.ShapeDtypeStruct((1, n), F32)


def call(body, steps, in_specs, out_specs, out_shape, scratch, name):
    return pl.pallas_call(
        body,
        grid=(steps,),
        in_specs=in_specs,
        out_specs=out_specs,
        out_shape=out_shape,
        scratch_shapes=scratch,
        compiler_params=pltpu.CompilerParams(vmem_limit_bytes=VMEM_BYTES),
        name=name,
    )


def shards(frames, tokens, frame_mass, token_mass):
    nf, d = frames.shape
    nt = tokens.shape[0]
    n_ctx = lax.axis_size("ctx")
    scale = math.log2(math.e) / math.sqrt(d)
    fm, tm = frame_mass.reshape(1, nf), token_mass.reshape(1, nt)
    f_steps, t_steps = nf // TILE, nt // TILE
    f_all, t_all = whole((nf, d)), whole((nt, d))

    lse = call(
        functools.partial(first_rows, scale), f_steps, [t_all, rows(d)], lanes(), row_shape(nf),
        [pltpu.VMEM((nt, TILE), F32)], "first_rows",
    )(tokens, frames)
    with jax.named_scope("rows_one"):
        own_token_mass = jnp.sum(token_mass)
        lse = lax.all_gather(lse, "tok", tiled=True)
    lse, u = call(
        functools.partial(first_cols, scale), t_steps,
        [whole((4, nf)), whole((1, nf)), f_all, rows(d)], [lanes(), whole((1, nf))], [row_shape(nt), row_shape(nf)],
        [pltpu.VMEM((nf, TILE), F32), pltpu.VMEM((nf, 128), F32)], "first_cols",
    )(lse, fm, frames, tokens)
    with jax.named_scope("cols_one"):
        packed = jnp.concatenate([lse, jnp.broadcast_to(jnp.sum(frame_mass), (1, 128))], axis=1)
        packed = jnp.broadcast_to(packed[None], (n_ctx, 1, nt + 128))
        packed = lax.all_to_all(packed, "ctx", 0, 0)[:, 0]
        lse = packed[:, :nt]
        frame_total = jnp.sum(packed[:, nt])
    part, v = call(
        functools.partial(second_rows, scale), f_steps,
        [whole((n_ctx, nt)), whole((1, nt)), lanes(), t_all, rows(d)], [lanes(), whole((1, nt))],
        [row_shape(nf), row_shape(nt)], [pltpu.VMEM((nt, 128), F32)], "second_rows",
    )(lse, tm, u, tokens, frames)
    with jax.named_scope("rows_two"):
        packed = jnp.concatenate([part, jnp.broadcast_to(own_token_mass, (1, 128))], axis=1)
        packed = lax.all_gather(packed, "tok", tiled=True)
        part = packed[:, :nf]
        row_one = jnp.sum(part, axis=0)
        token_total = jnp.sum(packed[:, nf])
    part, token_part, u2 = call(
        functools.partial(second_cols, scale), t_steps,
        [whole((4, nf)), whole((1, nf)), whole((1, nf)), lanes(), rows(d), f_all],
        [lanes(), rows(d), whole((1, nf))],
        [row_shape(nt), jax.ShapeDtypeStruct((nt, d), BF16), row_shape(nf)], [pltpu.VMEM((TILE, 128), F32)], "second_cols",
    )(part, fm, u, v, tokens, frames)
    with jax.named_scope("cols_two"):
        part = lax.all_to_all(jnp.broadcast_to(part[None], (n_ctx, 1, nt)), "ctx", 0, 0)[:, 0]
    shift = -log2(token_total).reshape(1, 1)
    part, frame_part, col_total, v2 = call(
        functools.partial(last_rows, scale), f_steps,
        [whole((n_ctx, nt)), whole((1, nt)), whole((1, nt)), lanes(),
         pl.BlockSpec(memory_space=pltpu.SMEM), rows(d), t_all],
        [lanes(), rows(d), whole((1, nt)), whole((1, nt))],
        [row_shape(nf), jax.ShapeDtypeStruct((nf, d), BF16), row_shape(nt), row_shape(nt)],
        [pltpu.VMEM((TILE, 128), F32)], "last_rows",
    )(part, tm, v, u2, shift, frames, tokens)

    with jax.named_scope("frame_sums"):
        row_sum = jnp.sum(lax.all_gather(part, "tok", tiled=True), axis=0)
        core = lax.axis_index("tok") % 2
        half = nf // 2
        mine = lax.dynamic_slice_in_dim(frame_part, core * half, half)
        theirs = lax.dynamic_slice_in_dim(frame_part, (1 - core) * half, half)
        mine = (mine.astype(F32) + swap(theirs, "tok", 1).astype(F32)).astype(BF16)
        other = swap(mine, "tok", 2)
    with jax.named_scope("token_sums"):
        pieces = lax.all_to_all(token_part.reshape(n_ctx, nt // n_ctx, d), "ctx", 0, 0)
        me = lax.axis_index("ctx")
        own = nt // n_ctx
        total = jnp.sum(pieces.astype(F32), axis=0)
        total = total / lax.dynamic_slice_in_dim(col_total[0], me * own, own)[:, None]
        piece = total.astype(BF16)
        token_map = lax.all_to_all(jnp.broadcast_to(piece[None], (n_ctx, own, d)), "ctx", 0, 0).reshape(nt, d)
    with jax.named_scope("frame_out"):
        done = mine.astype(F32) + other.astype(F32)
        done = (done / lax.dynamic_slice_in_dim(row_sum, core * half, half)[:, None]).astype(BF16)
        sibling = swap(done, "tok", 1)
        low = jnp.where(core == 0, done, sibling)
        high = jnp.where(core == 0, sibling, done)
        frame_map = jnp.concatenate([low, high])
    mass_ratio = row_sum / (frame_mass / frame_total)
    return frame_map, token_map, mass_ratio


def solution(mesh):
    return jax.shard_map(
        shards,
        mesh=mesh,
        in_specs=(P("ctx", None), P("tok", None), P("ctx"), P("tok")),
        out_specs=(P("ctx", None), P("tok", None), P("ctx")),
        check_vma=False,
    )
```

time: 950 us -> 193 us (0.20)
  blocking collectives: 519 us -> 42.6 us
  waiting for transfers between devices: 312 us -> 41.7 us
  other arithmetic: 74.2 us -> 12.2 us
  Pallas kernels: 0 us -> 51.5 us
  starting transfers between devices: 0.08 us -> 27.8 us
  matrix products: 26.1 us -> 0 us
  between operations: 14.2 us -> 1.59 us
  local copies, waits for them, and re-layouts: 3.23 us -> 15.2 us
    psum x7 -> x0, blocking collectives: 349 us -> none  [the longest x2 160 us: col_logsum(): lax.psum(jnp.sum(jnp.exp(shifted - highest[None, :]), axis=0), 'ctx')]
    psum x2 -> x0, waiting for transfers between devices: 312 us -> none  [the longest x1 312 us: shards(): token_whole, col_sum = lax.psum((token_part, col_part), 'ctx')]
    pmax x4 -> x0, blocking collectives: 170 us -> none  [the longest x2 156 us: col_logsum(): highest = lax.pmax(jnp.max(shifted, axis=0), 'ctx')]
    pallas_call x0 -> x5, Pallas kernels: none -> 51.5 us  [the longest x1 12.3 us: shards(): call(functools.partial(second_cols, scale), t_steps, [whole((4, nf)), who...]
    all_gather x0 -> x3, blocking collectives: none -> 42.6 us  [the longest x1 28.6 us: shards(): row_sum = jnp.sum(lax.all_gather(part, 'tok', tiled=True), axis=0)]
    all_to_all x0 -> x4, waiting for transfers between devices: none -> 38 us  [the longest x1 21 us: shards(): lax.all_to_all(jnp.broadcast_to(piece[None], (n_ctx, own, d)), 'ctx', 0, 0)]
    reduce_sum x7 -> x6, other arithmetic: 41.8 us -> 4.34 us  [the longest x1 1.9 us: shards(): total = jnp.sum(pieces.astype(F32), axis=0)]
    dot_general x3 -> x0, matrix products: 26.1 us -> none  [the longest x1 10.5 us: shards(): lax.dot_general(transport, frames, (((0,), (0,)), ((), ())), preferred_el...]
  transfers between devices with their start and end apart: 2 -> 7, of which waited for: 1 -> 5; matrix products, arithmetic and copies ran while one was open for 2% -> 7% of each run, Pallas kernels for 0% -> 6%
where the time goes in v1:
time: 193 us
  Pallas kernels  51.5 us (27%)
  blocking collectives  42.6 us (22%)
  waiting for transfers between devices  41.7 us (22%)
  starting transfers between devices  27.8 us (14%)
  local copies, waits for them, and re-layouts  15.2 us (8%)
  other arithmetic  12.2 us (6%)
    all_gather x1, blocking collectives, shards(): row_sum = jnp.sum(lax.all_gather(part, 'tok', tiled=True), axis=0)  28.6 us
    all_to_all x1, waiting for transfers between devices, shards(): lax.all_to_all(jnp.broadcast_to(piece[None], (n_ctx, own, d)), 'ctx', 0, 0)  21 us
    pallas_call x1, Pallas kernels, shards(): call(functools.partial(second_cols, scale), t_steps, [whole((4, nf)), who...  12.3 us
    pallas_call x1, Pallas kernels, shards(): call(functools.partial(last_rows, scale), f_steps, [whole((n_ctx, nt)), w...  12.3 us
    unnamed x28, local copies, waits for them, and re-layouts  11.1 us
    pallas_call x1, Pallas kernels, shards(): call(functools.partial(first_cols, scale), t_steps, [whole((4, nf)), whol...  10.2 us
    pallas_call x1, Pallas kernels, shards(): call(functools.partial(first_rows, scale), f_steps, [t_all, rows(d)], lan...  10.1 us
    all_to_all x1, waiting for transfers between devices, shards(): packed = lax.all_to_all(packed, 'ctx', 0, 0)[:, 0]  8.93 us
  transfers between devices with their start and end apart: 7, of which 5 were waited for; matrix products, arithmetic and copies ran while one was open for 7% of the time, Pallas kernels for 6%

profile of v1, /device:TPU:0, one launch (start us, length us, event | category | flops | bytes accessed | tf_op | source)
XLA Modules:
  0.0 192.6 jit_solution(1236036484255677531)
XLA Ops:
  0.6 0.0 copy-start
  0.6 1.6 copy-done
  2.2 1.6 copy-done.2
  3.8 10.1 %first_rows.1 = f32[1,2048]{1,0:T(1,128)S(1)} custom-call(bf16[2048,512]{1,0:T(8,128)(2,1)S(1)} %copy-done, bf16[2048,512]{1,0:T(8,128)(2,1)S(1)} %copy-done.2), custom_call_target="tpu_custom_call" | custom-call | tf_op jit(solution)/shard_map/first_rows/pallas_call | solution.py:151
  13.9 7.2 %all-gather = f32[4,1,2048]{2,1,0:T(1,128)S(1)} all-gather(f32[1,1,2048]{2,1,0:T(1,128)S(1)} %bitcast.31), channel_id=1, replica_groups=mesh['ctx'=32,'tok'=4] {'tok'}, dimensions={0}, use_global_device_ids=true | all-gather | bytes 40960 | tf_op jit(solution)/shard_map/rows_one/all_gather | solution.py:157
  21.1 0.6 reduce_sum.54
  21.7 1.6 copy-done.3
  23.3 10.2 %first_cols.1 = (f32[1,2048]{1,0:T(1,128)S(1)}, f32[1,2048]{1,0:T(1,128)S(1)}) custom-call(f32[4,2048]{1,0:T(4,128)S(1)} %bitcast.28, f32[1,2048]{1,0:T(1,128)S(1)} %bitcast.26, bf16[2048,512]{1,0:T(8,128)(2,1)S(1)} %copy-done.3, bf16[2048,512]{1,0:T(8,128)(2,1)S(1)} %copy-done.1), custom_call_target="tpu_custom_call" | custom-call | tf_op jit(solution)/shard_map/first_cols/pallas_call | solution.py:158
  33.6 0.7 pad_reduce_fusion
  34.3 0.9 broadcast_in_dim.11
  35.1 8.2 %all-to-all-start = ((f32[32,1,2176]{2,1,0:T(1,128)}), f32[32,1,2176]{2,1,0:T(1,128)S(1)}, u32[]{:S(2)}, u32[]{:S(2)}) async-start(f32[32,1,2176]{2,1,0:T(1,128)} %broadcast_in_dim.11), calls=%async_computation | async-start | bytes 557056 | tf_op jit(solution)/shard_map/cols_one/all_to_all | solution.py:166
  43.4 0.6 reduce_sum.55
  44.0 8.9 %all-to-all-done = f32[32,1,2176]{2,1,0:T(1,128)S(1)} async-done(((f32[32,1,2176]{2,1,0:T(1,128)}), f32[32,1,2176]{2,1,0:T(1,128)S(1)}, u32[]{:S(2)}, u32[]{:S(2)}) %all-to-all-start) | async-done | bytes 278560 | tf_op jit(solution)/shard_map/cols_one/all_to_all | solution.py:166
  52.9 0.0 copy-start.4
  53.0 1.6 copy-done.4
  54.5 6.6 %second_rows.1 = (f32[1,2048]{1,0:T(1,128)S(1)}, f32[1,2048]{1,0:T(1,128)S(1)}) custom-call(f32[32,2048]{1,0:T(8,128)S(1)} %slice.16.lse_parts_ref, f32[1,2048]{1,0:T(1,128)S(1)} %bitcast.29, f32[1,2048]{1,0:T(1,128)S(1)} %get-tuple-element.14.u_ref, bf16[2048,512]{1,0:T(8,128)(2,1)S(1)} %copy-done.1, bf16[2048,512]{1,0:T(8,128)(2,1)S(1)} %copy-done.4), custom_call_target="tpu_custom_call" | custom-call | tf_op jit(solution)/shard_map/second_rows/pallas_call | solution.py:169
  61.1 0.7 pad_bitcast_fusion
  61.8 6.8 %all-gather.1 = f32[4,1,2176]{2,1,0:T(1,128)S(1)} all-gather(f32[1,1,2176]{2,1,0:T(1,128)S(1)} %pad_bitcast_fusion), channel_id=1, replica_groups=mesh['ctx'=32,'tok'=4] {'tok'}, dimensions={0}, use_global_device_ids=true | all-gather | bytes 43520 | tf_op jit(solution)/shard_map/rows_two/all_gather | solution.py:176
  68.6 12.3 %second_cols.1 = (f32[1,2048]{1,0:T(1,128)S(1)}, bf16[2048,512]{1,0:T(8,128)(2,1)S(1)}, f32[1,2048]{1,0:T(1,128)S(1)}) custom-call(f32[4,2048]{1,0:T(4,128)S(1)} %slice.17.row_parts_ref, f32[1,2048]{1,0:T(1,128)S(1)} %bitcast.27, f32[1,2048]{1,0:T(1,128)S(1)} %get-tuple-element.14.u_ref, f32[1,2048]{1,0:T(1,128)S(1)} %get-tuple-element.16.v_ref, ...), custom_call_target="tpu_custom_call" | custom-call | tf_op jit(solution)/shard_map/second_cols/pallas_call | solution.py:180
  81.0 1.3 copy-done.7
  82.3 0.8 broadcast_in_dim.13
  83.1 4.1 %all-to-all-start.1 = ((f32[32,1,2048]{2,1,0:T(1,128)}), f32[32,1,2048]{2,1,0:T(1,128)S(1)}, u32[]{:S(2)}, u32[]{:S(2)}) async-start(f32[32,1,2048]{2,1,0:T(1,128)} %broadcast_in_dim.13), calls=%async_computation.1 | async-start | bytes 524288 | tf_op jit(solution)/shard_map/cols_two/all_to_all | solution.py:187
  87.3 0.6 slice_reduce_fusion.1
  88.5 8.1 %all-to-all-done.1 = f32[32,1,2048]{2,1,0:T(1,128)S(1)} async-done(((f32[32,1,2048]{2,1,0:T(1,128)}), f32[32,1,2048]{2,1,0:T(1,128)S(1)}, u32[]{:S(2)}, u32[]{:S(2)}) %all-to-all-start.1) | async-done | bytes 262176 | tf_op jit(solution)/shard_map/cols_two/all_to_all | solution.py:187
  96.7 4.9 %all-to-all-start.2 = ((bf16[32,64,512]{2,1,0:T(8,128)(2,1)}), bf16[32,64,512]{2,1,0:T(8,128)(2,1)}, u32[]{:S(2)}, u32[]{:S(2)}) async-start(bf16[32,64,512]{2,1,0:T(8,128)(2,1)} %bitcast.24), calls=%async_computation.2 | async-start | bytes 4194304 | tf_op jit(solution)/shard_map/token_sums/all_to_all | solution.py:207
  101.6 0.1 copy.16
  101.7 12.3 %last_rows.1 = (f32[1,2048]{1,0:T(1,128)S(1)}, bf16[2048,512]{1,0:T(8,128)(2,1)S(1)}, f32[1,2048]{1,0:T(1,128)S(1)}, f32[1,2048]{1,0:T(1,128)}) custom-call(f32[32,2048]{1,0:T(8,128)S(1)} %bitcast.25, f32[1,2048]{1,0:T(1,128)S(1)} %bitcast.30, f32[1,2048]{1,0:T(1,128)S(1)} %get-tuple-element.16.v_ref, f32[1,2048]{1,0:T(1,128)S(1)} %get-tuple-element.18.u2_ref, ...), custom_call_target="tpu_custom_call" | custom-call | tf_op jit(solution)/shard_map/last_rows/pallas_call | solution.py:189
  114.0 1.3 copy-done.6
  115.3 0.1 constant_dynamic-slice_fusion.1
  115.4 0.1 collective-permute-start
  115.5 2.8 %collective-permute-done = bf16[1024,512]{1,0:T(8,128)(2,1)} collective-permute-done((bf16[1024,512]{1,0:T(8,128)(2,1)S(1)}, bf16[1024,512]{1,0:T(8,128)(2,1)}, u32[]{:S(2)}, u32[]{:S(2)}) %collective-permute-start) | collective-permute-done | bytes 1048608 | tf_op jit(solution)/shard_map/frame_sums/ppermute | solution.py:18
  118.2 1.8 add_convert_fusion
  120.1 3.5 %collective-permute-start.1 = (bf16[1024,512]{1,0:T(8,128)(2,1)S(1)}, bf16[1024,512]{1,0:T(8,128)(2,1)}, u32[]{:S(2)}, u32[]{:S(2)}) collective-permute-start(bf16[1024,512]{1,0:T(8,128)(2,1)S(1)} %add_convert_fusion), channel_id=1, source_target_pairs={{0,2},{1,3},{2,0},{3,1},{4,6},{5,7},{6,4},{7,5},{8,10},{9,11},{10,... | collective-permute-start | bytes 3145736 | tf_op jit(solution)/shard_map/frame_sums/ppermute | solution.py:18
  123.6 28.6 %all-gather.2 = f32[4,1,2048]{2,1,0:T(1,128)S(1)} all-gather(f32[1,1,2048]{2,1,0:T(1,128)S(1)} %bitcast.32), channel_id=1, replica_groups=mesh['ctx'=32,'tok'=4] {'tok'}, dimensions={0}, use_global_device_ids=true | all-gather | bytes 40960 | tf_op jit(solution)/shard_map/frame_sums/all_gather | solution.py:199
  152.3 0.1 fusion
  152.4 1.9 convert_reduce_fusion
  154.3 0.1 divide_convert_fusion.1
  154.3 1.6 broadcast_in_dim.14
  155.9 6.8 %all-to-all-start.3 = ((bf16[32,64,512]{2,1,0:T(8,128)(2,1)}), bf16[32,64,512]{2,1,0:T(8,128)(2,1)S(1)}, u32[]{:S(2)}, u32[]{:S(2)}) async-start(bf16[32,64,512]{2,1,0:T(8,128)(2,1)} %broadcast_in_dim.14), calls=%async_computation.3 | async-start | bytes 4194304 | tf_op jit(solution)/shard_map/token_sums/all_to_all | solution.py:213
  162.7 1.9 divide_convert_fusion
  164.6 0.1 collective-permute-start.2
  164.7 0.6 slice_reduce_fusion
  165.3 1.3 multiply_divide_fusion
  166.6 0.9 collective-permute-done.2
  167.5 1.4 broadcast_select_fusion.1
  168.8 1.5 pad_maximum_fusion
  170.3 21.0 %all-to-all-done.3 = bf16[32,64,512]{2,1,0:T(8,128)(2,1)S(1)} async-done(((bf16[32,64,512]{2,1,0:T(8,128)(2,1)}), bf16[32,64,512]{2,1,0:T(8,128)(2,1)S(1)}, u32[]{:S(2)}, u32[]{:S(2)}) %all-to-all-start.3) | async-done | bytes 2097184 | tf_op jit(solution)/shard_map/token_sums/all_to_all | solution.py:213
  191.3 1.3 copy.20
  (23 shorter events, 0.1 us)
Async XLA Ops:
  0.6 1.6 copy-start
  2.2 1.6 copy-start.2
  3.8 17.3 %copy-start.8 = (f32[2048]{0:T(1024)S(1)}, f32[2048]{0:T(1024)}, u32[]{:S(2)}) copy-start(f32[2048]{0:T(1024)} %param.6) | copy-start | bytes 24580
  3.8 17.9 %copy-start.1 = (bf16[2048,512]{1,0:T(8,128)(2,1)S(1)}, bf16[2048,512]{1,0:T(8,128)(2,1)}, u32[]{:S(2)}) copy-start(bf16[2048,512]{1,0:T(8,128)(2,1)} %t_ref.9) | copy-start | bytes 6291460
  21.7 1.6 copy-start.3
  23.3 20.0 %copy-start.9 = (f32[2048]{0:T(1024)S(1)}, f32[2048]{0:T(1024)}, u32[]{:S(2)}) copy-start(f32[2048]{0:T(1024)} %param.7) | copy-start | bytes 24580
  35.1 17.8 %all-to-all-start = ((f32[32,1,2176]{2,1,0:T(1,128)}), f32[32,1,2176]{2,1,0:T(1,128)S(1)}, u32[]{:S(2)}, u32[]{:S(2)}) async-start(f32[32,1,2176]{2,1,0:T(1,128)} %broadcast_in_dim.11), calls=%async_computation | async-start | bytes 557056 | tf_op jit(solution)/shard_map/cols_one/all_to_all | solution.py:166
  52.9 1.6 copy-start.4
  80.9 1.3 copy-start.7
  83.1 13.6 %all-to-all-start.1 = ((f32[32,1,2048]{2,1,0:T(1,128)}), f32[32,1,2048]{2,1,0:T(1,128)S(1)}, u32[]{:S(2)}, u32[]{:S(2)}) async-start(f32[32,1,2048]{2,1,0:T(1,128)} %broadcast_in_dim.13), calls=%async_computation.1 | async-start | bytes 524288 | tf_op jit(solution)/shard_map/cols_two/all_to_all | solution.py:187
  96.7 5.0 %copy-start.5 = (bf16[2048,512]{1,0:T(8,128)(2,1)S(1)}, bf16[2048,512]{1,0:T(8,128)(2,1)}, u32[]{:S(2)}) copy-start(bf16[2048,512]{1,0:T(8,128)(2,1)} %f_ref.9) | copy-start | bytes 6291460
  96.7 55.7 %all-to-all-start.2 = ((bf16[32,64,512]{2,1,0:T(8,128)(2,1)}), bf16[32,64,512]{2,1,0:T(8,128)(2,1)}, u32[]{:S(2)}, u32[]{:S(2)}) async-start(bf16[32,64,512]{2,1,0:T(8,128)(2,1)} %bitcast.24), calls=%async_computation.2 | async-start | bytes 4194304 | tf_op jit(solution)/shard_map/token_sums/all_to_all | solution.py:207
  114.0 1.3 copy-start.6
  115.4 2.9 %collective-permute-start = (bf16[1024,512]{1,0:T(8,128)(2,1)S(1)}, bf16[1024,512]{1,0:T(8,128)(2,1)}, u32[]{:S(2)}, u32[]{:S(2)}) collective-permute-start(bf16[1024,512]{1,0:T(8,128)(2,1)S(1)} %constant_dynamic-slice_fusion.1), channel_id=1, source_target_pairs={{0,1},{1,0},{2,3},{3,2},{4,5},{5,4},{6,7},{7,6},{8,9},{9,8},{10,11... | collective-permute-start | bytes 3145736 | tf_op jit(solution)/shard_map/frame_sums/ppermute | solution.py:18
  120.1 35.8 %copy-start.10 = (bf16[1024,512]{1,0:T(8,128)(2,1)}, bf16[1024,512]{1,0:T(8,128)(2,1)S(1)}, u32[]{:S(2)}) copy-start(bf16[1024,512]{1,0:T(8,128)(2,1)S(1)} %add_convert_fusion) | copy-start | bytes 3145732
  120.1 42.6 %collective-permute-start.1 = (bf16[1024,512]{1,0:T(8,128)(2,1)S(1)}, bf16[1024,512]{1,0:T(8,128)(2,1)}, u32[]{:S(2)}, u32[]{:S(2)}) collective-permute-start(bf16[1024,512]{1,0:T(8,128)(2,1)S(1)} %add_convert_fusion), channel_id=1, source_target_pairs={{0,2},{1,3},{2,0},{3,1},{4,6},{5,7},{6,4},{7,5},{8,10},{9,11},{10,... | collective-permute-start | bytes 3145736 | tf_op jit(solution)/shard_map/frame_sums/ppermute | solution.py:18
  155.9 35.4 %all-to-all-start.3 = ((bf16[32,64,512]{2,1,0:T(8,128)(2,1)}), bf16[32,64,512]{2,1,0:T(8,128)(2,1)S(1)}, u32[]{:S(2)}, u32[]{:S(2)}) async-start(bf16[32,64,512]{2,1,0:T(8,128)(2,1)} %broadcast_in_dim.14), calls=%async_computation.3 | async-start | bytes 4194304 | tf_op jit(solution)/shard_map/token_sums/all_to_all | solution.py:213
  164.6 2.9 %collective-permute-start.2 = (bf16[1024,512]{1,0:T(8,128)(2,1)S(1)}, bf16[1024,512]{1,0:T(8,128)(2,1)}, u32[]{:S(2)}, u32[]{:S(2)}) collective-permute-start(bf16[1024,512]{1,0:T(8,128)(2,1)S(1)} %divide_convert_fusion), channel_id=1, source_target_pairs={{0,1},{1,0},{2,3},{3,2},{4,5},{5,4},{6,7},{7,6},{8,9},{9,8},{10,11... | collective-permute-start | bytes 3145736 | tf_op jit(solution)/shard_map/frame_out/ppermute | solution.py:18

commit v2 on v0

v2 whole, which is shorter than its diff:
```python
import functools
import math

import jax
import jax.numpy as jnp
from jax import lax
from jax.experimental import pallas as pl
from jax.experimental.pallas import tpu as pltpu
from jax.sharding import PartitionSpec as P

F32, BF16 = jnp.float32, jnp.bfloat16
W = 512
TOK = 256
CHUNK = 128
EXTRA = 256
VMEM_BYTES = 20 * 1024 * 1024
X, Y, Z = 1, 4, 16
VMEM = pl.BlockSpec(memory_space=pltpu.VMEM)
SMEM = pl.BlockSpec(memory_space=pltpu.SMEM)
ANY = pl.BlockSpec(memory_space=pl.ANY)


def swap_tok(value, bit):
    return lax.ppermute(value, "tok", [(i, i ^ bit) for i in range(lax.axis_size("tok"))])


def shift(value, stride, step, size=4):
    pairs = []
    for i in range(lax.axis_size("ctx")):
        c = i // stride % size
        pairs.append((i, i + ((c + step) % size - c) * stride))
    return lax.ppermute(value, "ctx", pairs)


def log2(x):
    return jnp.log(x) * (1.0 / math.log(2.0))


def column(row, out_ref):
    for start in range(0, row.shape[1], 128):
        block = jnp.broadcast_to(row[:, start : start + 128], (128, 128))
        out_ref[start : start + 128, :] = block.T


def wide(col, width):
    return jnp.concatenate([col] * (width // 128), axis=1)


def merge_lse(parts):
    highest = jnp.max(parts, axis=0, keepdims=True)
    return highest + log2(jnp.sum(jnp.exp2(parts - highest), axis=0, keepdims=True))


def row_slice(i, size):
    return pl.ds(pl.multiple_of(i * size, size), size)


def first_rows(scale, t_ref, f_ref, lse_ref, s_ref):
    i = pl.program_id(0)
    s_ref[i] = (
        lax.dot_general(t_ref[...], f_ref[...], (((1,), (1,)), ((), ())), preferred_element_type=F32) * scale
    )
    highest = total = None
    for c in range(0, t_ref.shape[0], CHUNK):
        s = s_ref[i, c : c + CHUNK, :].reshape(CHUNK // 8, 8, W)
        top = jnp.max(s, axis=0)
        if highest is None:
            highest = top
            total = jnp.sum(jnp.exp2(s - highest[None]), axis=0)
        else:
            top = jnp.maximum(highest, top)
            total = total * jnp.exp2(highest - top) + jnp.sum(jnp.exp2(s - top[None]), axis=0)
            highest = top
    top = jnp.max(highest, axis=0, keepdims=True)
    lse_ref[...] = top + log2(jnp.sum(total * jnp.exp2(highest - top), axis=0, keepdims=True))


def first_cols(s_ref, parts_ref, fm_ref, lse_ref, u_ref):
    i = pl.program_id(0)
    nt = s_ref.shape[1]

    @pl.when(i == 0)
    def _():
        u_ref[...] = log2(fm_ref[...]) - merge_lse(parts_ref[...])
        lse_ref[:, :, nt:] = jnp.broadcast_to(jnp.sum(fm_ref[...]).reshape(1, 1, 1), (lse_ref.shape[0], 1, EXTRA))

    step = 64
    found = []
    for r in range(0, TOK, step):
        rows = pl.ds(pl.multiple_of(i * TOK + r, step), step)
        highest = total = None
        for c in range(s_ref.shape[0]):
            for w in range(0, W, 256):
                lane = c * W + w
                s = s_ref[c, rows, w : w + 256] + u_ref[:, lane : lane + 256]
                low, high = s[:, :128], s[:, 128:]
                top = jnp.maximum(low, high)
                if highest is None:
                    highest = top
                    total = jnp.exp2(low - highest) + jnp.exp2(high - highest)
                else:
                    top = jnp.maximum(highest, top)
                    total = total * jnp.exp2(highest - top) + (jnp.exp2(low - top) + jnp.exp2(high - top))
                    highest = top
        top = jnp.max(highest, axis=1, keepdims=True)
        lse = top + log2(jnp.sum(total * jnp.exp2(highest - top), axis=1, keepdims=True))
        found.append(jnp.broadcast_to(lse, (step, 128)))
    row = jnp.concatenate(found).T[0:1]
    lse_ref[:, :, row_slice(i, TOK)] = jnp.broadcast_to(row[None], (lse_ref.shape[0], 1, TOK))


def second_rows(s_ref, parts_ref, tm_ref, u_ref, sum_ref, v_ref, mass_ref, e_ref, col_ref):
    i = pl.program_id(0)
    nt = s_ref.shape[1]
    nf = u_ref.shape[1]

    @pl.when(i == 0)
    def _():
        v = log2(tm_ref[...]) - merge_lse(parts_ref[:, :nt])
        v_ref[...] = v
        column(v, col_ref)
        mass_ref[...] = jnp.sum(parts_ref[:, nt : nt + 128], axis=0, keepdims=True)
        sum_ref[:, nf:] = jnp.broadcast_to(jnp.sum(tm_ref[...]).reshape(1, 1), (1, EXTRA))

    u = u_ref[:, row_slice(i, W)]
    total = None
    for c in range(0, nt, CHUNK):
        e = jnp.exp2(s_ref[i, c : c + CHUNK, :] + wide(col_ref[c : c + CHUNK, :], W) + u)
        e_ref[i, c : c + CHUNK, :] = e
        part = jnp.sum(e.reshape(CHUNK // 8, 8, W), axis=0)
        total = part if total is None else total + part
    sum_ref[:, row_slice(i, W)] = jnp.sum(total, axis=0, keepdims=True)


def col_sums(e_ref, parts_ref, fm_ref, sum_ref, alpha_ref, share_ref):
    i = pl.program_id(0)
    nf = fm_ref.shape[1]

    @pl.when(i == 0)
    def _():
        total = jnp.sum(parts_ref[...], axis=0, keepdims=True)
        alpha = fm_ref[...] / total[:, :nf]
        alpha_ref[...] = alpha
        share_ref[...] = alpha / wide(total[:, nf : nf + 128], nf)

    step = 64
    found = []
    for r in range(0, TOK, step):
        rows = pl.ds(pl.multiple_of(i * TOK + r, step), step)
        total = None
        for c in range(e_ref.shape[0]):
            p = e_ref[c, rows, :] * alpha_ref[:, c * W : (c + 1) * W]
            for w in range(0, W, 128):
                part = p[:, w : w + 128]
                total = part if total is None else total + part
        found.append(total)
    row = jnp.sum(jnp.concatenate(found).T, axis=0, keepdims=True)
    sum_ref[:, :, row_slice(i, TOK)] = jnp.broadcast_to(row[None], (sum_ref.shape[0], 1, TOK))


def token_parts(e_ref, alpha_ref, f_ref, out_ref):
    rows = row_slice(pl.program_id(0), TOK)
    acc = None
    for c in range(e_ref.shape[0]):
        p = (e_ref[c, rows, :] * alpha_ref[:, c * W : (c + 1) * W]).astype(BF16)
        part = jnp.dot(p, f_ref[c * W : (c + 1) * W, :], preferred_element_type=F32)
        acc = part if acc is None else acc + part
    out_ref[...] = acc.astype(BF16)


def frame_parts(base_ref, e_ref, parts_ref, tm_ref, share_ref, tt_ref, sum_ref, out_ref, total_ref, col_ref):
    i = pl.program_id(0)

    @pl.when(i == 0)
    def _():
        total = jnp.sum(parts_ref[...], axis=0, keepdims=True)
        total_ref[...] = total
        column(tm_ref[...] / total, col_ref)

    slab = base_ref[0] + i
    share = share_ref[:, row_slice(slab, W)]
    p = e_ref[slab] * wide(col_ref[...], W) * share
    sum_ref[...] = jnp.sum(p, axis=0, keepdims=True)
    out_ref[...] = jnp.dot(tt_ref[...], p.astype(BF16), preferred_element_type=F32).T.astype(BF16)


def place_tokens(place_ref, *refs):
    parts, out_ref, sems = refs[:8], refs[8], refs[9]
    x, y = place_ref[0], place_ref[1]
    block = parts[0].shape[0]
    piece = block // 4
    copies = []
    for side, (outer, inner) in enumerate(((x, y), (y, x))):
        for k in range(4):
            for j in range(4):
                start = side * 4 * block + lax.rem(outer + k, 4) * block + lax.rem(inner + j, 4) * piece
                copies.append(
                    pltpu.make_async_copy(
                        parts[side * 4 + k].at[pl.ds(j * piece, piece), :],
                        out_ref.at[pl.ds(pl.multiple_of(start, piece), piece), :],
                        sems.at[len(copies)],
                    )
                )
    for copy in copies:
        copy.start()
    for copy in copies:
        copy.wait()


def place_frames(core_ref, mine_ref, theirs_ref, out_ref, sems):
    half = mine_ref.shape[0]
    copies = []
    for k, ref in enumerate((mine_ref, theirs_ref)):
        start = lax.rem(core_ref[0] + k, 2) * half
        copies.append(
            pltpu.make_async_copy(ref, out_ref.at[pl.ds(pl.multiple_of(start, half), half), :], sems.at[k])
        )
    for copy in copies:
        copy.start()
    for copy in copies:
        copy.wait()


def whole(*shape):
    return pl.BlockSpec(shape, lambda i: (0,) * len(shape))


def rows(size, width):
    return pl.BlockSpec((size, width), lambda i: (i, 0))


def lanes(size):
    return pl.BlockSpec((1, size), lambda i: (0, i))


def f32(*shape):
    return jax.ShapeDtypeStruct(shape, F32)


def call(body, steps, in_specs, out_specs, out_shape, scratch=(), **kwargs):
    return pl.pallas_call(
        body,
        grid=(steps,),
        in_specs=in_specs,
        out_specs=out_specs,
        out_shape=out_shape,
        scratch_shapes=scratch,
        compiler_params=pltpu.CompilerParams(vmem_limit_bytes=VMEM_BYTES),
        **kwargs,
    )


def at(blocks, index):
    return lax.dynamic_index_in_dim(blocks, lax.rem(index, 4), keepdims=False)


def scatter(blocks, me, stride):
    total = at(blocks, me).astype(F32)
    for step in (1, 3, 2):
        total = total + shift(at(blocks, me + step), stride, step).astype(F32)
    return total.astype(BF16)


def gather(block, stride):
    return [block] + [shift(block, stride, -k) for k in (1, 2, 3)]


def shards(frames, tokens, frame_mass, token_mass):
    nf, d = frames.shape
    nt = tokens.shape[0]
    n_ctx, n_tok = lax.axis_size("ctx"), lax.axis_size("tok")
    scale = math.log2(math.e) / math.sqrt(d)
    fm, tm = frame_mass.reshape(1, nf), token_mass.reshape(1, nt)
    slabs, steps = nf // W, nt // TOK
    kept = pltpu.VMEM((slabs, nt, W), F32)
    ctx, core = lax.axis_index("ctx"), lax.axis_index("tok") % 2
    x, y = ctx % 4, ctx // 4 % 4

    lse, s = call(
        functools.partial(first_rows, scale), slabs, [whole(nt, d), rows(W, d)], [lanes(W), VMEM], [f32(1, nf), kept],
        name="first_rows",
    )(tokens, frames)
    with jax.named_scope("rows_one"):
        lse = lax.all_gather(lse, "tok", tiled=True)
    lse, u = call(
        first_cols, steps, [VMEM, whole(n_tok, nf), whole(1, nf)], [whole(n_ctx, 1, nt + EXTRA), whole(1, nf)],
        [f32(n_ctx, 1, nt + EXTRA), f32(1, nf)], name="first_cols",
    )(s, lse, fm)
    tokens_later, lse = lax.optimization_barrier((tokens, lse))
    with jax.named_scope("cols_one"):
        lse = lax.all_to_all(lse, "ctx", 0, 0)[:, 0]
    turned = tokens_later.T
    part, v, frame_total, e = call(
        second_rows, slabs, [VMEM, whole(n_ctx, nt + EXTRA), whole(1, nt), whole(1, nf)],
        [whole(1, nf + EXTRA), whole(1, nt), whole(1, 128), VMEM],
        [f32(1, nf + EXTRA), f32(1, nt), f32(1, 128), kept], [pltpu.VMEM((nt, 128), F32)],
        input_output_aliases={0: 3}, name="second_rows",
    )(s, lse, tm, u)
    with jax.named_scope("rows_two"):
        part = lax.all_gather(part, "tok", tiled=True)
    part, alpha, share = call(
        col_sums, steps, [VMEM, whole(n_tok, nf + EXTRA), whole(1, nf)],
        [whole(n_ctx, 1, nt), whole(1, nf), whole(1, nf)], [f32(n_ctx, 1, nt), f32(1, nf), f32(1, nf)], name="col_sums",
    )(e, part, fm)
    with jax.named_scope("cols_two"):
        part = lax.all_to_all(part, "ctx", 0, 0)[:, 0]
    token_part = call(
        token_parts, steps, [VMEM, whole(1, nf), whole(nf, d)], rows(TOK, d), jax.ShapeDtypeStruct((nt, d), BF16),
        name="token_parts",
    )(e, alpha, frames)

    def frame_half(which):
        base = (which * (slabs // 2)).reshape(1).astype(jnp.int32)
        return call(
            frame_parts, slabs // 2, [SMEM, VMEM, whole(n_ctx, nt), whole(1, nt), whole(1, nf), whole(d, nt)],
            [lanes(W), rows(W, d), whole(1, nt)],
            [f32(1, nf // 2), jax.ShapeDtypeStruct((nf // 2, d), BF16), f32(1, nt)], [pltpu.VMEM((nt, 128), F32)],
            name="frame_parts",
        )(base, e, part, tm, share, turned)

    with jax.named_scope("token_scatter"):
        half = token_part.reshape(2, 4, nt // 8, d)
        a = scatter(half[0], x, X)
        b = scatter(half[1], y, Y)
        a = scatter(a.reshape(4, nt // 32, d), y, Y)
        b = scatter(b.reshape(4, nt // 32, d), x, X)
        both = jnp.stack([a, b])
        both = both.astype(F32) + shift(both, Z, 1, 2).astype(F32)
    with jax.named_scope("frames_first_half"):
        their_sum, theirs, _ = frame_half(1 - core)
        theirs = swap_tok(theirs, 1)
    my_sum, mine, col_total = frame_half(core)
    with jax.named_scope("frame_rows"):
        my_sum = my_sum + swap_tok(their_sum, 1)
        mine = (mine.astype(F32) + theirs.astype(F32)).astype(BF16)
        my_sum = my_sum + swap_tok(my_sum, 2)
        other = swap_tok(mine, 2)
    with jax.named_scope("token_gather"):
        piece = nt // 32
        sums = [
            lax.dynamic_slice_in_dim(col_total[0], start, piece)
            for start in (x * 4 * piece + y * piece, nt // 2 + y * 4 * piece + x * piece)
        ]
        both = (both / jnp.stack(sums)[:, :, None]).astype(BF16)
        a = gather(jnp.concatenate(gather(both[0], Y)), X)
        b = gather(jnp.concatenate(gather(both[1], X)), Y)
        place = jnp.stack([x, y]).astype(jnp.int32)
        token_map = pl.pallas_call(
            place_tokens, in_specs=[SMEM] + [ANY] * 8, out_specs=ANY, out_shape=jax.ShapeDtypeStruct((nt, d), BF16),
            scratch_shapes=[pltpu.SemaphoreType.DMA((32,))], name="place_tokens",
        )(place, *a, *b)
    with jax.named_scope("frame_out"):
        mine = ((mine.astype(F32) + other.astype(F32)) / my_sum.reshape(-1, 1)).astype(BF16)
        theirs = swap_tok(mine, 1)
        their_sum = swap_tok(my_sum, 1)
        frame_map = pl.pallas_call(
            place_frames, in_specs=[SMEM, ANY, ANY], out_specs=ANY, out_shape=jax.ShapeDtypeStruct((nf, d), BF16),
            scratch_shapes=[pltpu.SemaphoreType.DMA((2,))], name="place_frames",
        )(core.reshape(1).astype(jnp.int32), mine, theirs)
        low = jnp.where(core == 0, my_sum, their_sum)
        high = jnp.where(core == 0, their_sum, my_sum)
        row_sum = jnp.concatenate([low, high], axis=1)[0]
        mass_ratio = row_sum / (frame_mass / frame_total[0, 0])
    return frame_map, token_map, mass_ratio


def solution(mesh):
    return jax.shard_map(
        shards,
        mesh=mesh,
        in_specs=(P("ctx", None), P("tok", None), P("ctx"), P("tok")),
        out_specs=(P("ctx", None), P("tok", None), P("ctx")),
        check_vma=False,
    )
```

time: 950 us -> 329 us (0.35)
  blocking collectives: 519 us -> 31.8 us
  waiting for transfers between devices: 312 us -> 46.8 us
  Pallas kernels: 0 us -> 163 us
  other arithmetic: 74.2 us -> 6.61 us
  starting transfers between devices: 0.08 us -> 45.5 us
  local copies, waits for them, and re-layouts: 3.23 us -> 32.4 us
  matrix products: 26.1 us -> 0 us
  between operations: 14.2 us -> 1.25 us
    psum x7 -> x0, blocking collectives: 349 us -> none  [the longest x2 160 us: col_logsum(): lax.psum(jnp.sum(jnp.exp(shifted - highest[None, :]), axis=0), 'ctx')]
    psum x2 -> x0, waiting for transfers between devices: 312 us -> none  [the longest x1 312 us: shards(): token_whole, col_sum = lax.psum((token_part, col_part), 'ctx')]
    pmax x4 -> x0, blocking collectives: 170 us -> none  [the longest x2 156 us: col_logsum(): highest = lax.pmax(jnp.max(shifted, axis=0), 'ctx')]
    pallas_call x0 -> x9, Pallas kernels: none -> 163 us  [the longest x1 65.6 us: shards(): pl.pallas_call(place_tokens, in_specs=[SMEM] + [ANY] * 8, out_specs=ANY,...]
    ppermute x0 -> x31, waiting for transfers between devices: none -> 46.8 us  [the longest x25 35.7 us: shift(): return lax.ppermute(value, 'ctx', pairs)]
    reduce_sum x7 -> x0, other arithmetic: 41.8 us -> none  [the longest x2 15.8 us: row_logsum(): jnp.sum(jnp.exp(shifted - highest[:, None]), axis=1)]
    ppermute x0 -> x31, starting transfers between devices: none -> 41.3 us  [the longest x25 36.2 us: shift(): return lax.ppermute(value, 'ctx', pairs)]
    dot_general x3 -> x0, matrix products: 26.1 us -> none  [the longest x1 10.5 us: shards(): lax.dot_general(transport, frames, (((0,), (0,)), ((), ())), preferred_el...]
  transfers between devices with their start and end apart: 2 -> 32, of which waited for: 1 -> 15; matrix products, arithmetic and copies ran while one was open for 2% -> 4% of each run, Pallas kernels for 0% -> 23%
where the time goes in v2:
time: 329 us; the launch traced here: 327 us
  Pallas kernels  163 us (50%)
  waiting for transfers between devices  46.8 us (14%)
  starting transfers between devices  45.5 us (14%)
  local copies, waits for them, and re-layouts  32.4 us (10%)
  blocking collectives  31.8 us (10%)
  other arithmetic  6.61 us (2%)
    pallas_call x1, Pallas kernels, shards(): pl.pallas_call(place_tokens, in_specs=[SMEM] + [ANY] * 8, out_specs=ANY,...  65.6 us
    pallas_call x1, Pallas kernels, shards(): pl.pallas_call(place_frames, in_specs=[SMEM, ANY, ANY], out_specs=ANY, ou...  64.6 us
    ppermute x25, starting transfers between devices, shift(): return lax.ppermute(value, 'ctx', pairs)  36.2 us
    ppermute x25, waiting for transfers between devices, shift(): return lax.ppermute(value, 'ctx', pairs)  35.7 us
    unnamed x48, local copies, waits for them, and re-layouts  26.2 us
    all_to_all x1, blocking collectives, shards(): lse = lax.all_to_all(lse, 'ctx', 0, 0)[:, 0]  17.7 us
    ppermute x6, waiting for transfers between devices, swap_tok(): lax.ppermute(value, 'tok', [(i, i ^ bit) for i in range(lax.axis_size('to...  11.1 us
    pallas_call x1, Pallas kernels, shards(): call(functools.partial(first_rows, scale), slabs, [whole(nt, d), rows(W,...  8.32 us
  transfers between devices with their start and end apart: 32, of which 15 were waited for; matrix products, arithmetic and copies ran while one was open for 4% of the time, Pallas kernels for 23%

profile of v2, /device:TPU:0, one launch (start us, length us, event | category | flops | bytes accessed | tf_op | source)
XLA Modules:
  0.0 327.4 jit_solution(7302222456381198892)
XLA Ops:
  0.6 1.6 copy-done.4
  2.2 1.6 copy-done.8
  3.8 8.3 %first_rows.1 = (f32[1,2048]{1,0:T(1,128)S(1)}, f32[4,2048,512]{2,1,0:T(8,128)S(1)}) custom-call(bf16[2048,512]{1,0:T(8,128)(2,1)S(1)} %copy-done.8, bf16[2048,512]{1,0:T(8,128)(2,1)S(1)} %copy-done.4), custom_call_target="tpu_custom_call" | custom-call | tf_op jit(solution)/shard_map/first_rows/pallas_call | solution.py:279
  12.1 7.2 %all-gather = f32[4,1,2048]{2,1,0:T(1,128)S(1)} all-gather(f32[1,1,2048]{2,1,0:T(1,128)S(1)} %bitcast.87), channel_id=1, replica_groups=mesh['ctx'=32,'tok'=4] {'tok'}, dimensions={0}, use_global_device_ids=true | all-gather | bytes 40960 | tf_op jit(solution)/shard_map/rows_one/all_gather | solution.py:284
  19.4 6.2 %first_cols.1 = (f32[32,1,2304]{2,1,0:T(1,128)S(1)}, f32[1,2048]{1,0:T(1,128)S(1)}) custom-call(f32[4,2048,512]{2,1,0:T(8,128)S(1)} %get-tuple-element.20.s_ref, f32[4,2048]{1,0:T(4,128)S(1)} %bitcast.80, f32[1,2048]{1,0:T(1,128)S(1)} %bitcast.84), custom_call_target="tpu_custom_call" | custom-call | tf_op jit(solution)/shard_map/first_cols/pallas_call | solution.py:285
  25.6 17.7 %all_to_all.10 = f32[32,1,2304]{2,1,0:T(1,128)S(1)} all-to-all(f32[32,1,2304]{2,1,0:T(1,128)S(1)} %get-tuple-element.23), channel_id=1, replica_groups=mesh['ctx'=32,'tok'=4] {'ctx'}, dimensions={0} | all-to-all | bytes 589824 | tf_op jit(solution)/shard_map/cols_one/all_to_all | solution.py:291
  43.4 3.6 %second_rows.1 = (f32[1,2304]{1,0:T(1,128)S(1)}, f32[1,2048]{1,0:T(1,128)}, f32[1,128]{1,0:T(1,128)S(1)}, f32[4,2048,512]{2,1,0:T(8,128)S(1)}) custom-call(f32[4,2048,512]{2,1,0:T(8,128)S(1)} %get-tuple-element.20.s_ref, f32[32,2304]{1,0:T(8,128)S(1)} %bitcast.78, f32[1,2048]{1,0:T(1,128)S(1)} %bitcast.81, ...), custom_call_target="tpu_custom_call", output_to_operand_aliasing={{3}: (0, {})} | custom-call | tf_op jit(solution)/shard_map/second_rows/pallas_call | solution.py:293
  47.0 6.8 %all-gather.1 = f32[4,1,2304]{2,1,0:T(1,128)S(1)} all-gather(f32[1,1,2304]{2,1,0:T(1,128)S(1)} %bitcast.86), channel_id=1, replica_groups=mesh['ctx'=32,'tok'=4] {'tok'}, dimensions={0}, use_global_device_ids=true | all-gather | bytes 46080 | tf_op jit(solution)/shard_map/rows_two/all_gather | solution.py:300
  53.8 2.7 col_sums.1
  56.5 4.2 %all-to-all-start.1 = ((f32[32,1,2048]{2,1,0:T(1,128)}), f32[32,1,2048]{2,1,0:T(1,128)S(1)}, u32[]{:S(2)}, u32[]{:S(2)}) async-start(f32[32,1,2048]{2,1,0:T(1,128)} %get-tuple-element.27), calls=%async_computation.1 | async-start | bytes 524288 | tf_op jit(solution)/shard_map/cols_two/all_to_all | solution.py:306
  60.7 2.9 copy.11
  63.6 5.8 %copy-done.1 = f32[4,2048,512]{2,1,0:T(8,128)S(1)} copy-done((f32[4,2048,512]{2,1,0:T(8,128)S(1)}, f32[4,2048,512]{2,1,0:T(8,128)}, u32[]{:S(2)}) %copy-start.1) | copy-done | bytes 16777240
  69.4 1.6 copy-done.5
  71.0 5.7 %token_parts.1 = bf16[2048,512]{1,0:T(8,128)(2,1)S(1)} custom-call(f32[4,2048,512]{2,1,0:T(8,128)S(1)} %copy-done.1, f32[1,2048]{1,0:T(1,128)S(1)} %get-tuple-element.34.alpha_ref, bf16[2048,512]{1,0:T(8,128)(2,1)S(1)} %copy-done.5), custom_call_target="tpu_custom_call" | custom-call | tf_op jit(solution)/shard_map/token_parts/pallas_call | solution.py:307
  78.1 5.8 %copy-done.2 = f32[4,2048,512]{2,1,0:T(8,128)S(1)} copy-done((f32[4,2048,512]{2,1,0:T(8,128)S(1)}, f32[4,2048,512]{2,1,0:T(8,128)}, u32[]{:S(2)}) %copy-start.2) | copy-done | bytes 16777240
  83.9 3.2 frame_parts.3
  90.2 1.8 collective-permute-start.5
  92.0 1.5 collective-permute-start.6
  93.4 2.1 collective-permute-start.7
  96.7 1.5 collective-permute-start.11
  98.2 5.8 %copy-done.3 = f32[4,2048,512]{2,1,0:T(8,128)S(1)} copy-done((f32[4,2048,512]{2,1,0:T(8,128)S(1)}, f32[4,2048,512]{2,1,0:T(8,128)}, u32[]{:S(2)}) %copy-start.3) | copy-done | bytes 16777240
  104.0 3.2 frame_parts.2
  107.2 2.0 collective-permute-start.12
  109.2 1.8 collective-permute-start.13
  112.3 1.9 collective-permute-start.10
  114.2 7.2 %collective-permute-done.12 = bf16[256,512]{1,0:T(8,128)(2,1)S(1)} collective-permute-done((bf16[256,512]{1,0:T(8,128)(2,1)S(1)}, bf16[256,512]{1,0:T(8,128)(2,1)S(1)}, u32[]{:S(2)}, u32[]{:S(2)}) %collective-permute-start.12) | collective-permute-done | bytes 262176 | tf_op jit(solution)/shard_map/token_scatter/ppermute | solution.py:32
  121.4 3.7 %collective-permute-start.9 = (bf16[64,512]{1,0:T(8,128)(2,1)S(1)}, bf16[64,512]{1,0:T(8,128)(2,1)S(1)}, u32[]{:S(2)}, u32[]{:S(2)}) collective-permute-start(bf16[64,512]{1,0:T(8,128)(2,1)S(1)} %get-tuple-element.47), channel_id=1, source_target_pairs={{0,48},{4,52},{8,56},{12,60},{16,0},{20,4},{24,8},{28,12},{32,16},... | collective-permute-start | bytes 196616 | tf_op jit(solution)/shard_map/token_scatter/ppermute | solution.py:32
  126.1 1.5 add_convert_fusion
  127.6 3.5 %collective-permute-start.1 = (bf16[1024,512]{1,0:T(8,128)(2,1)S(1)}, bf16[1024,512]{1,0:T(8,128)(2,1)S(1)}, u32[]{:S(2)}, u32[]{:S(2)}) collective-permute-start(bf16[1024,512]{1,0:T(8,128)(2,1)S(1)} %add_convert_fusion), channel_id=1, source_target_pairs={{0,2},{1,3},{2,0},{3,1},{4,6},{5,7},{6,4},{7,5},{8,10},{9,11},{10,... | collective-permute-start | bytes 3145736 | tf_op jit(solution)/shard_map/frame_rows/ppermute | solution.py:24
  131.8 2.7 collective-permute-start.15
  134.5 2.2 collective-permute-done.14
  137.0 3.3 collective-permute-done.16
  142.7 11.1 %collective-permute-done.3 = f32[1,1024]{1,0:T(1,128)S(1)} collective-permute-done((f32[1,1024]{1,0:T(1,128)S(1)}, f32[1,1024]{1,0:T(1,128)S(1)}, u32[]{:S(2)}, u32[]{:S(2)}) %collective-permute-start.3) | collective-permute-done | bytes 4128 | tf_op jit(solution)/shard_map/frame_rows/ppermute | solution.py:24
  156.2 1.5 collective-permute-start.25
  158.5 1.4 collective-permute-done.24
  159.9 2.4 collective-permute-done.25
  163.8 1.5 collective-permute-start.28
  165.2 2.1 collective-permute-start.19
  167.3 1.7 collective-permute-start.20
  169.7 5.4 %collective-permute-done.19 = bf16[64,512]{1,0:T(8,128)(2,1)S(1)} collective-permute-done((bf16[64,512]{1,0:T(8,128)(2,1)S(1)}, bf16[64,512]{1,0:T(8,128)(2,1)S(1)}, u32[]{:S(2)}, u32[]{:S(2)}) %collective-permute-start.19) | collective-permute-done | bytes 65568 | tf_op jit(solution)/shard_map/token_gather/ppermute | solution.py:32
  175.7 3.6 %collective-permute-start.29 = (bf16[256,512]{1,0:T(8,128)(2,1)S(1)}, bf16[256,512]{1,0:T(8,128)(2,1)S(1)}, u32[]{:S(2)}, u32[]{:S(2)}) collective-permute-start(bf16[256,512]{1,0:T(8,128)(2,1)S(1)} %pad_maximum_fusion.1.refs_4_), channel_id=1, source_target_pairs={{0,16},{4,20},{8,24},{12,28},{16,32},{20,36},{24,40},{28,44},{32,4... | collective-permute-start | bytes 786440 | tf_op jit(solution)/shard_map/token_gather/ppermute | solution.py:32
  180.6 1.4 collective-permute-start.22
  183.9 4.1 %collective-permute-done.29.refs_7_ = bf16[256,512]{1,0:T(8,128)(2,1)S(1)} collective-permute-done((bf16[256,512]{1,0:T(8,128)(2,1)S(1)}, bf16[256,512]{1,0:T(8,128)(2,1)S(1)}, u32[]{:S(2)}, u32[]{:S(2)}) %collective-permute-start.29) | collective-permute-done | bytes 262176 | tf_op jit(solution)/shard_map/token_gather/ppermute | solution.py:32
  188.0 1.4 collective-permute-done.21.refs_1_
  189.4 1.9 collective-permute-done.22.refs_2_
  192.0 3.9 %collective-permute-done.23.refs_3_ = bf16[256,512]{1,0:T(8,128)(2,1)} collective-permute-done((bf16[256,512]{1,0:T(8,128)(2,1)S(1)}, bf16[256,512]{1,0:T(8,128)(2,1)}, u32[]{:S(2)}, u32[]{:S(2)}) %collective-permute-start.23) | collective-permute-done | bytes 262176 | tf_op jit(solution)/shard_map/token_gather/ppermute | solution.py:32
  196.0 65.6 %place_tokens.1 = bf16[2048,512]{1,0:T(8,128)(2,1)} custom-call(s32[2]{0:T(128)} %pad_add_fusion.place_ref, bf16[256,512]{1,0:T(8,128)(2,1)} %copy-done.15, bf16[256,512]{1,0:T(8,128)(2,1)} %copy-done.19, bf16[256,512]{1,0:T(8,128)(2,1)} %copy-done.20, bf16[256,512]{1,0:T(8,128)(2,1)} %collective-permute-done.23.refs_3_, bf16[256,512]{1,0:T(8,128)(2,1)} %copy-done.14, ...), custom_call_target="tpu_custom_call" | custom-call | tf_op jit(solution)/shard_map/token_gather/place_tokens/pallas_call | solution.py:348
  262.6 64.6 %place_frames.1 = bf16[2048,512]{1,0:T(8,128)(2,1)} custom-call(s32[1]{0:T(128)} %bitcast.core_ref, bf16[1024,512]{1,0:T(8,128)(2,1)} %copy-done.11, bf16[1024,512]{1,0:T(8,128)(2,1)} %copy-done.13), custom_call_target="tpu_custom_call" | custom-call | tf_op jit(solution)/shard_map/frame_out/place_frames/pallas_call | solution.py:356
  (101 shorter events, 22.3 us)
Async XLA Ops:
  0.6 1.6 copy-start.4
  3.8 15.5 %copy-start.10 = (f32[2048]{0:T(1024)S(1)}, f32[2048]{0:T(1024)}, u32[]{:S(2)}) copy-start(f32[2048]{0:T(1024)} %param.6) | copy-start | bytes 24580
  19.4 24.0 %copy-start.9 = (f32[2048]{0:T(1024)S(1)}, f32[2048]{0:T(1024)}, u32[]{:S(2)}) copy-start(f32[2048]{0:T(1024)} %param.7) | copy-start | bytes 24580
  46.9 9.5 %copy-start = (f32[4,2048,512]{2,1,0:T(8,128)}, f32[4,2048,512]{2,1,0:T(8,128)S(1)}, u32[]{:S(2)}) copy-start(f32[4,2048,512]{2,1,0:T(8,128)S(1)} %get-tuple-element.25.e_ref) | copy-start | bytes 50331652
  56.5 21.6 %all-to-all-start.1 = ((f32[32,1,2048]{2,1,0:T(1,128)}), f32[32,1,2048]{2,1,0:T(1,128)S(1)}, u32[]{:S(2)}, u32[]{:S(2)}) async-start(f32[32,1,2048]{2,1,0:T(1,128)} %get-tuple-element.27), calls=%async_computation.1 | async-start | bytes 524288 | tf_op jit(solution)/shard_map/cols_two/all_to_all | solution.py:306
  63.6 5.8 %copy-start.1 = (f32[4,2048,512]{2,1,0:T(8,128)S(1)}, f32[4,2048,512]{2,1,0:T(8,128)}, u32[]{:S(2)}) copy-start(f32[4,2048,512]{2,1,0:T(8,128)} %copy-done) | copy-start | bytes 50331652
  78.1 5.8 %copy-start.2 = (f32[4,2048,512]{2,1,0:T(8,128)S(1)}, f32[4,2048,512]{2,1,0:T(8,128)}, u32[]{:S(2)}) copy-start(f32[4,2048,512]{2,1,0:T(8,128)} %copy-done) | copy-start | bytes 50331652
  83.9 3.3 %copy-start.7 = (bf16[2048,512]{1,0:T(8,128)(2,1)S(1)}, bf16[2048,512]{1,0:T(8,128)(2,1)}, u32[]{:S(2)}) copy-start(bf16[2048,512]{1,0:T(8,128)(2,1)} %copy-done.6) | copy-start | bytes 6291460
  87.1 39.0 %collective-permute-start = (bf16[1024,512]{1,0:T(8,128)(2,1)S(1)}, bf16[1024,512]{1,0:T(8,128)(2,1)}, u32[]{:S(2)}, u32[]{:S(2)}) collective-permute-start(bf16[1024,512]{1,0:T(8,128)(2,1)S(1)} %get-tuple-element.31), channel_id=1, source_target_pairs={{0,1},{1,0},{2,3},{3,2},{4,5},{5,4},{6,7},{7,6},{8,9},{9,8},{10,11... | collective-permute-start | bytes 3145736 | tf_op jit(solution)/shard_map/frames_first_half/ppermute | solution.py:24
  90.2 17.0 %collective-permute-start.5 = (bf16[256,512]{1,0:T(8,128)(2,1)}, bf16[256,512]{1,0:T(8,128)(2,1)}, u32[]{:S(2)}, u32[]{:S(2)}) collective-permute-start(bf16[256,512]{1,0:T(8,128)(2,1)} %get-tuple-element.39), channel_id=1, source_target_pairs={{0,4},{4,8},{8,12},{12,0},{16,20},{20,24},{24,28},{28,16},{32,36},... | collective-permute-start | bytes 786440 | tf_op jit(solution)/shard_map/token_scatter/ppermute | solution.py:32
  92.0 17.2 %collective-permute-start.6 = (bf16[256,512]{1,0:T(8,128)(2,1)}, bf16[256,512]{1,0:T(8,128)(2,1)}, u32[]{:S(2)}, u32[]{:S(2)}) collective-permute-start(bf16[256,512]{1,0:T(8,128)(2,1)} %get-tuple-element.41), channel_id=1, source_target_pairs={{0,12},{4,0},{8,4},{12,8},{16,28},{20,16},{24,20},{28,24},{32,44},... | collective-permute-start | bytes 786440 | tf_op jit(solution)/shard_map/token_scatter/ppermute | solution.py:32
  93.4 17.5 %collective-permute-start.7 = (bf16[256,512]{1,0:T(8,128)(2,1)}, bf16[256,512]{1,0:T(8,128)(2,1)}, u32[]{:S(2)}, u32[]{:S(2)}) collective-permute-start(bf16[256,512]{1,0:T(8,128)(2,1)} %get-tuple-element.40), channel_id=1, source_target_pairs={{0,8},{4,12},{8,0},{12,4},{16,24},{20,28},{24,16},{28,20},{32,40},... | collective-permute-start | bytes 786440 | tf_op jit(solution)/shard_map/token_scatter/ppermute | solution.py:32
  96.7 15.7 %collective-permute-start.11 = (bf16[256,512]{1,0:T(8,128)(2,1)S(1)}, bf16[256,512]{1,0:T(8,128)(2,1)S(1)}, u32[]{:S(2)}, u32[]{:S(2)}) collective-permute-start(bf16[256,512]{1,0:T(8,128)(2,1)S(1)} %get-tuple-element.42), channel_id=1, source_target_pairs={{0,16},{4,20},{8,24},{12,28},{16,32},{20,36},{24,40},{28,44},{32,4... | collective-permute-start | bytes 786440 | tf_op jit(solution)/shard_map/token_scatter/ppermute | solution.py:32
  98.2 5.8 %copy-start.3 = (f32[4,2048,512]{2,1,0:T(8,128)S(1)}, f32[4,2048,512]{2,1,0:T(8,128)}, u32[]{:S(2)}) copy-start(f32[4,2048,512]{2,1,0:T(8,128)} %copy-done) | copy-start | bytes 50331652
  107.2 14.2 %collective-permute-start.12 = (bf16[256,512]{1,0:T(8,128)(2,1)S(1)}, bf16[256,512]{1,0:T(8,128)(2,1)S(1)}, u32[]{:S(2)}, u32[]{:S(2)}) collective-permute-start(bf16[256,512]{1,0:T(8,128)(2,1)S(1)} %get-tuple-element.44), channel_id=1, source_target_pairs={{0,48},{4,52},{8,56},{12,60},{16,0},{20,4},{24,8},{28,12},{32,16},... | collective-permute-start | bytes 786440 | tf_op jit(solution)/shard_map/token_scatter/ppermute | solution.py:32
  109.2 12.1 %collective-permute-start.13 = (bf16[256,512]{1,0:T(8,128)(2,1)S(1)}, bf16[256,512]{1,0:T(8,128)(2,1)S(1)}, u32[]{:S(2)}, u32[]{:S(2)}) collective-permute-start(bf16[256,512]{1,0:T(8,128)(2,1)S(1)} %get-tuple-element.43), channel_id=1, source_target_pairs={{0,32},{4,36},{8,40},{12,44},{16,48},{20,52},{24,56},{28,60},{32,0... | collective-permute-start | bytes 786440 | tf_op jit(solution)/shard_map/token_scatter/ppermute | solution.py:32
  111.0 30.4 %collective-permute-start.2 = (f32[1,1024]{1,0:T(1,128)S(1)}, f32[1,1024]{1,0:T(1,128)S(1)}, u32[]{:S(2)}, u32[]{:S(2)}) collective-permute-start(f32[1,1024]{1,0:T(1,128)S(1)} %get-tuple-element.33), channel_id=1, source_target_pairs={{0,1},{1,0},{2,3},{3,2},{4,5},{5,4},{6,7},{7,6},{8,9},{9,8},{10,11... | collective-permute-start | bytes 12296 | tf_op jit(solution)/shard_map/frame_rows/ppermute | solution.py:24
  112.3 18.8 %collective-permute-start.10 = (bf16[64,512]{1,0:T(8,128)(2,1)S(1)}, bf16[64,512]{1,0:T(8,128)(2,1)S(1)}, u32[]{:S(2)}, u32[]{:S(2)}) collective-permute-start(bf16[64,512]{1,0:T(8,128)(2,1)S(1)} %get-tuple-element.46), channel_id=1, source_target_pairs={{0,32},{4,36},{8,40},{12,44},{16,48},{20,52},{24,56},{28,60},{32,0... | collective-permute-start | bytes 196616 | tf_op jit(solution)/shard_map/token_scatter/ppermute | solution.py:32
  121.4 10.5 %collective-permute-start.8 = (bf16[64,512]{1,0:T(8,128)(2,1)S(1)}, bf16[64,512]{1,0:T(8,128)(2,1)S(1)}, u32[]{:S(2)}, u32[]{:S(2)}) collective-permute-start(bf16[64,512]{1,0:T(8,128)(2,1)S(1)} %get-tuple-element.45), channel_id=1, source_target_pairs={{0,16},{4,20},{8,24},{12,28},{16,32},{20,36},{24,40},{28,44},{32,4... | collective-permute-start | bytes 196616 | tf_op jit(solution)/shard_map/token_scatter/ppermute | solution.py:32
  121.4 13.1 %collective-permute-start.9 = (bf16[64,512]{1,0:T(8,128)(2,1)S(1)}, bf16[64,512]{1,0:T(8,128)(2,1)S(1)}, u32[]{:S(2)}, u32[]{:S(2)}) collective-permute-start(bf16[64,512]{1,0:T(8,128)(2,1)S(1)} %get-tuple-element.47), channel_id=1, source_target_pairs={{0,48},{4,52},{8,56},{12,60},{16,0},{20,4},{24,8},{28,12},{32,16},... | collective-permute-start | bytes 196616 | tf_op jit(solution)/shard_map/token_scatter/ppermute | solution.py:32
  127.6 26.9 %collective-permute-start.1 = (bf16[1024,512]{1,0:T(8,128)(2,1)S(1)}, bf16[1024,512]{1,0:T(8,128)(2,1)S(1)}, u32[]{:S(2)}, u32[]{:S(2)}) collective-permute-start(bf16[1024,512]{1,0:T(8,128)(2,1)S(1)} %add_convert_fusion), channel_id=1, source_target_pairs={{0,2},{1,3},{2,0},{3,1},{4,6},{5,7},{6,4},{7,5},{8,10},{9,11},{10,... | collective-permute-start | bytes 3145736 | tf_op jit(solution)/shard_map/frame_rows/ppermute | solution.py:24
  131.2 5.5 %collective-permute-start.14 = (bf16[64,512]{1,0:T(8,128)(2,1)S(1)}, bf16[64,512]{1,0:T(8,128)(2,1)S(1)}, u32[]{:S(2)}, u32[]{:S(2)}) collective-permute-start(bf16[64,512]{1,0:T(8,128)(2,1)S(1)} %get-tuple-element.48), channel_id=1, source_target_pairs={{0,4},{4,8},{8,12},{12,0},{16,20},{20,24},{24,28},{28,16},{32,36},... | collective-permute-start | bytes 196616 | tf_op jit(solution)/shard_map/token_scatter/ppermute | solution.py:32
  131.8 5.2 %collective-permute-start.15 = (bf16[64,512]{1,0:T(8,128)(2,1)S(1)}, bf16[64,512]{1,0:T(8,128)(2,1)S(1)}, u32[]{:S(2)}, u32[]{:S(2)}) collective-permute-start(bf16[64,512]{1,0:T(8,128)(2,1)S(1)} %get-tuple-element.50), channel_id=1, source_target_pairs={{0,12},{4,0},{8,4},{12,8},{16,28},{20,16},{24,20},{28,24},{32,44},... | collective-permute-start | bytes 196616 | tf_op jit(solution)/shard_map/token_scatter/ppermute | solution.py:32
  134.5 5.8 %collective-permute-start.16 = (bf16[64,512]{1,0:T(8,128)(2,1)S(1)}, bf16[64,512]{1,0:T(8,128)(2,1)S(1)}, u32[]{:S(2)}, u32[]{:S(2)}) collective-permute-start(bf16[64,512]{1,0:T(8,128)(2,1)S(1)} %get-tuple-element.49), channel_id=1, source_target_pairs={{0,8},{4,12},{8,0},{12,4},{16,24},{20,28},{24,16},{28,20},{32,40},... | collective-permute-start | bytes 196616 | tf_op jit(solution)/shard_map/token_scatter/ppermute | solution.py:32
  140.3 14.1 %collective-permute-start.17 = (bf16[2,64,512]{2,1,0:T(8,128)(2,1)S(1)}, bf16[2,64,512]{2,1,0:T(8,128)(2,1)S(1)}, u32[]{:S(2)}, u32[]{:S(2)}) collective-permute-start(bf16[2,64,512]{2,1,0:T(8,128)(2,1)S(1)} %pad_maximum_fusion.2), channel_id=1, source_target_pairs={{0,64},{4,68},{8,72},{12,76},{16,80},{20,84},{24,88},{28,92},{32,9... | collective-permute-start | bytes 393224 | tf_op jit(solution)/shard_map/token_scatter/ppermute | solution.py:32
  141.4 12.5 %collective-permute-start.3 = (f32[1,1024]{1,0:T(1,128)S(1)}, f32[1,1024]{1,0:T(1,128)S(1)}, u32[]{:S(2)}, u32[]{:S(2)}) collective-permute-start(f32[1,1024]{1,0:T(1,128)S(1)} %add.135), channel_id=1, source_target_pairs={{0,2},{1,3},{2,0},{3,1},{4,6},{5,7},{6,4},{7,5},{8,10},{9,11},{10,... | collective-permute-start | bytes 12296 | tf_op jit(solution)/shard_map/frame_rows/ppermute | solution.py:24
  154.9 106.7 %copy-start.11 = (bf16[1024,512]{1,0:T(8,128)(2,1)}, bf16[1024,512]{1,0:T(8,128)(2,1)S(1)}, u32[]{:S(2)}) copy-start(bf16[1024,512]{1,0:T(8,128)(2,1)S(1)} %divide_convert_fusion.mine_ref) | copy-start | bytes 3145732
  154.9 106.7 %collective-permute-start.4 = (bf16[1024,512]{1,0:T(8,128)(2,1)S(1)}, bf16[1024,512]{1,0:T(8,128)(2,1)S(1)}, u32[]{:S(2)}, u32[]{:S(2)}) collective-permute-start(bf16[1024,512]{1,0:T(8,128)(2,1)S(1)} %divide_convert_fusion.mine_ref), channel_id=1, source_target_pairs={{0,1},{1,0},{2,3},{3,2},{4,5},{5,4},{6,7},{7,6},{8,9},{9,8},{10,11... | collective-permute-start | bytes 3145736 | tf_op jit(solution)/shard_map/frame_out/ppermute | solution.py:24
  155.0 5.0 %collective-permute-start.24 = (bf16[64,512]{1,0:T(8,128)(2,1)S(1)}, bf16[64,512]{1,0:T(8,128)(2,1)S(1)}, u32[]{:S(2)}, u32[]{:S(2)}) collective-permute-start(bf16[64,512]{1,0:T(8,128)(2,1)S(1)} %get-tuple-element.51), channel_id=1, source_target_pairs={{0,12},{4,0},{8,4},{12,8},{16,28},{20,16},{24,20},{28,24},{32,44},... | collective-permute-start | bytes 196616 | tf_op jit(solution)/shard_map/token_gather/ppermute | solution.py:32
  156.2 6.1 %collective-permute-start.25 = (bf16[64,512]{1,0:T(8,128)(2,1)S(1)}, bf16[64,512]{1,0:T(8,128)(2,1)S(1)}, u32[]{:S(2)}, u32[]{:S(2)}) collective-permute-start(bf16[64,512]{1,0:T(8,128)(2,1)S(1)} %get-tuple-element.51), channel_id=1, source_target_pairs={{0,8},{4,12},{8,0},{12,4},{16,24},{20,28},{24,16},{28,20},{32,40},... | collective-permute-start | bytes 196616 | tf_op jit(solution)/shard_map/token_gather/ppermute | solution.py:32
  157.7 5.7 %collective-permute-start.26 = (bf16[64,512]{1,0:T(8,128)(2,1)S(1)}, bf16[64,512]{1,0:T(8,128)(2,1)S(1)}, u32[]{:S(2)}, u32[]{:S(2)}) collective-permute-start(bf16[64,512]{1,0:T(8,128)(2,1)S(1)} %get-tuple-element.51), channel_id=1, source_target_pairs={{0,4},{4,8},{8,12},{12,0},{16,20},{20,24},{24,28},{28,16},{32,36},... | collective-permute-start | bytes 196616 | tf_op jit(solution)/shard_map/token_gather/ppermute | solution.py:32
  158.2 9.1 %collective-permute-start.18 = (bf16[64,512]{1,0:T(8,128)(2,1)S(1)}, bf16[64,512]{1,0:T(8,128)(2,1)S(1)}, u32[]{:S(2)}, u32[]{:S(2)}) collective-permute-start(bf16[64,512]{1,0:T(8,128)(2,1)S(1)} %get-tuple-element.52), channel_id=1, source_target_pairs={{0,48},{4,52},{8,56},{12,60},{16,0},{20,4},{24,8},{28,12},{32,16},... | collective-permute-start | bytes 196616 | tf_op jit(solution)/shard_map/token_gather/ppermute | solution.py:32
  163.4 32.6 %copy-start.14 = (bf16[256,512]{1,0:T(8,128)(2,1)}, bf16[256,512]{1,0:T(8,128)(2,1)S(1)}, u32[]{:S(2)}) copy-start(bf16[256,512]{1,0:T(8,128)(2,1)S(1)} %pad_maximum_fusion.1.refs_4_) | copy-start | bytes 786436
  163.4 17.2 %collective-permute-start.27 = (bf16[256,512]{1,0:T(8,128)(2,1)S(1)}, bf16[256,512]{1,0:T(8,128)(2,1)S(1)}, u32[]{:S(2)}, u32[]{:S(2)}) collective-permute-start(bf16[256,512]{1,0:T(8,128)(2,1)S(1)} %pad_maximum_fusion.1.refs_4_), channel_id=1, source_target_pairs={{0,48},{4,52},{8,56},{12,60},{16,0},{20,4},{24,8},{28,12},{32,16},... | collective-permute-start | bytes 786440 | tf_op jit(solution)/shard_map/token_gather/ppermute | solution.py:32
  163.8 18.2 %collective-permute-start.28 = (bf16[256,512]{1,0:T(8,128)(2,1)S(1)}, bf16[256,512]{1,0:T(8,128)(2,1)S(1)}, u32[]{:S(2)}, u32[]{:S(2)}) collective-permute-start(bf16[256,512]{1,0:T(8,128)(2,1)S(1)} %pad_maximum_fusion.1.refs_4_), channel_id=1, source_target_pairs={{0,32},{4,36},{8,40},{12,44},{16,48},{20,52},{24,56},{28,60},{32,0... | collective-permute-start | bytes 786440 | tf_op jit(solution)/shard_map/token_gather/ppermute | solution.py:32
  165.2 9.9 %collective-permute-start.19 = (bf16[64,512]{1,0:T(8,128)(2,1)S(1)}, bf16[64,512]{1,0:T(8,128)(2,1)S(1)}, u32[]{:S(2)}, u32[]{:S(2)}) collective-permute-start(bf16[64,512]{1,0:T(8,128)(2,1)S(1)} %get-tuple-element.52), channel_id=1, source_target_pairs={{0,32},{4,36},{8,40},{12,44},{16,48},{20,52},{24,56},{28,60},{32,0... | collective-permute-start | bytes 196616 | tf_op jit(solution)/shard_map/token_gather/ppermute | solution.py:32
  167.3 7.8 %copy-start.21 = (bf16[64,512]{1,0:T(8,128)(2,1)}, bf16[64,512]{1,0:T(8,128)(2,1)S(1)}, u32[]{:S(2)}) copy-start(bf16[64,512]{1,0:T(8,128)(2,1)S(1)} %collective-permute-done.18) | copy-start | bytes 196612
  167.3 8.4 %collective-permute-start.20 = (bf16[64,512]{1,0:T(8,128)(2,1)S(1)}, bf16[64,512]{1,0:T(8,128)(2,1)S(1)}, u32[]{:S(2)}, u32[]{:S(2)}) collective-permute-start(bf16[64,512]{1,0:T(8,128)(2,1)S(1)} %get-tuple-element.52), channel_id=1, source_target_pairs={{0,16},{4,20},{8,24},{12,28},{16,32},{20,36},{24,40},{28,44},{32,4... | collective-permute-start | bytes 196616 | tf_op jit(solution)/shard_map/token_gather/ppermute | solution.py:32
  175.1 5.0 %collective-permute-start.30 = (f32[1,1024]{1,0:T(1,128)S(1)}, f32[1,1024]{1,0:T(1,128)S(1)}, u32[]{:S(2)}, u32[]{:S(2)}) collective-permute-start(f32[1,1024]{1,0:T(1,128)S(1)} %add.136), channel_id=1, source_target_pairs={{0,1},{1,0},{2,3},{3,2},{4,5},{5,4},{6,7},{7,6},{8,9},{9,8},{10,11... | collective-permute-start | bytes 12296 | tf_op jit(solution)/shard_map/frame_out/ppermute | solution.py:24
  175.7 12.3 %collective-permute-start.29 = (bf16[256,512]{1,0:T(8,128)(2,1)S(1)}, bf16[256,512]{1,0:T(8,128)(2,1)S(1)}, u32[]{:S(2)}, u32[]{:S(2)}) collective-permute-start(bf16[256,512]{1,0:T(8,128)(2,1)S(1)} %pad_maximum_fusion.1.refs_4_), channel_id=1, source_target_pairs={{0,16},{4,20},{8,24},{12,28},{16,32},{20,36},{24,40},{28,44},{32,4... | collective-permute-start | bytes 786440 | tf_op jit(solution)/shard_map/token_gather/ppermute | solution.py:32
  180.2 15.8 %copy-start.15 = (bf16[256,512]{1,0:T(8,128)(2,1)}, bf16[256,512]{1,0:T(8,128)(2,1)S(1)}, u32[]{:S(2)}) copy-start(bf16[256,512]{1,0:T(8,128)(2,1)S(1)} %pad_maximum_fusion.refs_0_) | copy-start | bytes 786436
  180.2 9.2 %collective-permute-start.21 = (bf16[256,512]{1,0:T(8,128)(2,1)S(1)}, bf16[256,512]{1,0:T(8,128)(2,1)S(1)}, u32[]{:S(2)}, u32[]{:S(2)}) collective-permute-start(bf16[256,512]{1,0:T(8,128)(2,1)S(1)} %pad_maximum_fusion.refs_0_), channel_id=1, source_target_pairs={{0,12},{4,0},{8,4},{12,8},{16,28},{20,16},{24,20},{28,24},{32,44},... | collective-permute-start | bytes 786440 | tf_op jit(solution)/shard_map/token_gather/ppermute | solution.py:32
  180.6 15.4 %copy-start.16 = (bf16[256,512]{1,0:T(8,128)(2,1)}, bf16[256,512]{1,0:T(8,128)(2,1)S(1)}, u32[]{:S(2)}) copy-start(bf16[256,512]{1,0:T(8,128)(2,1)S(1)} %collective-permute-done.27.refs_5_) | copy-start | bytes 786436
  180.6 10.7 %collective-permute-start.22 = (bf16[256,512]{1,0:T(8,128)(2,1)S(1)}, bf16[256,512]{1,0:T(8,128)(2,1)S(1)}, u32[]{:S(2)}, u32[]{:S(2)}) collective-permute-start(bf16[256,512]{1,0:T(8,128)(2,1)S(1)} %pad_maximum_fusion.refs_0_), channel_id=1, source_target_pairs={{0,8},{4,12},{8,0},{12,4},{16,24},{20,28},{24,16},{28,20},{32,40},... | collective-permute-start | bytes 786440 | tf_op jit(solution)/shard_map/token_gather/ppermute | solution.py:32
  182.0 14.0 %copy-start.17 = (bf16[256,512]{1,0:T(8,128)(2,1)}, bf16[256,512]{1,0:T(8,128)(2,1)S(1)}, u32[]{:S(2)}) copy-start(bf16[256,512]{1,0:T(8,128)(2,1)S(1)} %collective-permute-done.28.refs_6_) | copy-start | bytes 786436
  182.0 14.0 %collective-permute-start.23 = (bf16[256,512]{1,0:T(8,128)(2,1)S(1)}, bf16[256,512]{1,0:T(8,128)(2,1)}, u32[]{:S(2)}, u32[]{:S(2)}) collective-permute-start(bf16[256,512]{1,0:T(8,128)(2,1)S(1)} %pad_maximum_fusion.refs_0_), channel_id=1, source_target_pairs={{0,4},{4,8},{8,12},{12,0},{16,20},{20,24},{24,28},{28,16},{32,36},... | collective-permute-start | bytes 786440 | tf_op jit(solution)/shard_map/token_gather/ppermute | solution.py:32
  188.0 8.0 %copy-start.18 = (bf16[256,512]{1,0:T(8,128)(2,1)}, bf16[256,512]{1,0:T(8,128)(2,1)S(1)}, u32[]{:S(2)}) copy-start(bf16[256,512]{1,0:T(8,128)(2,1)S(1)} %collective-permute-done.29.refs_7_) | copy-start | bytes 786436
  189.4 1.9 copy-start.19
  (6 other events, 7.2 us)

commit v3 on v2

v3 whole, which is shorter than its diff:
```python
import functools
import math

import jax
import jax.numpy as jnp
from jax import lax
from jax.experimental import pallas as pl
from jax.experimental.pallas import tpu as pltpu
from jax.sharding import PartitionSpec as P

F32, BF16 = jnp.float32, jnp.bfloat16
W = 256
TOK = 256
CHUNK = 128
SPLIT = 4
HELD = 4
EXTRA = 256
ORDER = ((16, 2), (1, 4), (4, 4))
VMEM_BYTES = 20 * 1024 * 1024
VMEM = pl.BlockSpec(memory_space=pltpu.VMEM)
SMEM = pl.BlockSpec(memory_space=pltpu.SMEM)
ANY = pl.BlockSpec(memory_space=pl.ANY)


def swap_tok(value, bit):
    return lax.ppermute(value, "tok", [(i, i ^ bit) for i in range(lax.axis_size("tok"))])


def shift(value, stride, step, size):
    pairs = []
    for i in range(lax.axis_size("ctx")):
        c = i // stride % size
        pairs.append((i, i + ((c + step) % size - c) * stride))
    return lax.ppermute(value, "ctx", pairs)


def log2(x):
    return jnp.log(x) * (1.0 / math.log(2.0))


def column(row, out_ref):
    for start in range(0, row.shape[1], 128):
        block = jnp.broadcast_to(row[:, start : start + 128], (128, 128))
        out_ref[start : start + 128, :] = block.T


def wide(col, width):
    return jnp.concatenate([col] * (width // 128), axis=1)


def merge_lse(parts):
    highest = functools.reduce(jnp.maximum, parts)
    return highest + log2(sum(jnp.exp2(part - highest) for part in parts))


def ring(value, stride, size):
    return [value] + [shift(value, stride, step, size) for step in range(1, size)]


def row_slice(i, size):
    return pl.ds(pl.multiple_of(i * size, size), size)


def turn(in_ref, out_ref):
    out_ref[...] = in_ref[...].T


def first_rows(scale, *refs):
    t_refs, (f_ref, lse_ref, s_ref) = refs[:SPLIT], refs[SPLIT:]
    i = pl.program_id(0)
    tokens = jnp.concatenate([t_ref[...] for t_ref in t_refs])
    s_ref[i] = (
        lax.dot_general(tokens, f_ref[...], (((1,), (1,)), ((), ())), preferred_element_type=F32) * scale
    )
    highest = total = None
    for c in range(0, tokens.shape[0], CHUNK):
        s = s_ref[i, c : c + CHUNK, :].reshape(CHUNK // 8, 8, W)
        top = jnp.max(s, axis=0)
        if highest is None:
            highest = top
            total = jnp.sum(jnp.exp2(s - highest[None]), axis=0)
        else:
            top = jnp.maximum(highest, top)
            total = total * jnp.exp2(highest - top) + jnp.sum(jnp.exp2(s - top[None]), axis=0)
            highest = top
    top = jnp.max(highest, axis=0, keepdims=True)
    lse_ref[...] = top + log2(jnp.sum(total * jnp.exp2(highest - top), axis=0, keepdims=True))


def first_cols(s_ref, all_ref, fm_ref, lse_ref, u_ref, mass_ref):
    i = pl.program_id(0)

    @pl.when(i == 0)
    def _():
        u_ref[...] = log2(fm_ref[...]) - all_ref[...]
        mass_ref[...] = jnp.broadcast_to(jnp.sum(fm_ref[...]).reshape(1, 1), (1, 128))

    step = 16
    found = []
    for r in range(0, TOK, step):
        rows = pl.ds(pl.multiple_of(i * TOK + r, step), step)
        tiles = [
            s_ref[c, rows, w : w + 128] + u_ref[:, c * W + w : c * W + w + 128]
            for c in range(s_ref.shape[0])
            for w in range(0, W, 128)
        ]
        highest = functools.reduce(jnp.maximum, tiles)
        total = sum(jnp.exp2(tile - highest) for tile in tiles)
        top = jnp.max(highest, axis=1, keepdims=True)
        lse = top + log2(jnp.sum(total * jnp.exp2(highest - top), axis=1, keepdims=True))
        found.append(jnp.broadcast_to(lse, (step, 128)))
    lse_ref[...] = jnp.concatenate(found).T[0:1]


def second_rows(s_ref, all_ref, tm_ref, u_ref, sum_ref, e_ref, col_ref):
    i = pl.program_id(0)
    nt = s_ref.shape[1]
    nf = u_ref.shape[1]

    @pl.when(i == 0)
    def _():
        column(log2(tm_ref[...]) - all_ref[...], col_ref)
        sum_ref[:, nf:] = jnp.broadcast_to(jnp.sum(tm_ref[...]).reshape(1, 1), (1, EXTRA))

    u = u_ref[:, row_slice(i, W)]
    total = None
    for c in range(0, nt, CHUNK):
        e = jnp.exp2(s_ref[i, c : c + CHUNK, :] + wide(col_ref[c : c + CHUNK, :], W) + u)
        e_ref[i, c : c + CHUNK, :] = e
        part = jnp.sum(e.reshape(CHUNK // 8, 8, W), axis=0)
        total = part if total is None else total + part
    sum_ref[:, row_slice(i, W)] = jnp.sum(total, axis=0, keepdims=True)


def second_cols(e_ref, total_ref, fm_ref, f_ref, sum_ref, out_ref, share_ref, stored_ref, alpha_ref, sems):
    i = pl.program_id(0)
    nf = fm_ref.shape[1]

    def store(step):
        some = row_slice(step, TOK)
        return pltpu.make_async_copy(e_ref.at[:, some, :], stored_ref.at[:, some, :], sems.at[step])

    store(i).start()

    @pl.when(i == 0)
    def _():
        alpha = fm_ref[...] / total_ref[:, :nf]
        alpha_ref[...] = alpha
        share_ref[...] = alpha / wide(total_ref[:, nf : nf + 128], nf)

    rows = row_slice(i, TOK)
    acc = total = None
    for c in range(e_ref.shape[0]):
        p = e_ref[c, rows, :] * alpha_ref[:, c * W : (c + 1) * W]
        part = p[:, :128]
        for w in range(128, W, 128):
            part = part + p[:, w : w + 128]
        total = part if total is None else total + part
        part = jnp.dot(p.astype(BF16), f_ref[c * W : (c + 1) * W, :], preferred_element_type=F32)
        acc = part if acc is None else acc + part
    sum_ref[...] = jnp.sum(total.T, axis=0, keepdims=True)
    out_ref[...] = acc.astype(BF16)

    @pl.when(i == pl.num_programs(0) - 1)
    def _():
        for step in range(e_ref.shape[1] // TOK):
            store(step).wait()


def frame_parts(
    base_ref, e_ref, total_ref, tm_ref, share_ref, tt_ref, sum_ref, out_ref, col_ref, held_ref, sems
):
    i = pl.program_id(0)
    slabs = pl.num_programs(0)

    def fetch(k):
        slot = lax.rem(k, HELD)
        return pltpu.make_async_copy(e_ref.at[lax.rem(base_ref[0] + k, slabs)], held_ref.at[slot], sems.at[slot])

    @pl.when(i == 0)
    def _():
        for k in range(HELD - 1):
            fetch(k).start()
        column(tm_ref[...] / total_ref[...], col_ref)

    @pl.when(i + HELD - 1 < slabs)
    def _():
        fetch(i + HELD - 1).start()

    fetch(i).wait()
    share = share_ref[:, row_slice(lax.rem(base_ref[0] + i, slabs), W)]
    p = held_ref[lax.rem(i, HELD)] * wide(col_ref[...], W) * share
    sum_ref[...] = jnp.sum(p, axis=0, keepdims=True)
    out_ref[...] = jnp.dot(tt_ref[...], p.astype(BF16), preferred_element_type=F32).T.astype(BF16)


def sum_pieces(*refs):
    out_ref = refs[-1]
    rows = refs[0].shape[1]
    for k, pieces_ref in enumerate(refs[:-1]):
        acc = pieces_ref[0].astype(F32)
        for n in range(1, pieces_ref.shape[0]):
            acc = acc + pieces_ref[n].astype(F32)
        out_ref[k * rows : (k + 1) * rows, :] = acc.astype(BF16)


def finish_pieces(mine_ref, other_ref, total_ref, out_ref, col_ref, done_ref, sems):
    column(total_ref[...], col_ref)
    d = mine_ref.shape[1]
    done = (mine_ref[...].astype(F32) + other_ref[...].astype(F32)) / wide(col_ref[...], d)
    done_ref[...] = done.astype(BF16)
    copies = [pltpu.make_async_copy(done_ref, out_ref.at[k], sems.at[k]) for k in range(out_ref.shape[0])]
    for copy in copies:
        copy.start()
    for copy in copies:
        copy.wait()


def place_tokens(pieces_ref, out_ref, held_ref, sems, out_sems):
    count, rows = pieces_ref.shape[0], pieces_ref.shape[1]
    ins = [pltpu.make_async_copy(pieces_ref.at[k], held_ref.at[k], sems.at[k]) for k in range(count)]
    outs = [
        pltpu.make_async_copy(held_ref.at[k], out_ref.at[k * rows : (k + 1) * rows, :], out_sems.at[k])
        for k in range(count)
    ]
    for copy in ins:
        copy.start()
    for k in range(count):
        ins[k].wait()
        outs[k].start()
    for copy in outs:
        copy.wait()


def finish_frames(mine_ref, other_ref, total_ref, out_ref, col_ref):
    column(total_ref[...], col_ref)
    rows, d = mine_ref.shape
    for r in range(0, rows, 128):
        some = slice(r, r + 128)
        done = (mine_ref[some, :].astype(F32) + other_ref[some, :].astype(F32)) / wide(col_ref[some, :], d)
        out_ref[some, :] = done.astype(BF16)


def place_frames(core_ref, mine_ref, theirs_ref, out_ref, sems):
    half = mine_ref.shape[0]
    copies = []
    for k, ref in enumerate((mine_ref, theirs_ref)):
        start = lax.rem(core_ref[0] + k, 2) * half
        copies.append(
            pltpu.make_async_copy(ref, out_ref.at[pl.ds(pl.multiple_of(start, half), half), :], sems.at[k])
        )
    for copy in copies:
        copy.start()
    for copy in copies:
        copy.wait()


def whole(*shape):
    return pl.BlockSpec(shape, lambda i: (0,) * len(shape))


def rows(size, width):
    return pl.BlockSpec((size, width), lambda i: (i, 0))


def lanes(size):
    return pl.BlockSpec((1, size), lambda i: (0, i))


def f32(*shape):
    return jax.ShapeDtypeStruct(shape, F32)


def call(body, steps, in_specs, out_specs, out_shape, scratch=(), **kwargs):
    return pl.pallas_call(
        body,
        grid=(steps,),
        in_specs=in_specs,
        out_specs=out_specs,
        out_shape=out_shape,
        scratch_shapes=scratch,
        compiler_params=pltpu.CompilerParams(vmem_limit_bytes=VMEM_BYTES),
        **kwargs,
    )


def shards(frames, tokens, frame_mass, token_mass):
    nf, d = frames.shape
    nt = tokens.shape[0]
    n_ctx = lax.axis_size("ctx")
    scale = math.log2(math.e) / math.sqrt(d)
    fm, tm = frame_mass.reshape(1, nf), token_mass.reshape(1, nt)
    slabs, steps = nf // W, nt // TOK
    kept = pltpu.VMEM((slabs, nt, W), F32)
    ctx, core = lax.axis_index("ctx"), lax.axis_index("tok") % 2
    hbm = pl.BlockSpec(memory_space=pltpu.HBM)

    lse, s = call(
        functools.partial(first_rows, scale), slabs,
        [pl.BlockSpec((nt // SPLIT, d), lambda i, k=k: (k, 0)) for k in range(SPLIT)] + [rows(W, d)],
        [lanes(W), VMEM], [f32(1, nf), kept], name="first_rows",
    )(*[pltpu.with_memory_space_constraint(tokens, pltpu.HBM)] * SPLIT, pltpu.with_memory_space_constraint(frames, pltpu.HBM))
    with jax.named_scope("rows_one"):
        lse = merge_lse([lse, swap_tok(lse, 1)])
        lse = merge_lse([lse, swap_tok(lse, 2)])
    lse, u, frame_total = call(
        first_cols, steps, [VMEM, whole(1, nf), whole(1, nf)], [lanes(TOK), whole(1, nf), whole(1, 128)],
        [f32(1, nt), f32(1, nf), f32(1, 128)], name="first_cols",
    )(s, lse, fm)
    tokens_later, lse = lax.optimization_barrier((tokens, lse))
    turned = call(
        turn, 4, [rows(nt // 4, d)], pl.BlockSpec((d, nt // 4), lambda i: (0, i)), jax.ShapeDtypeStruct((d, nt), BF16),
        name="turn",
    )(tokens_later)
    with jax.named_scope("cols_one"):
        lse = jnp.concatenate([lse, frame_total], axis=1)
        for stride, size in ORDER:
            parts = ring(lse, stride, size)
            merged = merge_lse([part[:, :nt] for part in parts])
            lse = jnp.concatenate([merged, sum(part[:, nt:] for part in parts)], axis=1)
        lse, frame_total = lse[:, :nt], lse[0, nt]
        turned, lse = lax.optimization_barrier((turned, lse))
    part, e = call(
        second_rows, slabs, [VMEM, whole(1, nt), whole(1, nt), whole(1, nf)], [whole(1, nf + EXTRA), VMEM],
        [f32(1, nf + EXTRA), kept], [pltpu.VMEM((nt, 128), F32)], input_output_aliases={0: 1}, name="second_rows",
    )(s, lse, tm, u)
    with jax.named_scope("rows_two"):
        part = part + swap_tok(part, 1)
        part = part + swap_tok(part, 2)
    part, token_part, share, e = call(
        second_cols, steps, [VMEM, whole(1, nf + EXTRA), whole(1, nf), whole(nf, d)],
        [lanes(TOK), rows(TOK, d), whole(1, nf), hbm],
        [f32(1, nt), jax.ShapeDtypeStruct((nt, d), BF16), f32(1, nf), pltpu.HBM((slabs, nt, W), F32)],
        [pltpu.VMEM((1, nf), F32), pltpu.SemaphoreType.DMA((steps,))], name="second_cols",
    )(e, part, fm, frames)
    with jax.named_scope("cols_two"):
        col_total = part
        for stride, size in ORDER:
            col_total = sum(ring(col_total, stride, size))
    with jax.named_scope("token_scatter"):
        token_part, col_total = lax.optimization_barrier((token_part, col_total))
        plane, own = 16, nt // 16
        planes = [list(range(z, z + plane)) for z in range(0, n_ctx, plane)]
        pieces = lax.all_to_all(token_part.reshape(plane, own, d), "ctx", 0, 0, axis_index_groups=planes)
        deal = own // (2 * SPLIT)
        piece = call(
            sum_pieces, 2,
            [pl.BlockSpec((plane, deal, d), lambda i, k=k: (0, i * SPLIT + k, 0)) for k in range(SPLIT)],
            rows(own // 2, d), jax.ShapeDtypeStruct((own, d), BF16), name="sum_pieces",
        )(*[pieces] * SPLIT)
        other_piece = shift(piece, 16, 1, 2)

    e = pltpu.with_memory_space_constraint(e, pltpu.HBM)
    half = slabs // 2
    base = ((1 - core) * half).reshape(1).astype(jnp.int32)
    with jax.named_scope("frame_rows"):
        sums, parts = pl.pallas_call(
            frame_parts,
            grid=(slabs,),
            in_specs=[SMEM, hbm, whole(1, nt), whole(1, nt), whole(1, nf), whole(d, nt)],
            out_specs=[lanes(W), rows(W, d)],
            out_shape=[f32(1, nf), jax.ShapeDtypeStruct((nf, d), BF16)],
            scratch_shapes=[
                pltpu.VMEM((nt, 128), F32),
                pltpu.VMEM((HELD, nt, W), F32),
                pltpu.SemaphoreType.DMA((HELD,)),
            ],
            compiler_params=pltpu.CompilerParams(vmem_limit_bytes=VMEM_BYTES),
            name="frame_parts",
        )(base, e, col_total, tm, share, turned)
        my_sum = sums[:, nf // 2 :] + swap_tok(sums[:, : nf // 2], 1)
        mine = (parts[nf // 2 :].astype(F32) + swap_tok(parts[: nf // 2], 1).astype(F32)).astype(BF16)
        mine, my_sum = lax.optimization_barrier((mine, my_sum))
        other_sum = swap_tok(my_sum, 2)
        mine, other_piece, other_sum = lax.optimization_barrier((mine, other_piece, other_sum))
        other = swap_tok(mine, 2)
        my_sum = my_sum + other_sum
    with jax.named_scope("token_gather"):
        col_mine = lax.dynamic_slice_in_dim(col_total, ctx % plane * own, own, axis=1)
        pieces = pl.pallas_call(
            finish_pieces, in_specs=[VMEM] * 3, out_specs=hbm, out_shape=pltpu.HBM((plane, own, d), BF16),
            scratch_shapes=[
                pltpu.VMEM((own, 128), F32),
                pltpu.VMEM((own, d), BF16),
                pltpu.SemaphoreType.DMA((plane,)),
            ],
            compiler_params=pltpu.CompilerParams(vmem_limit_bytes=VMEM_BYTES), name="finish_pieces",
        )(piece, other_piece, col_mine)
        pieces = lax.all_to_all(pieces, "ctx", 0, 0, axis_index_groups=planes)
        token_map = pl.pallas_call(
            place_tokens, in_specs=[hbm], out_specs=hbm, out_shape=pltpu.HBM((nt, d), BF16),
            scratch_shapes=[
                pltpu.VMEM((plane, own, d), BF16),
                pltpu.SemaphoreType.DMA((plane,)),
                pltpu.SemaphoreType.DMA((plane,)),
            ],
            compiler_params=pltpu.CompilerParams(vmem_limit_bytes=VMEM_BYTES), name="place_tokens",
        )(pltpu.with_memory_space_constraint(pieces, pltpu.HBM))
    with jax.named_scope("frame_out"):
        mine = pl.pallas_call(
            finish_frames, in_specs=[VMEM] * 3, out_specs=VMEM, out_shape=jax.ShapeDtypeStruct((nf // 2, d), BF16),
            scratch_shapes=[pltpu.VMEM((nf // 2, 128), F32)],
            compiler_params=pltpu.CompilerParams(vmem_limit_bytes=VMEM_BYTES), name="finish_frames",
        )(mine, other, my_sum)
        theirs = swap_tok(mine, 1)
        their_sum = swap_tok(my_sum, 1)
        frame_map = pl.pallas_call(
            place_frames, in_specs=[SMEM, VMEM, VMEM], out_specs=ANY, out_shape=jax.ShapeDtypeStruct((nf, d), BF16),
            scratch_shapes=[pltpu.SemaphoreType.DMA((2,))], name="place_frames",
        )(core.reshape(1).astype(jnp.int32), mine, theirs)
        low = jnp.where(core == 0, my_sum, their_sum)
        high = jnp.where(core == 0, their_sum, my_sum)
        row_sum = jnp.concatenate([low, high], axis=1)[0]
        mass_ratio = row_sum / (frame_mass / frame_total)
    return frame_map, token_map, mass_ratio


def solution(mesh):
    return jax.shard_map(
        shards,
        mesh=mesh,
        in_specs=(P("ctx", None), P("tok", None), P("ctx"), P("tok")),
        out_specs=(P("ctx", None), P("tok", None), P("ctx")),
        check_vma=False,
    )
```

time: 329 us -> 156 us (0.47)
  Pallas kernels: 163 us -> 42.3 us
  blocking collectives: 31.8 us -> 0 us
  local copies, waits for them, and re-layouts: 32.4 us -> 5.11 us
  waiting for transfers between devices: 46.8 us -> 59.1 us
  other arithmetic: 6.61 us -> 1.37 us
    pallas_call x9 -> x11, Pallas kernels: 163 us -> 42.3 us  [the longest x1 9.45 us: shards(): pl.pallas_call(frame_parts, grid=(slabs,), in_specs=[SMEM, hbm, whole(1,...]
    unnamed x48 -> x22, local copies, waits for them, and re-layouts: 26.2 us -> 3.94 us
    ppermute x25 -> x15, waiting for transfers between devices: 35.7 us -> 14.9 us  [shift(): return lax.ppermute(value, 'ctx', pairs)]
    all_to_all x1 -> x2, waiting for transfers between devices: 0.01 us -> 19.5 us  [the longest x1 11.7 us: shards(): lax.all_to_all(token_part.reshape(plane, own, d), 'ctx', 0, 0, axis_index...]
    all_to_all x1 -> x0, blocking collectives: 17.7 us -> none  [shards(): lse = lax.all_to_all(lse, 'ctx', 0, 0)[:, 0]]
    all_gather x2 -> x0, blocking collectives: 14 us -> none  [the longest x1 7.2 us: shards(): lse = lax.all_gather(lse, 'tok', tiled=True)]
    ppermute x6 -> x10, waiting for transfers between devices: 11.1 us -> 24.7 us  [swap_tok(): lax.ppermute(value, 'tok', [(i, i ^ bit) for i in range(lax.axis_size('to...]
    ppermute x25 -> x15, starting transfers between devices: 36.2 us -> 24.7 us  [shift(): return lax.ppermute(value, 'ctx', pairs)]
  transfers between devices with their start and end apart: 32 -> 27, of which waited for: 15 -> 21; matrix products, arithmetic and copies ran while one was open for 4% -> 1% of each run, Pallas kernels for 23% -> 10%
where the time goes in v3:
time: 156 us; the launch traced here: 155 us
  waiting for transfers between devices  59.1 us (38%)
  starting transfers between devices  46.6 us (30%)
  Pallas kernels  42.3 us (27%)
  local copies, waits for them, and re-layouts  5.11 us (3%)
    ppermute x10, waiting for transfers between devices, swap_tok(): lax.ppermute(value, 'tok', [(i, i ^ bit) for i in range(lax.axis_size('to...  24.7 us
    ppermute x15, starting transfers between devices, shift(): return lax.ppermute(value, 'ctx', pairs)  24.7 us
    ppermute x15, waiting for transfers between devices, shift(): return lax.ppermute(value, 'ctx', pairs)  14.9 us
    ppermute x10, starting transfers between devices, swap_tok(): lax.ppermute(value, 'tok', [(i, i ^ bit) for i in range(lax.axis_size('to...  13.6 us
    all_to_all x1, waiting for transfers between devices, shards(): lax.all_to_all(token_part.reshape(plane, own, d), 'ctx', 0, 0, axis_index...  11.7 us
    pallas_call x1, Pallas kernels, shards(): pl.pallas_call(frame_parts, grid=(slabs,), in_specs=[SMEM, hbm, whole(1,...  9.45 us
    pallas_call x1, Pallas kernels, shards(): call(functools.partial(first_rows, scale), slabs, [pl.BlockSpec((nt // SP...  8.55 us
    all_to_all x1, waiting for transfers between devices, shards(): pieces = lax.all_to_all(pieces, 'ctx', 0, 0, axis_index_groups=planes)  7.78 us
  transfers between devices with their start and end apart: 27, of which 21 were waited for; matrix products, arithmetic and copies ran while one was open for 1% of the time, Pallas kernels for 10%

profile of v3, /device:TPU:0, one launch (start us, length us, event | category | flops | bytes accessed | tf_op | source)
XLA Modules:
  0.0 155.4 jit_solution(12230223937986844609)
XLA Ops:
  0.6 8.6 %first_rows.1 = (f32[1,2048]{1,0:T(1,128)S(1)}, f32[8,2048,256]{2,1,0:T(8,128)S(1)}) custom-call(bf16[2048,512]{1,0:T(8,128)(2,1)} %in_ref, bf16[2048,512]{1,0:T(8,128)(2,1)} %in_ref, bf16[2048,512]{1,0:T(8,128)(2,1)} %in_ref, bf16[2048,512]{1,0:T(8,128)(2,1)} %in_ref, bf16[2048,512]{1,0:T(8,128)(2,1)} %f_ref.1), custom_call_target="tpu_custom_call" | custom-call | tf_op jit(solution)/shard_map/first_rows/pallas_call | solution.py:298
  9.3 1.2 collective-permute-done
  10.5 4.0 %collective-permute-start.1 = (f32[1,2048]{1,0:T(1,128)S(1)}, f32[1,2048]{1,0:T(1,128)S(1)}, u32[]{:S(2)}, u32[]{:S(2)}) collective-permute-start(f32[1,2048]{1,0:T(1,128)S(1)} %multiply_add_fusion.4), channel_id=1, source_target_pairs={{0,2},{1,3},{2,0},{3,1},{4,6},{5,7},{6,4},{7,5},{8,10},{9,11},{10,... | collective-permute-start | bytes 24584 | tf_op jit(solution)/shard_map/rows_one/ppermute | solution.py:26
  14.5 1.6 %collective-permute-done.1 = f32[1,2048]{1,0:T(1,128)S(1)} collective-permute-done((f32[1,2048]{1,0:T(1,128)S(1)}, f32[1,2048]{1,0:T(1,128)S(1)}, u32[]{:S(2)}, u32[]{:S(2)}) %collective-permute-start.1) | collective-permute-done | bytes 8224 | tf_op jit(solution)/shard_map/rows_one/ppermute | solution.py:26
  16.2 4.8 %first_cols.1 = (f32[1,2048]{1,0:T(1,128)S(1)}, f32[1,2048]{1,0:T(1,128)S(1)}, f32[1,128]{1,0:T(1,128)S(1)}) custom-call(f32[8,2048,256]{2,1,0:T(8,128)S(1)} %get-tuple-element.27.s_ref, f32[1,2048]{1,0:T(1,128)S(1)} %multiply_add_fusion.3.all_ref, f32[1,2048]{1,0:T(1,128)S(1)} %bitcast.9), custom_call_target="tpu_custom_call" | custom-call | tf_op jit(solution)/shard_map/first_cols/pallas_call | solution.py:306
  21.1 1.7 %collective-permute-start.2 = (f32[1,2176]{1,0:T(1,128)S(1)}, f32[1,2176]{1,0:T(1,128)S(1)}, u32[]{:S(2)}, u32[]{:S(2)}) collective-permute-start(f32[1,2176]{1,0:T(1,128)S(1)} %pad_maximum_fusion), channel_id=1, source_target_pairs={{0,64},{4,68},{8,72},{12,76},{16,80},{20,84},{24,88},{28,92},{32,9... | collective-permute-start | bytes 26120 | tf_op jit(solution)/shard_map/cols_one/ppermute | solution.py:34
  22.7 2.1 %collective-permute-done.2 = f32[1,2176]{1,0:T(1,128)S(1)} collective-permute-done((f32[1,2176]{1,0:T(1,128)S(1)}, f32[1,2176]{1,0:T(1,128)S(1)}, u32[]{:S(2)}, u32[]{:S(2)}) %collective-permute-start.2) | collective-permute-done | bytes 8736 | tf_op jit(solution)/shard_map/cols_one/ppermute | solution.py:34
  24.9 1.6 %collective-permute-start.3 = (f32[1,2176]{1,0:T(1,128)S(1)}, f32[1,2176]{1,0:T(1,128)S(1)}, u32[]{:S(2)}, u32[]{:S(2)}) collective-permute-start(f32[1,2176]{1,0:T(1,128)S(1)} %pad_maximum_fusion.1), channel_id=1, source_target_pairs={{0,4},{4,8},{8,12},{12,0},{16,20},{20,24},{24,28},{28,16},{32,36},... | collective-permute-start | bytes 26120 | tf_op jit(solution)/shard_map/cols_one/ppermute | solution.py:34
  26.4 2.7 %collective-permute-start.4 = (f32[1,2176]{1,0:T(1,128)S(1)}, f32[1,2176]{1,0:T(1,128)S(1)}, u32[]{:S(2)}, u32[]{:S(2)}) collective-permute-start(f32[1,2176]{1,0:T(1,128)S(1)} %pad_maximum_fusion.1), channel_id=1, source_target_pairs={{0,8},{4,12},{8,0},{12,4},{16,24},{20,28},{24,16},{28,20},{32,40},... | collective-permute-start | bytes 26120 | tf_op jit(solution)/shard_map/cols_one/ppermute | solution.py:34
  29.2 1.4 collective-permute-start.5
  30.6 1.0 collective-permute-done.4
  31.6 1.2 collective-permute-done.5
  32.9 1.6 %collective-permute-start.6 = (f32[1,2176]{1,0:T(1,128)S(1)}, f32[1,2176]{1,0:T(1,128)S(1)}, u32[]{:S(2)}, u32[]{:S(2)}) collective-permute-start(f32[1,2176]{1,0:T(1,128)S(1)} %pad_maximum_fusion.2), channel_id=1, source_target_pairs={{0,16},{4,20},{8,24},{12,28},{16,32},{20,36},{24,40},{28,44},{32,4... | collective-permute-start | bytes 26120 | tf_op jit(solution)/shard_map/cols_one/ppermute | solution.py:34
  34.6 2.9 %collective-permute-start.7 = (f32[1,2176]{1,0:T(1,128)S(1)}, f32[1,2176]{1,0:T(1,128)S(1)}, u32[]{:S(2)}, u32[]{:S(2)}) collective-permute-start(f32[1,2176]{1,0:T(1,128)S(1)} %pad_maximum_fusion.2), channel_id=1, source_target_pairs={{0,32},{4,36},{8,40},{12,44},{16,48},{20,52},{24,56},{28,60},{32,0... | collective-permute-start | bytes 26120 | tf_op jit(solution)/shard_map/cols_one/ppermute | solution.py:34
  37.5 1.3 collective-permute-start.8
  38.8 0.9 turn.1.tt_ref
  39.8 1.3 collective-permute-done.8
  41.2 4.0 %second_rows.1 = (f32[1,2304]{1,0:T(1,128)S(1)}, f32[8,2048,256]{2,1,0:T(8,128)S(1)}) custom-call(f32[8,2048,256]{2,1,0:T(8,128)S(1)} %get-tuple-element.27.s_ref, f32[1,2048]{1,0:T(1,128)S(1)} %multiply_add_fusion.all_ref, f32[1,2048]{1,0:T(1,128)S(1)} %bitcast.11, f32[1,2048]{1,0:T(1,128)S(1)} %get-tuple-element.34.u_ref), custom_call_target="tpu_custom_call", output_to_operand_aliasing={{1}: (0, {})} | custom-call | tf_op jit(solution)/shard_map/second_rows/pallas_call | solution.py:323
  45.3 1.2 collective-permute-done.9
  46.5 3.6 %collective-permute-start.10 = (f32[1,2304]{1,0:T(1,128)S(1)}, f32[1,2304]{1,0:T(1,128)S(1)}, u32[]{:S(2)}, u32[]{:S(2)}) collective-permute-start(f32[1,2304]{1,0:T(1,128)S(1)} %add.128), channel_id=1, source_target_pairs={{0,2},{1,3},{2,0},{3,1},{4,6},{5,7},{6,4},{7,5},{8,10},{9,11},{10,... | collective-permute-start | bytes 27656 | tf_op jit(solution)/shard_map/rows_two/ppermute | solution.py:26
  50.1 1.6 %collective-permute-done.10 = f32[1,2304]{1,0:T(1,128)S(1)} collective-permute-done((f32[1,2304]{1,0:T(1,128)S(1)}, f32[1,2304]{1,0:T(1,128)S(1)}, u32[]{:S(2)}, u32[]{:S(2)}) %collective-permute-start.10) | collective-permute-done | bytes 9248 | tf_op jit(solution)/shard_map/rows_two/ppermute | solution.py:26
  51.8 6.8 %second_cols.1 = (f32[1,2048]{1,0:T(1,128)S(1)}, bf16[2048,512]{1,0:T(8,128)(2,1)S(1)}, f32[1,2048]{1,0:T(1,128)S(1)}, f32[8,2048,256]{2,1,0:T(8,128)}) custom-call(f32[8,2048,256]{2,1,0:T(8,128)S(1)} %get-tuple-element.35.e_ref, f32[1,2304]{1,0:T(1,128)S(1)} %add.129.total_ref, f32[1,2048]{1,0:T(1,128)S(1)} %bitcast.10, bf16[2048,512]{1,0:T(8,128)(2,1)S(1)} %copy-done.3), custom_call_target="tpu_custom_call" | custom-call | tf_op jit(solution)/shard_map/second_cols/pallas_call | solution.py:330
  58.6 1.3 copy-done.7
  59.9 1.6 %collective-permute-start.11 = (f32[1,2048]{1,0:T(1,128)S(1)}, f32[1,2048]{1,0:T(1,128)S(1)}, u32[]{:S(2)}, u32[]{:S(2)}) collective-permute-start(f32[1,2048]{1,0:T(1,128)S(1)} %get-tuple-element.39), channel_id=1, source_target_pairs={{0,64},{4,68},{8,72},{12,76},{16,80},{20,84},{24,88},{28,92},{32,9... | collective-permute-start | bytes 24584 | tf_op jit(solution)/shard_map/cols_two/ppermute | solution.py:34
  61.4 2.1 %collective-permute-done.11 = f32[1,2048]{1,0:T(1,128)S(1)} collective-permute-done((f32[1,2048]{1,0:T(1,128)S(1)}, f32[1,2048]{1,0:T(1,128)S(1)}, u32[]{:S(2)}, u32[]{:S(2)}) %collective-permute-start.11) | collective-permute-done | bytes 8224 | tf_op jit(solution)/shard_map/cols_two/ppermute | solution.py:34
  63.9 3.8 %collective-permute-start.13 = (f32[1,2048]{1,0:T(1,128)S(1)}, f32[1,2048]{1,0:T(1,128)S(1)}, u32[]{:S(2)}, u32[]{:S(2)}) collective-permute-start(f32[1,2048]{1,0:T(1,128)S(1)} %add.130), channel_id=1, source_target_pairs={{0,8},{4,12},{8,0},{12,4},{16,24},{20,28},{24,16},{28,20},{32,40},... | collective-permute-start | bytes 24584 | tf_op jit(solution)/shard_map/cols_two/ppermute | solution.py:34
  68.5 1.0 collective-permute-done.13
  69.4 1.9 %collective-permute-done.14 = f32[1,2048]{1,0:T(1,128)S(1)} collective-permute-done((f32[1,2048]{1,0:T(1,128)S(1)}, f32[1,2048]{1,0:T(1,128)S(1)}, u32[]{:S(2)}, u32[]{:S(2)}) %collective-permute-start.14) | collective-permute-done | bytes 8224 | tf_op jit(solution)/shard_map/cols_two/ppermute | solution.py:34
  71.6 3.8 %collective-permute-start.16 = (f32[1,2048]{1,0:T(1,128)S(1)}, f32[1,2048]{1,0:T(1,128)S(1)}, u32[]{:S(2)}, u32[]{:S(2)}) collective-permute-start(f32[1,2048]{1,0:T(1,128)S(1)} %add_add_fusion.1), channel_id=1, source_target_pairs={{0,32},{4,36},{8,40},{12,44},{16,48},{20,52},{24,56},{28,60},{32,0... | collective-permute-start | bytes 24584 | tf_op jit(solution)/shard_map/cols_two/ppermute | solution.py:34
  77.2 1.9 %collective-permute-done.17 = f32[1,2048]{1,0:T(1,128)S(1)} collective-permute-done((f32[1,2048]{1,0:T(1,128)S(1)}, f32[1,2048]{1,0:T(1,128)S(1)}, u32[]{:S(2)}, u32[]{:S(2)}) %collective-permute-start.17) | collective-permute-done | bytes 8224 | tf_op jit(solution)/shard_map/cols_two/ppermute | solution.py:34
  79.1 3.8 %all-to-all-start = ((bf16[16,128,512]{2,1,0:T(8,128)(2,1)}), bf16[16,128,512]{2,1,0:T(8,128)(2,1)S(1)}, u32[]{:S(2)}, u32[]{:S(2)}) async-start(bf16[16,128,512]{2,1,0:T(8,128)(2,1)} %bitcast.8), calls=%async_computation | async-start | bytes 4194304 | tf_op jit(solution)/shard_map/token_scatter/all_to_all | solution.py:344
  83.0 1.6 %copy-done.2 = bf16[512,2048]{1,0:T(8,128)(2,1)S(1)} copy-done((bf16[512,2048]{1,0:T(8,128)(2,1)S(1)}, bf16[512,2048]{1,0:T(8,128)(2,1)}, u32[]{:S(2)}) %copy-start.2) | copy-done | bytes 2097176
  84.6 9.5 %frame_parts.1 = (f32[1,2048]{1,0:T(1,128)S(1)}, bf16[2048,512]{1,0:T(8,128)(2,1)S(1)}) custom-call(s32[1]{0:T(128)} %bitcast.1.base_ref, f32[8,2048,256]{2,1,0:T(8,128)} %get-tuple-element.37.e_ref, f32[1,2048]{1,0:T(1,128)S(1)} %add_add_fusion.total_ref, f32[1,2048]{1,0:T(1,128)S(1)} %bitcast.12, f32[1,2048]{1,0:T(1,128)S(1)} %get-tuple-element.41.share_ref, ...), custom_call_target="tpu_custom_call" | custom-call | tf_op jit(solution)/shard_map/frame_rows/frame_parts/pallas_call | solution.py:357
  94.1 1.2 slice.69
  95.8 1.8 %collective-permute-done.19 = f32[1,1024]{1,0:T(1,128)S(1)} collective-permute-done((f32[1,1024]{1,0:T(1,128)S(1)}, f32[1,1024]{1,0:T(1,128)S(1)}, u32[]{:S(2)}, u32[]{:S(2)}) %collective-permute-start.19) | collective-permute-done | bytes 4128 | tf_op jit(solution)/shard_map/frame_rows/ppermute | solution.py:26
  97.6 11.7 %all-to-all-done.refs_0_.refs_1_.refs_2_.refs_3_ = bf16[16,128,512]{2,1,0:T(8,128)(2,1)S(1)} async-done(((bf16[16,128,512]{2,1,0:T(8,128)(2,1)}), bf16[16,128,512]{2,1,0:T(8,128)(2,1)S(1)}, u32[]{:S(2)}, u32[]{:S(2)}) %all-to-all-start) | async-done | bytes 2097184 | tf_op jit(solution)/shard_map/token_scatter/all_to_all | solution.py:344
  109.8 1.4 collective-permute-start.20
  111.5 3.6 %collective-permute-start.21 = (f32[1,1024]{1,0:T(1,128)S(1)}, f32[1,1024]{1,0:T(1,128)S(1)}, u32[]{:S(2)}, u32[]{:S(2)}) collective-permute-start(f32[1,1024]{1,0:T(1,128)S(1)} %slice_add_fusion), channel_id=1, source_target_pairs={{0,2},{1,3},{2,0},{3,1},{4,6},{5,7},{6,4},{7,5},{8,10},{9,11},{10,... | collective-permute-start | bytes 12296 | tf_op jit(solution)/shard_map/frame_rows/ppermute | solution.py:26
  115.1 4.1 %collective-permute-done.21 = f32[1,1024]{1,0:T(1,128)S(1)} collective-permute-done((f32[1,1024]{1,0:T(1,128)S(1)}, f32[1,1024]{1,0:T(1,128)S(1)}, u32[]{:S(2)}, u32[]{:S(2)}) %collective-permute-start.21) | collective-permute-done | bytes 4128 | tf_op jit(solution)/shard_map/frame_rows/ppermute | solution.py:26
  119.2 1.1 collective-permute-start.22
  120.3 1.5 finish_pieces.1
  121.9 4.4 %all-to-all-start.1 = ((bf16[16,128,512]{2,1,0:T(8,128)(2,1)}), bf16[16,128,512]{2,1,0:T(8,128)(2,1)}, u32[]{:S(2)}, u32[]{:S(2)}) async-start(bf16[16,128,512]{2,1,0:T(8,128)(2,1)} %finish_pieces.1), calls=%async_computation.1 | async-start | bytes 4194304 | tf_op jit(solution)/shard_map/token_gather/all_to_all | solution.py:389
  126.3 11.1 %collective-permute-done.22.other_ref = bf16[1024,512]{1,0:T(8,128)(2,1)S(1)} collective-permute-done((bf16[1024,512]{1,0:T(8,128)(2,1)S(1)}, bf16[1024,512]{1,0:T(8,128)(2,1)S(1)}, u32[]{:S(2)}, u32[]{:S(2)}) %collective-permute-start.22) | collective-permute-done | bytes 1048608 | tf_op jit(solution)/shard_map/frame_rows/ppermute | solution.py:26
  138.3 2.1 %collective-permute-done.24 = f32[1,1024]{1,0:T(1,128)S(1)} collective-permute-done((f32[1,1024]{1,0:T(1,128)S(1)}, f32[1,1024]{1,0:T(1,128)S(1)}, u32[]{:S(2)}, u32[]{:S(2)}) %collective-permute-start.24) | collective-permute-done | bytes 4128 | tf_op jit(solution)/shard_map/frame_out/ppermute | solution.py:26
  141.2 7.8 %all-to-all-done.1.pieces_ref = bf16[16,128,512]{2,1,0:T(8,128)(2,1)} async-done(((bf16[16,128,512]{2,1,0:T(8,128)(2,1)}), bf16[16,128,512]{2,1,0:T(8,128)(2,1)}, u32[]{:S(2)}, u32[]{:S(2)}) %all-to-all-start.1) | async-done | bytes 2097184 | tf_op jit(solution)/shard_map/token_gather/all_to_all | solution.py:389
  148.9 2.6 %place_tokens.1 = bf16[2048,512]{1,0:T(8,128)(2,1)} custom-call(bf16[16,128,512]{2,1,0:T(8,128)(2,1)} %all-to-all-done.1.pieces_ref), custom_call_target="tpu_custom_call" | custom-call | tf_op jit(solution)/shard_map/token_gather/place_tokens/pallas_call | solution.py:390
  151.6 1.0 copy-done.10
  152.5 2.9 %place_frames.1 = bf16[2048,512]{1,0:T(8,128)(2,1)} custom-call(s32[1]{0:T(128)} %bitcast.core_ref, bf16[1024,512]{1,0:T(8,128)(2,1)} %copy-done.4, bf16[1024,512]{1,0:T(8,128)(2,1)} %copy-done.10), custom_call_target="tpu_custom_call" | custom-call | tf_op jit(solution)/shard_map/frame_out/place_frames/pallas_call | solution.py:407
  (64 shorter events, 6.6 us)
Async XLA Ops:
  0.6 15.6 %copy-start.8 = (f32[2048]{0:T(1024)S(1)}, f32[2048]{0:T(1024)}, u32[]{:S(2)}) copy-start(f32[2048]{0:T(1024)} %param.6) | copy-start | bytes 24580
  9.2 1.3 collective-permute-start
  10.5 5.7 %collective-permute-start.1 = (f32[1,2048]{1,0:T(1,128)S(1)}, f32[1,2048]{1,0:T(1,128)S(1)}, u32[]{:S(2)}, u32[]{:S(2)}) collective-permute-start(f32[1,2048]{1,0:T(1,128)S(1)} %multiply_add_fusion.4), channel_id=1, source_target_pairs={{0,2},{1,3},{2,0},{3,1},{4,6},{5,7},{6,4},{7,5},{8,10},{9,11},{10,... | collective-permute-start | bytes 24584 | tf_op jit(solution)/shard_map/rows_one/ppermute | solution.py:26
  16.2 22.6 %copy-start = (bf16[2048,512]{1,0:T(8,128)(2,1)S(1)}, bf16[2048,512]{1,0:T(8,128)(2,1)}, u32[]{:S(2)}) copy-start(bf16[2048,512]{1,0:T(8,128)(2,1)} %in_ref) | copy-start | bytes 6291460
  21.1 3.7 %collective-permute-start.2 = (f32[1,2176]{1,0:T(1,128)S(1)}, f32[1,2176]{1,0:T(1,128)S(1)}, u32[]{:S(2)}, u32[]{:S(2)}) collective-permute-start(f32[1,2176]{1,0:T(1,128)S(1)} %pad_maximum_fusion), channel_id=1, source_target_pairs={{0,64},{4,68},{8,72},{12,76},{16,80},{20,84},{24,88},{28,92},{32,9... | collective-permute-start | bytes 26120 | tf_op jit(solution)/shard_map/cols_one/ppermute | solution.py:34
  24.9 5.7 %collective-permute-start.3 = (f32[1,2176]{1,0:T(1,128)S(1)}, f32[1,2176]{1,0:T(1,128)S(1)}, u32[]{:S(2)}, u32[]{:S(2)}) collective-permute-start(f32[1,2176]{1,0:T(1,128)S(1)} %pad_maximum_fusion.1), channel_id=1, source_target_pairs={{0,4},{4,8},{8,12},{12,0},{16,20},{20,24},{24,28},{28,16},{32,36},... | collective-permute-start | bytes 26120 | tf_op jit(solution)/shard_map/cols_one/ppermute | solution.py:34
  26.4 5.2 %collective-permute-start.4 = (f32[1,2176]{1,0:T(1,128)S(1)}, f32[1,2176]{1,0:T(1,128)S(1)}, u32[]{:S(2)}, u32[]{:S(2)}) collective-permute-start(f32[1,2176]{1,0:T(1,128)S(1)} %pad_maximum_fusion.1), channel_id=1, source_target_pairs={{0,8},{4,12},{8,0},{12,4},{16,24},{20,28},{24,16},{28,20},{32,40},... | collective-permute-start | bytes 26120 | tf_op jit(solution)/shard_map/cols_one/ppermute | solution.py:34
  29.2 3.7 %collective-permute-start.5 = (f32[1,2176]{1,0:T(1,128)S(1)}, f32[1,2176]{1,0:T(1,128)S(1)}, u32[]{:S(2)}, u32[]{:S(2)}) collective-permute-start(f32[1,2176]{1,0:T(1,128)S(1)} %pad_maximum_fusion.1), channel_id=1, source_target_pairs={{0,12},{4,0},{8,4},{12,8},{16,28},{20,16},{24,20},{28,24},{32,44},... | collective-permute-start | bytes 26120 | tf_op jit(solution)/shard_map/cols_one/ppermute | solution.py:34
  32.9 8.3 %copy-start.9 = (f32[2048]{0:T(1024)S(1)}, f32[2048]{0:T(1024)}, u32[]{:S(2)}) copy-start(f32[2048]{0:T(1024)} %param.7) | copy-start | bytes 24580
  32.9 6.8 %collective-permute-start.6 = (f32[1,2176]{1,0:T(1,128)S(1)}, f32[1,2176]{1,0:T(1,128)S(1)}, u32[]{:S(2)}, u32[]{:S(2)}) collective-permute-start(f32[1,2176]{1,0:T(1,128)S(1)} %pad_maximum_fusion.2), channel_id=1, source_target_pairs={{0,16},{4,20},{8,24},{12,28},{16,32},{20,36},{24,40},{28,44},{32,4... | collective-permute-start | bytes 26120 | tf_op jit(solution)/shard_map/cols_one/ppermute | solution.py:34
  34.6 5.2 %collective-permute-start.7 = (f32[1,2176]{1,0:T(1,128)S(1)}, f32[1,2176]{1,0:T(1,128)S(1)}, u32[]{:S(2)}, u32[]{:S(2)}) collective-permute-start(f32[1,2176]{1,0:T(1,128)S(1)} %pad_maximum_fusion.2), channel_id=1, source_target_pairs={{0,32},{4,36},{8,40},{12,44},{16,48},{20,52},{24,56},{28,60},{32,0... | collective-permute-start | bytes 26120 | tf_op jit(solution)/shard_map/cols_one/ppermute | solution.py:34
  37.5 3.7 %collective-permute-start.8 = (f32[1,2176]{1,0:T(1,128)S(1)}, f32[1,2176]{1,0:T(1,128)S(1)}, u32[]{:S(2)}, u32[]{:S(2)}) collective-permute-start(f32[1,2176]{1,0:T(1,128)S(1)} %pad_maximum_fusion.2), channel_id=1, source_target_pairs={{0,48},{4,52},{8,56},{12,60},{16,0},{20,4},{24,8},{28,12},{32,16},... | collective-permute-start | bytes 26120 | tf_op jit(solution)/shard_map/cols_one/ppermute | solution.py:34
  39.8 5.5 %copy-start.1 = (bf16[512,2048]{1,0:T(8,128)(2,1)}, bf16[512,2048]{1,0:T(8,128)(2,1)S(1)}, u32[]{:S(2)}) copy-start(bf16[512,2048]{1,0:T(8,128)(2,1)S(1)} %turn.1.tt_ref) | copy-start | bytes 6291460
  41.2 10.5 %copy-start.3 = (bf16[2048,512]{1,0:T(8,128)(2,1)S(1)}, bf16[2048,512]{1,0:T(8,128)(2,1)}, u32[]{:S(2)}) copy-start(bf16[2048,512]{1,0:T(8,128)(2,1)} %f_ref.1) | copy-start | bytes 6291460
  45.2 1.3 collective-permute-start.9
  46.5 5.2 %collective-permute-start.10 = (f32[1,2304]{1,0:T(1,128)S(1)}, f32[1,2304]{1,0:T(1,128)S(1)}, u32[]{:S(2)}, u32[]{:S(2)}) collective-permute-start(f32[1,2304]{1,0:T(1,128)S(1)} %add.128), channel_id=1, source_target_pairs={{0,2},{1,3},{2,0},{3,1},{4,6},{5,7},{6,4},{7,5},{8,10},{9,11},{10,... | collective-permute-start | bytes 27656 | tf_op jit(solution)/shard_map/rows_two/ppermute | solution.py:26
  58.6 1.3 copy-start.7
  59.9 3.7 %collective-permute-start.11 = (f32[1,2048]{1,0:T(1,128)S(1)}, f32[1,2048]{1,0:T(1,128)S(1)}, u32[]{:S(2)}, u32[]{:S(2)}) collective-permute-start(f32[1,2048]{1,0:T(1,128)S(1)} %get-tuple-element.39), channel_id=1, source_target_pairs={{0,64},{4,68},{8,72},{12,76},{16,80},{20,84},{24,88},{28,92},{32,9... | collective-permute-start | bytes 24584 | tf_op jit(solution)/shard_map/cols_two/ppermute | solution.py:34
  63.5 4.9 %collective-permute-start.12 = (f32[1,2048]{1,0:T(1,128)S(1)}, f32[1,2048]{1,0:T(1,128)S(1)}, u32[]{:S(2)}, u32[]{:S(2)}) collective-permute-start(f32[1,2048]{1,0:T(1,128)S(1)} %add.130), channel_id=1, source_target_pairs={{0,4},{4,8},{8,12},{12,0},{16,20},{20,24},{24,28},{28,16},{32,36},... | collective-permute-start | bytes 24584 | tf_op jit(solution)/shard_map/cols_two/ppermute | solution.py:34
  63.9 5.5 %collective-permute-start.13 = (f32[1,2048]{1,0:T(1,128)S(1)}, f32[1,2048]{1,0:T(1,128)S(1)}, u32[]{:S(2)}, u32[]{:S(2)}) collective-permute-start(f32[1,2048]{1,0:T(1,128)S(1)} %add.130), channel_id=1, source_target_pairs={{0,8},{4,12},{8,0},{12,4},{16,24},{20,28},{24,16},{28,20},{32,40},... | collective-permute-start | bytes 24584 | tf_op jit(solution)/shard_map/cols_two/ppermute | solution.py:34
  67.7 3.7 %collective-permute-start.14 = (f32[1,2048]{1,0:T(1,128)S(1)}, f32[1,2048]{1,0:T(1,128)S(1)}, u32[]{:S(2)}, u32[]{:S(2)}) collective-permute-start(f32[1,2048]{1,0:T(1,128)S(1)} %add.130), channel_id=1, source_target_pairs={{0,12},{4,0},{8,4},{12,8},{16,28},{20,16},{24,20},{28,24},{32,44},... | collective-permute-start | bytes 24584 | tf_op jit(solution)/shard_map/cols_two/ppermute | solution.py:34
  71.4 4.9 %collective-permute-start.15 = (f32[1,2048]{1,0:T(1,128)S(1)}, f32[1,2048]{1,0:T(1,128)S(1)}, u32[]{:S(2)}, u32[]{:S(2)}) collective-permute-start(f32[1,2048]{1,0:T(1,128)S(1)} %add_add_fusion.1), channel_id=1, source_target_pairs={{0,16},{4,20},{8,24},{12,28},{16,32},{20,36},{24,40},{28,44},{32,4... | collective-permute-start | bytes 24584 | tf_op jit(solution)/shard_map/cols_two/ppermute | solution.py:34
  71.6 5.5 %collective-permute-start.16 = (f32[1,2048]{1,0:T(1,128)S(1)}, f32[1,2048]{1,0:T(1,128)S(1)}, u32[]{:S(2)}, u32[]{:S(2)}) collective-permute-start(f32[1,2048]{1,0:T(1,128)S(1)} %add_add_fusion.1), channel_id=1, source_target_pairs={{0,32},{4,36},{8,40},{12,44},{16,48},{20,52},{24,56},{28,60},{32,0... | collective-permute-start | bytes 24584 | tf_op jit(solution)/shard_map/cols_two/ppermute | solution.py:34
  75.5 3.7 %collective-permute-start.17 = (f32[1,2048]{1,0:T(1,128)S(1)}, f32[1,2048]{1,0:T(1,128)S(1)}, u32[]{:S(2)}, u32[]{:S(2)}) collective-permute-start(f32[1,2048]{1,0:T(1,128)S(1)} %add_add_fusion.1), channel_id=1, source_target_pairs={{0,48},{4,52},{8,56},{12,60},{16,0},{20,4},{24,8},{28,12},{32,16},... | collective-permute-start | bytes 24584 | tf_op jit(solution)/shard_map/cols_two/ppermute | solution.py:34
  79.1 30.1 %all-to-all-start = ((bf16[16,128,512]{2,1,0:T(8,128)(2,1)}), bf16[16,128,512]{2,1,0:T(8,128)(2,1)S(1)}, u32[]{:S(2)}, u32[]{:S(2)}) async-start(bf16[16,128,512]{2,1,0:T(8,128)(2,1)} %bitcast.8), calls=%async_computation | async-start | bytes 4194304 | tf_op jit(solution)/shard_map/token_scatter/all_to_all | solution.py:344
  83.0 1.6 %copy-start.2 = (bf16[512,2048]{1,0:T(8,128)(2,1)S(1)}, bf16[512,2048]{1,0:T(8,128)(2,1)}, u32[]{:S(2)}) copy-start(bf16[512,2048]{1,0:T(8,128)(2,1)} %copy-done.1) | copy-start | bytes 6291460
  94.1 3.5 %copy-start.5 = (bf16[2048,512]{1,0:T(8,128)(2,1)}, bf16[2048,512]{1,0:T(8,128)(2,1)S(1)}, u32[]{:S(2)}) copy-start(bf16[2048,512]{1,0:T(8,128)(2,1)S(1)} %get-tuple-element.43) | copy-start | bytes 6291460
  95.3 15.9 %collective-permute-start.18 = (bf16[1024,512]{1,0:T(8,128)(2,1)}, bf16[1024,512]{1,0:T(8,128)(2,1)S(1)}, u32[]{:S(2)}, u32[]{:S(2)}) collective-permute-start(bf16[1024,512]{1,0:T(8,128)(2,1)} %slice.69), channel_id=1, source_target_pairs={{0,1},{1,0},{2,3},{3,2},{4,5},{5,4},{6,7},{7,6},{8,9},{9,8},{10,11... | collective-permute-start | bytes 3145736 | tf_op jit(solution)/shard_map/frame_rows/ppermute | solution.py:26
  95.3 2.3 %collective-permute-start.19 = (f32[1,1024]{1,0:T(1,128)S(1)}, f32[1,1024]{1,0:T(1,128)S(1)}, u32[]{:S(2)}, u32[]{:S(2)}) collective-permute-start(f32[1,1024]{1,0:T(1,128)S(1)} %slice.71), channel_id=1, source_target_pairs={{0,1},{1,0},{2,3},{3,2},{4,5},{5,4},{6,7},{7,6},{8,9},{9,8},{10,11... | collective-permute-start | bytes 12296 | tf_op jit(solution)/shard_map/frame_rows/ppermute | solution.py:26
  109.3 1.9 %copy-start.6 = (bf16[2048,512]{1,0:T(8,128)(2,1)S(1)}, bf16[2048,512]{1,0:T(8,128)(2,1)}, u32[]{:S(2)}) copy-start(bf16[2048,512]{1,0:T(8,128)(2,1)} %copy-done.5) | copy-start | bytes 6291460
  109.8 9.4 %collective-permute-start.20 = (bf16[128,512]{1,0:T(8,128)(2,1)S(1)}, bf16[128,512]{1,0:T(8,128)(2,1)S(1)}, u32[]{:S(2)}, u32[]{:S(2)}) collective-permute-start(bf16[128,512]{1,0:T(8,128)(2,1)S(1)} %sum_pieces.1.mine_ref), channel_id=1, source_target_pairs={{0,64},{4,68},{8,72},{12,76},{16,80},{20,84},{24,88},{28,92},{32,9... | collective-permute-start | bytes 393224 | tf_op jit(solution)/shard_map/token_scatter/ppermute | solution.py:34
  111.5 7.8 %collective-permute-start.21 = (f32[1,1024]{1,0:T(1,128)S(1)}, f32[1,1024]{1,0:T(1,128)S(1)}, u32[]{:S(2)}, u32[]{:S(2)}) collective-permute-start(f32[1,1024]{1,0:T(1,128)S(1)} %slice_add_fusion), channel_id=1, source_target_pairs={{0,2},{1,3},{2,0},{3,1},{4,6},{5,7},{6,4},{7,5},{8,10},{9,11},{10,... | collective-permute-start | bytes 12296 | tf_op jit(solution)/shard_map/frame_rows/ppermute | solution.py:26
  119.2 18.2 %collective-permute-start.22 = (bf16[1024,512]{1,0:T(8,128)(2,1)S(1)}, bf16[1024,512]{1,0:T(8,128)(2,1)S(1)}, u32[]{:S(2)}, u32[]{:S(2)}) collective-permute-start(bf16[1024,512]{1,0:T(8,128)(2,1)S(1)} %add_convert_fusion.mine_ref), channel_id=1, source_target_pairs={{0,2},{1,3},{2,0},{3,1},{4,6},{5,7},{6,4},{7,5},{8,10},{9,11},{10,... | collective-permute-start | bytes 3145736 | tf_op jit(solution)/shard_map/frame_rows/ppermute | solution.py:26
  121.9 27.1 %all-to-all-start.1 = ((bf16[16,128,512]{2,1,0:T(8,128)(2,1)}), bf16[16,128,512]{2,1,0:T(8,128)(2,1)}, u32[]{:S(2)}, u32[]{:S(2)}) async-start(bf16[16,128,512]{2,1,0:T(8,128)(2,1)} %finish_pieces.1), calls=%async_computation.1 | async-start | bytes 4194304 | tf_op jit(solution)/shard_map/token_gather/all_to_all | solution.py:389
  137.7 13.8 %copy-start.4 = (bf16[1024,512]{1,0:T(8,128)(2,1)}, bf16[1024,512]{1,0:T(8,128)(2,1)S(1)}, u32[]{:S(2)}) copy-start(bf16[1024,512]{1,0:T(8,128)(2,1)S(1)} %finish_frames.1.mine_ref) | copy-start | bytes 3145732
  137.7 13.8 %collective-permute-start.23 = (bf16[1024,512]{1,0:T(8,128)(2,1)S(1)}, bf16[1024,512]{1,0:T(8,128)(2,1)S(1)}, u32[]{:S(2)}, u32[]{:S(2)}) collective-permute-start(bf16[1024,512]{1,0:T(8,128)(2,1)S(1)} %finish_frames.1.mine_ref), channel_id=1, source_target_pairs={{0,1},{1,0},{2,3},{3,2},{4,5},{5,4},{6,7},{7,6},{8,9},{9,8},{10,11... | collective-permute-start | bytes 3145736 | tf_op jit(solution)/shard_map/frame_out/ppermute | solution.py:26
  137.8 2.6 %collective-permute-start.24 = (f32[1,1024]{1,0:T(1,128)S(1)}, f32[1,1024]{1,0:T(1,128)S(1)}, u32[]{:S(2)}, u32[]{:S(2)}) collective-permute-start(f32[1,1024]{1,0:T(1,128)S(1)} %add.139.total_ref), channel_id=1, source_target_pairs={{0,1},{1,0},{2,3},{3,2},{4,5},{5,4},{6,7},{7,6},{8,9},{9,8},{10,11... | collective-permute-start | bytes 12296 | tf_op jit(solution)/shard_map/frame_out/ppermute | solution.py:26
  151.5 1.0 copy-start.10

commit v4 on v3

--- a/solution.py
+++ b/solution.py
@@ -13,7 +13,9 @@
 TOK = 256
 CHUNK = 128
 SPLIT = 4
+SHARES = (2, 3, 3)
 HELD = 4
+PAIR = 1
 EXTRA = 256
 ORDER = ((16, 2), (1, 4), (4, 4))
 VMEM_BYTES = 20 * 1024 * 1024
@@ -69,22 +71,25 @@
     t_refs, (f_ref, lse_ref, s_ref) = refs[:SPLIT], refs[SPLIT:]
     i = pl.program_id(0)
     tokens = jnp.concatenate([t_ref[...] for t_ref in t_refs])
-    s_ref[i] = (
-        lax.dot_general(tokens, f_ref[...], (((1,), (1,)), ((), ())), preferred_element_type=F32) * scale
-    )
-    highest = total = None
-    for c in range(0, tokens.shape[0], CHUNK):
-        s = s_ref[i, c : c + CHUNK, :].reshape(CHUNK // 8, 8, W)
-        top = jnp.max(s, axis=0)
-        if highest is None:
-            highest = top
-            total = jnp.sum(jnp.exp2(s - highest[None]), axis=0)
-        else:
-            top = jnp.maximum(highest, top)
-            total = total * jnp.exp2(highest - top) + jnp.sum(jnp.exp2(s - top[None]), axis=0)
-            highest = top
-    top = jnp.max(highest, axis=0, keepdims=True)
-    lse_ref[...] = top + log2(jnp.sum(total * jnp.exp2(highest - top), axis=0, keepdims=True))
+    product = lax.dot_general(tokens, f_ref[...], (((1,), (1,)), ((), ())), preferred_element_type=F32) * scale
+    count = f_ref.shape[0] // W
+    for n in range(count):
+        s_ref[i * count + n] = product[:, n * W : (n + 1) * W]
+    for n in range(count):
+        highest = total = None
+        for c in range(0, tokens.shape[0], CHUNK):
+            s = s_ref[i * count + n, c : c + CHUNK, :].reshape(CHUNK // 8, 8, W)
+            top = jnp.max(s, axis=0)
+            if highest is None:
+                highest = top
+                total = jnp.sum(jnp.exp2(s - highest[None]), axis=0)
+            else:
+                top = jnp.maximum(highest, top)
+                total = total * jnp.exp2(highest - top) + jnp.sum(jnp.exp2(s - top[None]), axis=0)
+                highest = top
+        top = jnp.max(highest, axis=0, keepdims=True)
+        lse = top + log2(jnp.sum(total * jnp.exp2(highest - top), axis=0, keepdims=True))
+        lse_ref[:, n * W : (n + 1) * W] = lse
 
 
 def first_cols(s_ref, all_ref, fm_ref, lse_ref, u_ref, mass_ref):
@@ -132,15 +137,9 @@
     sum_ref[:, row_slice(i, W)] = jnp.sum(total, axis=0, keepdims=True)
 
 
-def second_cols(e_ref, total_ref, fm_ref, f_ref, sum_ref, out_ref, share_ref, stored_ref, alpha_ref, sems):
+def col_sums(e_ref, total_ref, fm_ref, sum_ref, alpha_ref, share_ref):
     i = pl.program_id(0)
     nf = fm_ref.shape[1]
-
-    def store(step):
-        some = row_slice(step, TOK)
-        return pltpu.make_async_copy(e_ref.at[:, some, :], stored_ref.at[:, some, :], sems.at[step])
-
-    store(i).start()
 
     @pl.when(i == 0)
     def _():
@@ -148,27 +147,46 @@
         alpha_ref[...] = alpha
         share_ref[...] = alpha / wide(total_ref[:, nf : nf + 128], nf)
 
-    rows = row_slice(i, TOK)
-    acc = total = None
+    step = 64
+    found = []
+    for r in range(0, TOK, step):
+        rows = pl.ds(pl.multiple_of(i * TOK + r, step), step)
+        total = None
+        for c in range(e_ref.shape[0]):
+            p = e_ref[c, rows, :] * alpha_ref[:, c * W : (c + 1) * W]
+            for w in range(0, W, 128):
+                part = p[:, w : w + 128]
+                total = part if total is None else total + part
+        found.append(total)
+    sum_ref[...] = jnp.sum(jnp.concatenate(found).T, axis=0, keepdims=True)
+
+
+def token_parts(first, e_ref, alpha_ref, f_ref, *refs):
+    out_ref, stored_ref, sems = refs[-3:]
+    i = pl.program_id(0)
+
+    def store(step):
+        some = row_slice(first + step, TOK)
+        return pltpu.make_async_copy(e_ref.at[:, some, :], stored_ref.at[:, some, :], sems.at[step])
+
+    store(i).start()
+    rows = row_slice(first + i, TOK)
+    acc = None
     for c in range(e_ref.shape[0]):
-        p = e_ref[c, rows, :] * alpha_ref[:, c * W : (c + 1) * W]
-        part = p[:, :128]
-        for w in range(128, W, 128):
-            part = part + p[:, w : w + 128]
-        total = part if total is None else total + part
-        part = jnp.dot(p.astype(BF16), f_ref[c * W : (c + 1) * W, :], preferred_element_type=F32)
+        p = (e_ref[c, rows, :] * alpha_ref[:, c * W : (c + 1) * W]).astype(BF16)
+        part = jnp.dot(p, f_ref[c * W : (c + 1) * W, :], preferred_element_type=F32)
         acc = part if acc is None else acc + part
-    sum_ref[...] = jnp.sum(total.T, axis=0, keepdims=True)
     out_ref[...] = acc.astype(BF16)
 
     @pl.when(i == pl.num_programs(0) - 1)
     def _():
-        for step in range(e_ref.shape[1] // TOK):
+        for step in range(sems.shape[0]):
             store(step).wait()
 
 
 def frame_parts(
-    base_ref, e_ref, total_ref, tm_ref, share_ref, tt_ref, sum_ref, out_ref, col_ref, held_ref, sems
+    base_ref, e_ref, total_ref, tm_ref, share_ref, turned_ref, sum_ref, theirs_ref, mine_ref,
+    col_ref, held_ref, tt_ref, sems, tt_sem,
 ):
     i = pl.program_id(0)
     slabs = pl.num_programs(0)
@@ -179,9 +197,13 @@
 
     @pl.when(i == 0)
     def _():
-        for k in range(HELD - 1):
+        fetch(0).start()
+        copy = pltpu.make_async_copy(turned_ref, tt_ref, tt_sem)
+        copy.start()
+        for k in range(1, HELD - 1):
             fetch(k).start()
         column(tm_ref[...] / total_ref[...], col_ref)
+        copy.wait()
 
     @pl.when(i + HELD - 1 < slabs)
     def _():
@@ -191,7 +213,15 @@
     share = share_ref[:, row_slice(lax.rem(base_ref[0] + i, slabs), W)]
     p = held_ref[lax.rem(i, HELD)] * wide(col_ref[...], W) * share
     sum_ref[...] = jnp.sum(p, axis=0, keepdims=True)
-    out_ref[...] = jnp.dot(tt_ref[...], p.astype(BF16), preferred_element_type=F32).T.astype(BF16)
+    block = jnp.dot(tt_ref[...], p.astype(BF16), preferred_element_type=F32).T.astype(BF16)
+
+    @pl.when(i < slabs // 2)
+    def _():
+        theirs_ref[...] = block
+
+    @pl.when(i >= slabs // 2)
+    def _():
+        mine_ref[...] = block
 
 
 def sum_pieces(*refs):
@@ -232,27 +262,23 @@
         copy.wait()
 
 
-def finish_frames(mine_ref, other_ref, total_ref, out_ref, col_ref):
+def finish_frames(core_ref, mine_ref, other_ref, total_ref, out_ref, map_ref, col_ref, sem):
     column(total_ref[...], col_ref)
     rows, d = mine_ref.shape
     for r in range(0, rows, 128):
         some = slice(r, r + 128)
         done = (mine_ref[some, :].astype(F32) + other_ref[some, :].astype(F32)) / wide(col_ref[some, :], d)
         out_ref[some, :] = done.astype(BF16)
-
-
-def place_frames(core_ref, mine_ref, theirs_ref, out_ref, sems):
-    half = mine_ref.shape[0]
-    copies = []
-    for k, ref in enumerate((mine_ref, theirs_ref)):
-        start = lax.rem(core_ref[0] + k, 2) * half
-        copies.append(
-            pltpu.make_async_copy(ref, out_ref.at[pl.ds(pl.multiple_of(start, half), half), :], sems.at[k])
-        )
-    for copy in copies:
-        copy.start()
-    for copy in copies:
-        copy.wait()
+    copy = pltpu.make_async_copy(out_ref, map_ref.at[row_slice(core_ref[0], rows), :], sem)
+    copy.start()
+    copy.wait()
+
+
+def place_frames(core_ref, theirs_ref, half_ref, map_ref, sem):
+    rows = theirs_ref.shape[0]
+    copy = pltpu.make_async_copy(theirs_ref, map_ref.at[row_slice(1 - core_ref[0], rows), :], sem)
+    copy.start()
+    copy.wait()
 
 
 def whole(*shape):
@@ -296,9 +322,9 @@
     hbm = pl.BlockSpec(memory_space=pltpu.HBM)
 
     lse, s = call(
-        functools.partial(first_rows, scale), slabs,
-        [pl.BlockSpec((nt // SPLIT, d), lambda i, k=k: (k, 0)) for k in range(SPLIT)] + [rows(W, d)],
-        [lanes(W), VMEM], [f32(1, nf), kept], name="first_rows",
+        functools.partial(first_rows, scale), slabs // PAIR,
+        [pl.BlockSpec((nt // SPLIT, d), lambda i, k=k: (k, 0)) for k in range(SPLIT)] + [rows(PAIR * W, d)],
+        [lanes(PAIR * W), VMEM], [f32(1, nf), kept], name="first_rows",
     )(*[pltpu.with_memory_space_constraint(tokens, pltpu.HBM)] * SPLIT, pltpu.with_memory_space_constraint(frames, pltpu.HBM))
     with jax.named_scope("rows_one"):
         lse = merge_lse([lse, swap_tok(lse, 1)])
@@ -307,41 +333,80 @@
         first_cols, steps, [VMEM, whole(1, nf), whole(1, nf)], [lanes(TOK), whole(1, nf), whole(1, 128)],
         [f32(1, nt), f32(1, nf), f32(1, 128)], name="first_cols",
     )(s, lse, fm)
-    tokens_later, lse = lax.optimization_barrier((tokens, lse))
-    turned = call(
-        turn, 4, [rows(nt // 4, d)], pl.BlockSpec((d, nt // 4), lambda i: (0, i)), jax.ShapeDtypeStruct((d, nt), BF16),
-        name="turn",
-    )(tokens_later)
     with jax.named_scope("cols_one"):
         lse = jnp.concatenate([lse, frame_total], axis=1)
-        for stride, size in ORDER:
-            parts = ring(lse, stride, size)
-            merged = merge_lse([part[:, :nt] for part in parts])
-            lse = jnp.concatenate([merged, sum(part[:, nt:] for part in parts)], axis=1)
-        lse, frame_total = lse[:, :nt], lse[0, nt]
-        turned, lse = lax.optimization_barrier((turned, lse))
+        parts = lax.all_to_all(jnp.broadcast_to(lse[None], (n_ctx, 1, nt + 128)), "ctx", 0, 0)[:, 0]
+        highest = jnp.max(parts[:, :nt], axis=0, keepdims=True)
+        lse = highest + log2(jnp.sum(jnp.exp2(parts[:, :nt] - highest), axis=0, keepdims=True))
+        frame_total = jnp.sum(parts[:, nt])
     part, e = call(
         second_rows, slabs, [VMEM, whole(1, nt), whole(1, nt), whole(1, nf)], [whole(1, nf + EXTRA), VMEM],
         [f32(1, nf + EXTRA), kept], [pltpu.VMEM((nt, 128), F32)], input_output_aliases={0: 1}, name="second_rows",
     )(s, lse, tm, u)
     with jax.named_scope("rows_two"):
         part = part + swap_tok(part, 1)
+        tokens_later, part = lax.optimization_barrier((tokens, part))
+        turned = call(
+            turn, 4, [rows(nt // 4, d)], pl.BlockSpec((d, nt // 4), lambda i: (0, i)),
+            pltpu.HBM((d, nt), BF16), name="turn",
+        )(tokens_later)
         part = part + swap_tok(part, 2)
-    part, token_part, share, e = call(
-        second_cols, steps, [VMEM, whole(1, nf + EXTRA), whole(1, nf), whole(nf, d)],
-        [lanes(TOK), rows(TOK, d), whole(1, nf), hbm],
-        [f32(1, nt), jax.ShapeDtypeStruct((nt, d), BF16), f32(1, nf), pltpu.HBM((slabs, nt, W), F32)],
-        [pltpu.VMEM((1, nf), F32), pltpu.SemaphoreType.DMA((steps,))], name="second_cols",
-    )(e, part, fm, frames)
+        part, turned = lax.optimization_barrier((part, turned))
+    part, alpha, share = call(
+        col_sums, steps, [VMEM, whole(1, nf + EXTRA), whole(1, nf)], [lanes(TOK), whole(1, nf), whole(1, nf)],
+        [f32(1, nt), f32(1, nf), f32(1, nf)], name="col_sums",
+    )(e, part, fm)
+
+    def some_token_parts(first, count, held):
+        return call(
+            functools.partial(token_parts, first), count, [VMEM, whole(1, nf), whole(nf, d)] + [hbm] * len(held),
+            [pl.BlockSpec((TOK, d), lambda i: (first + i, 0)), hbm],
+            [pltpu.HBM((nt, d), BF16), pltpu.HBM((slabs, nt, W), F32)], [pltpu.SemaphoreType.DMA((count,))],
+            input_output_aliases={3 + k: k for k in range(len(held))}, name="token_parts",
+        )(e, alpha, frames, *held)
+
     with jax.named_scope("cols_two"):
+        held, first = [], 0
         col_total = part
-        for stride, size in ORDER:
+        for (stride, size), count in zip(ORDER, SHARES):
+            held = list(some_token_parts(first, count, held))
+            first += count
             col_total = sum(ring(col_total, stride, size))
+            col_total, held[0] = lax.optimization_barrier((col_total, held[0]))
+        token_part, e = held
     with jax.named_scope("token_scatter"):
-        token_part, col_total = lax.optimization_barrier((token_part, col_total))
         plane, own = 16, nt // 16
         planes = [list(range(z, z + plane)) for z in range(0, n_ctx, plane)]
         pieces = lax.all_to_all(token_part.reshape(plane, own, d), "ctx", 0, 0, axis_index_groups=planes)
+    e = pltpu.with_memory_space_constraint(e, pltpu.HBM)
+    half = slabs // 2
+    base = ((1 - core) * half).reshape(1).astype(jnp.int32)
+    with jax.named_scope("frame_rows"):
+        sums, theirs, mine = pl.pallas_call(
+            frame_parts,
+            grid=(slabs,),
+            in_specs=[SMEM, hbm, whole(1, nt), whole(1, nt), whole(1, nf), hbm],
+            out_specs=[
+                lanes(W),
+                pl.BlockSpec((W, d), lambda i: (jnp.minimum(i, half - 1), 0)),
+                pl.BlockSpec((W, d), lambda i: (jnp.maximum(i - half, 0), 0)),
+            ],
+            out_shape=[f32(1, nf)] + [jax.ShapeDtypeStruct((nf // 2, d), BF16)] * 2,
+            scratch_shapes=[
+                pltpu.VMEM((nt, 128), F32),
+                pltpu.VMEM((HELD, nt, W), F32),
+                pltpu.VMEM((d, nt), BF16),
+                pltpu.SemaphoreType.DMA((HELD,)),
+                pltpu.SemaphoreType.DMA,
+            ],
+            compiler_params=pltpu.CompilerParams(vmem_limit_bytes=VMEM_BYTES),
+            name="frame_parts",
+        )(base, e, col_total, tm, share, pltpu.with_memory_space_constraint(turned, pltpu.HBM))
+        my_sum = sums[:, nf // 2 :] + swap_tok(sums[:, : nf // 2], 1)
+        other_sum = swap_tok(my_sum, 2)
+        mine = (mine.astype(F32) + swap_tok(theirs, 1).astype(F32)).astype(BF16)
+    with jax.named_scope("token_sums"):
+        pieces, mine, other_sum = lax.optimization_barrier((pieces, mine, other_sum))
         deal = own // (2 * SPLIT)
         piece = call(
             sum_pieces, 2,
@@ -350,31 +415,6 @@
         )(*[pieces] * SPLIT)
         other_piece = shift(piece, 16, 1, 2)
 
-    e = pltpu.with_memory_space_constraint(e, pltpu.HBM)
-    half = slabs // 2
-    base = ((1 - core) * half).reshape(1).astype(jnp.int32)
-    with jax.named_scope("frame_rows"):
-        sums, parts = pl.pallas_call(
-            frame_parts,
-            grid=(slabs,),
-            in_specs=[SMEM, hbm, whole(1, nt), whole(1, nt), whole(1, nf), whole(d, nt)],
-            out_specs=[lanes(W), rows(W, d)],
-            out_shape=[f32(1, nf), jax.ShapeDtypeStruct((nf, d), BF16)],
-            scratch_shapes=[
-                pltpu.VMEM((nt, 128), F32),
-                pltpu.VMEM((HELD, nt, W), F32),
-                pltpu.SemaphoreType.DMA((HELD,)),
-            ],
-            compiler_params=pltpu.CompilerParams(vmem_limit_bytes=VMEM_BYTES),
-            name="frame_parts",
-        )(base, e, col_total, tm, share, turned)
-        my_sum = sums[:, nf // 2 :] + swap_tok(sums[:, : nf // 2], 1)
-        mine = (parts[nf // 2 :].astype(F32) + swap_tok(parts[: nf // 2], 1).astype(F32)).astype(BF16)
-        mine, my_sum = lax.optimization_barrier((mine, my_sum))
-        other_sum = swap_tok(my_sum, 2)
-        mine, other_piece, other_sum = lax.optimization_barrier((mine, other_piece, other_sum))
-        other = swap_tok(mine, 2)
-        my_sum = my_sum + other_sum
     with jax.named_scope("token_gather"):
         col_mine = lax.dynamic_slice_in_dim(col_total, ctx % plane * own, own, axis=1)
         pieces = pl.pallas_call(
@@ -386,7 +426,30 @@
             ],
             compiler_params=pltpu.CompilerParams(vmem_limit_bytes=VMEM_BYTES), name="finish_pieces",
         )(piece, other_piece, col_mine)
+        mine, pieces = lax.optimization_barrier((mine, pieces))
+        other = swap_tok(mine, 2)
         pieces = lax.all_to_all(pieces, "ctx", 0, 0, axis_index_groups=planes)
+    with jax.named_scope("frame_sums"):
+        my_sum = my_sum + other_sum
+        their_sum = swap_tok(my_sum, 1)
+        low = jnp.where(core == 0, my_sum, their_sum)
+        high = jnp.where(core == 0, their_sum, my_sum)
+        row_sum = jnp.concatenate([low, high], axis=1)[0]
+        mass_ratio = row_sum / (frame_mass / frame_total)
+        other, mass_ratio = lax.optimization_barrier((other, mass_ratio))
+    with jax.named_scope("frame_out"):
+        which = core.reshape(1).astype(jnp.int32)
+        mine, frame_map = pl.pallas_call(
+            finish_frames, in_specs=[SMEM] + [VMEM] * 3, out_specs=[VMEM, hbm],
+            out_shape=[jax.ShapeDtypeStruct((nf // 2, d), BF16), pltpu.HBM((nf, d), BF16)],
+            scratch_shapes=[pltpu.VMEM((nf // 2, 128), F32), pltpu.SemaphoreType.DMA],
+            compiler_params=pltpu.CompilerParams(vmem_limit_bytes=VMEM_BYTES), name="finish_frames",
+        )(which, mine, other, my_sum)
+        frame_map = pl.pallas_call(
+            place_frames, in_specs=[SMEM, VMEM, hbm], out_specs=hbm, out_shape=pltpu.HBM((nf, d), BF16),
+            scratch_shapes=[pltpu.SemaphoreType.DMA], input_output_aliases={2: 0}, name="place_frames",
+        )(which, swap_tok(mine, 1), frame_map)
+        pieces, frame_map = lax.optimization_barrier((pieces, frame_map))
         token_map = pl.pallas_call(
             place_tokens, in_specs=[hbm], out_specs=hbm, out_shape=pltpu.HBM((nt, d), BF16),
             scratch_shapes=[
@@ -396,22 +459,6 @@
             ],
             compiler_params=pltpu.CompilerParams(vmem_limit_bytes=VMEM_BYTES), name="place_tokens",
         )(pltpu.with_memory_space_constraint(pieces, pltpu.HBM))
-    with jax.named_scope("frame_out"):
-        mine = pl.pallas_call(
-            finish_frames, in_specs=[VMEM] * 3, out_specs=VMEM, out_shape=jax.ShapeDtypeStruct((nf // 2, d), BF16),
-            scratch_shapes=[pltpu.VMEM((nf // 2, 128), F32)],
-            compiler_params=pltpu.CompilerParams(vmem_limit_bytes=VMEM_BYTES), name="finish_frames",
-        )(mine, other, my_sum)
-        theirs = swap_tok(mine, 1)
-        their_sum = swap_tok(my_sum, 1)
-        frame_map = pl.pallas_call(
-            place_frames, in_specs=[SMEM, VMEM, VMEM], out_specs=ANY, out_shape=jax.ShapeDtypeStruct((nf, d), BF16),
-            scratch_shapes=[pltpu.SemaphoreType.DMA((2,))], name="place_frames",
-        )(core.reshape(1).astype(jnp.int32), mine, theirs)
-        low = jnp.where(core == 0, my_sum, their_sum)
-        high = jnp.where(core == 0, their_sum, my_sum)
-        row_sum = jnp.concatenate([low, high], axis=1)[0]
-        mass_ratio = row_sum / (frame_mass / frame_total)
     return frame_map, token_map, mass_ratio
 
 

time: 156 us -> 150 us (0.962)
  waiting for transfers between devices: 59.1 us -> 41.9 us
  blocking collectives: 0 us -> 17.1 us
  starting transfers between devices: 46.6 us -> 34.1 us
  Pallas kernels: 42.3 us -> 50 us
  local copies, waits for them, and re-layouts: 5.11 us -> 1.74 us
  other arithmetic: 1.37 us -> 3.25 us
    all_to_all x0 -> x1, blocking collectives: none -> 17.1 us  [shards(): lax.all_to_all(jnp.broadcast_to(lse[None], (n_ctx, 1, nt + 128)), 'ctx',...]
    ppermute x15 -> x8, starting transfers between devices: 24.7 us -> 8.79 us  [shift(): return lax.ppermute(value, 'ctx', pairs)]
    ppermute x15 -> x8, waiting for transfers between devices: 14.9 us -> 5.74 us  [shift(): return lax.ppermute(value, 'ctx', pairs)]
    pallas_call x4 -> x7, Pallas kernels: 18.5 us -> 24 us  [the longest x3 10 us: some_token_parts(): call(functools.partial(token_parts, first), count, [VMEM, whole(1, nf), w...]
    ppermute x10, waiting for transfers between devices: 24.7 us -> 21.2 us  [swap_tok(): lax.ppermute(value, 'tok', [(i, i ^ bit) for i in range(lax.axis_size('to...]
    all_to_all x1, waiting for transfers between devices: 11.7 us -> 8.87 us  [shards(): lax.all_to_all(token_part.reshape(plane, own, d), 'ctx', 0, 0, axis_index...]
    unnamed x22 -> x13, local copies, waits for them, and re-layouts: 3.94 us -> 1.6 us
    all_to_all x1, starting transfers between devices: 3.84 us -> 5.72 us  [shards(): lax.all_to_all(token_part.reshape(plane, own, d), 'ctx', 0, 0, axis_index...]
  transfers between devices with their start and end apart: 27 -> 20, of which waited for: 21 -> 13; matrix products, arithmetic and copies ran while one was open for 1% -> 2% of each run, Pallas kernels for 10% -> 18%
where the time goes in v4:
time: 150 us; the launch traced here: 149 us
  Pallas kernels  50 us (33%)
  waiting for transfers between devices  41.9 us (28%)
  starting transfers between devices  34.1 us (23%)
  blocking collectives  17.1 us (11%)
  other arithmetic  3.25 us (2%)
  local copies, waits for them, and re-layouts  1.74 us (1%)
    ppermute x10, waiting for transfers between devices, swap_tok(): lax.ppermute(value, 'tok', [(i, i ^ bit) for i in range(lax.axis_size('to...  21.2 us
    all_to_all x1, blocking collectives, shards(): lax.all_to_all(jnp.broadcast_to(lse[None], (n_ctx, 1, nt + 128)), 'ctx',...  17.1 us
    ppermute x10, starting transfers between devices, swap_tok(): lax.ppermute(value, 'tok', [(i, i ^ bit) for i in range(lax.axis_size('to...  15.2 us
    pallas_call x1, Pallas kernels, shards(): pl.pallas_call(frame_parts, grid=(slabs,), in_specs=[SMEM, hbm, whole(1,...  10.5 us
    pallas_call x3, Pallas kernels, some_token_parts(): call(functools.partial(token_parts, first), count, [VMEM, whole(1, nf), w...  10 us
    all_to_all x1, waiting for transfers between devices, shards(): lax.all_to_all(token_part.reshape(plane, own, d), 'ctx', 0, 0, axis_index...  8.87 us
    ppermute x8, starting transfers between devices, shift(): return lax.ppermute(value, 'ctx', pairs)  8.79 us
    pallas_call x1, Pallas kernels, shards(): call(functools.partial(first_rows, scale), slabs // PAIR, [pl.BlockSpec((...  8.55 us
  transfers between devices with their start and end apart: 20, of which 13 were waited for; matrix products, arithmetic and copies ran while one was open for 2% of the time, Pallas kernels for 18%

profile of v4, /device:TPU:0, one launch (start us, length us, event | category | flops | bytes accessed | tf_op | source)
XLA Modules:
  0.0 149.1 jit_solution(11137242216799532268)
XLA Ops:
  0.6 8.6 %first_rows.1 = (f32[1,2048]{1,0:T(1,128)S(1)}, f32[8,2048,256]{2,1,0:T(8,128)S(1)}) custom-call(bf16[2048,512]{1,0:T(8,128)(2,1)} %in_ref, bf16[2048,512]{1,0:T(8,128)(2,1)} %in_ref, bf16[2048,512]{1,0:T(8,128)(2,1)} %in_ref, bf16[2048,512]{1,0:T(8,128)(2,1)} %in_ref, bf16[2048,512]{1,0:T(8,128)(2,1)} %f_ref.5), custom_call_target="tpu_custom_call" | custom-call | tf_op jit(solution)/shard_map/first_rows/pallas_call | solution.py:324
  9.3 1.2 collective-permute-done
  10.5 4.0 %collective-permute-start.1 = (f32[1,2048]{1,0:T(1,128)S(1)}, f32[1,2048]{1,0:T(1,128)S(1)}, u32[]{:S(2)}, u32[]{:S(2)}) collective-permute-start(f32[1,2048]{1,0:T(1,128)S(1)} %multiply_add_fusion.2), channel_id=1, source_target_pairs={{0,2},{1,3},{2,0},{3,1},{4,6},{5,7},{6,4},{7,5},{8,10},{9,11},{10,... | collective-permute-start | bytes 24584 | tf_op jit(solution)/shard_map/rows_one/ppermute | solution.py:28
  14.5 1.6 %collective-permute-done.1 = f32[1,2048]{1,0:T(1,128)S(1)} collective-permute-done((f32[1,2048]{1,0:T(1,128)S(1)}, f32[1,2048]{1,0:T(1,128)S(1)}, u32[]{:S(2)}, u32[]{:S(2)}) %collective-permute-start.1) | collective-permute-done | bytes 8224 | tf_op jit(solution)/shard_map/rows_one/ppermute | solution.py:28
  16.2 4.8 %first_cols.1 = (f32[1,2048]{1,0:T(1,128)S(1)}, f32[1,2048]{1,0:T(1,128)S(1)}, f32[1,128]{1,0:T(1,128)S(1)}) custom-call(f32[8,2048,256]{2,1,0:T(8,128)S(1)} %get-tuple-element.43.s_ref, f32[1,2048]{1,0:T(1,128)S(1)} %multiply_add_fusion.1.all_ref, f32[1,2048]{1,0:T(1,128)S(1)} %bitcast.10), custom_call_target="tpu_custom_call" | custom-call | tf_op jit(solution)/shard_map/first_cols/pallas_call | solution.py:332
  21.2 17.1 %all_to_all.15 = f32[32,1,2176]{2,1,0:T(1,128)S(1)} all-to-all(f32[32,1,2176]{2,1,0:T(1,128)S(1)} %broadcast_in_dim.5), channel_id=1, replica_groups=mesh['ctx'=32,'tok'=4] {'ctx'}, dimensions={0} | all-to-all | bytes 557056 | tf_op jit(solution)/shard_map/cols_one/all_to_all | solution.py:338
  38.5 0.6 copy-done.4
  39.1 4.0 %second_rows.1 = (f32[1,2304]{1,0:T(1,128)S(1)}, f32[8,2048,256]{2,1,0:T(8,128)S(1)}) custom-call(f32[8,2048,256]{2,1,0:T(8,128)S(1)} %get-tuple-element.43.s_ref, f32[1,2048]{1,0:T(1,128)S(1)} %bitcast.14, f32[1,2048]{1,0:T(1,128)S(1)} %bitcast.12, f32[1,2048]{1,0:T(1,128)S(1)} %get-tuple-element.47.u_ref), custom_call_target="tpu_custom_call", output_to_operand_aliasing={{1}: (0, {})} | custom-call | tf_op jit(solution)/shard_map/second_rows/pallas_call | solution.py:342
  43.1 1.2 collective-permute-done.2
  44.3 3.7 %collective-permute-start.3 = (f32[1,2304]{1,0:T(1,128)S(1)}, f32[1,2304]{1,0:T(1,128)S(1)}, u32[]{:S(2)}, u32[]{:S(2)}) collective-permute-start(f32[1,2304]{1,0:T(1,128)S(1)} %add.69), channel_id=1, source_target_pairs={{0,2},{1,3},{2,0},{3,1},{4,6},{5,7},{6,4},{7,5},{8,10},{9,11},{10,... | collective-permute-start | bytes 27656 | tf_op jit(solution)/shard_map/rows_two/ppermute | solution.py:28
  48.0 2.2 %turn.1.turned_ref = bf16[512,2048]{1,0:T(8,128)(2,1)} custom-call(bf16[2048,512]{1,0:T(8,128)(2,1)S(1)} %copy-done), custom_call_target="tpu_custom_call" | custom-call | tf_op jit(solution)/shard_map/rows_two/turn/pallas_call | solution.py:349
  50.2 1.9 %col_sums.1 = (f32[1,2048]{1,0:T(1,128)S(1)}, f32[1,2048]{1,0:T(1,128)S(1)}, f32[1,2048]{1,0:T(1,128)S(1)}) custom-call(f32[8,2048,256]{2,1,0:T(8,128)S(1)} %get-tuple-element.48.e_ref, f32[1,2304]{1,0:T(1,128)S(1)} %add.70.total_ref, f32[1,2048]{1,0:T(1,128)S(1)} %bitcast.11), custom_call_target="tpu_custom_call" | custom-call | tf_op jit(solution)/shard_map/col_sums/pallas_call | solution.py:355
  52.1 0.3 collective-permute-start.4
  52.4 2.8 %token_parts.3 = (bf16[2048,512]{1,0:T(8,128)(2,1)}, f32[8,2048,256]{2,1,0:T(8,128)}) custom-call(f32[8,2048,256]{2,1,0:T(8,128)S(1)} %get-tuple-element.48.e_ref, f32[1,2048]{1,0:T(1,128)S(1)} %get-tuple-element.54.alpha_ref, bf16[2048,512]{1,0:T(8,128)(2,1)S(1)} %copy-done.1), custom_call_target="tpu_custom_call" | custom-call | tf_op jit(solution)/shard_map/cols_two/token_parts/pallas_call | solution.py:361
  55.2 0.6 collective-permute-done.4
  55.8 1.6 %collective-permute-start.7 = (f32[1,2048]{1,0:T(1,128)S(1)}, f32[1,2048]{1,0:T(1,128)S(1)}, u32[]{:S(2)}, u32[]{:S(2)}) collective-permute-start(f32[1,2048]{1,0:T(1,128)S(1)} %add.71), channel_id=1, source_target_pairs={{0,12},{4,0},{8,4},{12,8},{16,28},{20,16},{24,20},{28,24},{32,44},... | collective-permute-start | bytes 24584 | tf_op jit(solution)/shard_map/cols_two/ppermute | solution.py:36
  57.4 1.1 collective-permute-start.6
  58.5 0.5 collective-permute-start.5
  59.0 3.6 %token_parts.4 = (bf16[2048,512]{1,0:T(8,128)(2,1)}, f32[8,2048,256]{2,1,0:T(8,128)}) custom-call(f32[8,2048,256]{2,1,0:T(8,128)S(1)} %get-tuple-element.48.e_ref, f32[1,2048]{1,0:T(1,128)S(1)} %get-tuple-element.54.alpha_ref, bf16[2048,512]{1,0:T(8,128)(2,1)S(1)} %copy-done.1, ...), custom_call_target="tpu_custom_call", output_to_operand_aliasing={{0}: (3, {}), {1}: (4, {})} | custom-call | tf_op jit(solution)/shard_map/cols_two/token_parts/pallas_call | solution.py:361
  62.6 0.7 collective-permute-done.5
  63.4 1.2 collective-permute-start.10
  64.6 1.3 collective-permute-start.9
  65.8 0.6 collective-permute-start.8
  66.4 3.6 %token_parts.5 = (bf16[2048,512]{1,0:T(8,128)(2,1)}, f32[8,2048,256]{2,1,0:T(8,128)}) custom-call(f32[8,2048,256]{2,1,0:T(8,128)S(1)} %get-tuple-element.48.e_ref, f32[1,2048]{1,0:T(1,128)S(1)} %get-tuple-element.54.alpha_ref, bf16[2048,512]{1,0:T(8,128)(2,1)S(1)} %copy-done.1, ...), custom_call_target="tpu_custom_call", output_to_operand_aliasing={{0}: (3, {}), {1}: (4, {})} | custom-call | tf_op jit(solution)/shard_map/cols_two/token_parts/pallas_call | solution.py:361
  70.1 0.6 collective-permute-done.8
  70.7 5.7 %all-to-all-start.1 = ((bf16[16,128,512]{2,1,0:T(8,128)(2,1)}), bf16[16,128,512]{2,1,0:T(8,128)(2,1)S(1)}, u32[]{:S(2)}, u32[]{:S(2)}) async-start(bf16[16,128,512]{2,1,0:T(8,128)(2,1)} %bitcast.15), calls=%async_computation.1 | async-start | bytes 4194304 | tf_op jit(solution)/shard_map/token_scatter/all_to_all | solution.py:380
  76.5 10.5 %frame_parts.1 = (f32[1,2048]{1,0:T(1,128)S(1)}, bf16[1024,512]{1,0:T(8,128)(2,1)S(1)}, bf16[1024,512]{1,0:T(8,128)(2,1)S(1)}) custom-call(s32[1]{0:T(128)} %bitcast.4.base_ref, f32[8,2048,256]{2,1,0:T(8,128)} %get-tuple-element.65.e_ref, f32[1,2048]{1,0:T(1,128)S(1)} %add_add_fusion.total_ref, f32[1,2048]{1,0:T(1,128)S(1)} %bitcast.13, ...), custom_call_target="tpu_custom_call" | custom-call | tf_op jit(solution)/shard_map/frame_rows/frame_parts/pallas_call | solution.py:385
  87.1 0.5 collective-permute-start.12
  87.6 2.2 %collective-permute-done.12 = f32[1,1024]{1,0:T(1,128)S(1)} collective-permute-done((f32[1,1024]{1,0:T(1,128)S(1)}, f32[1,1024]{1,0:T(1,128)S(1)}, u32[]{:S(2)}, u32[]{:S(2)}) %collective-permute-start.12) | collective-permute-done | bytes 4128 | tf_op jit(solution)/shard_map/frame_rows/ppermute | solution.py:28
  89.7 3.0 %collective-permute-start.13 = (f32[1,1024]{1,0:T(1,128)S(1)}, f32[1,1024]{1,0:T(1,128)S(1)}, u32[]{:S(2)}, u32[]{:S(2)}) collective-permute-start(f32[1,1024]{1,0:T(1,128)S(1)} %slice_add_fusion), channel_id=1, source_target_pairs={{0,2},{1,3},{2,0},{3,1},{4,6},{5,7},{6,4},{7,5},{8,10},{9,11},{10,... | collective-permute-start | bytes 12296 | tf_op jit(solution)/shard_map/frame_rows/ppermute | solution.py:28
  93.1 1.8 %collective-permute-done.13 = f32[1,1024]{1,0:T(1,128)S(1)} collective-permute-done((f32[1,1024]{1,0:T(1,128)S(1)}, f32[1,1024]{1,0:T(1,128)S(1)}, u32[]{:S(2)}, u32[]{:S(2)}) %collective-permute-start.13) | collective-permute-done | bytes 4128 | tf_op jit(solution)/shard_map/frame_rows/ppermute | solution.py:28
  94.9 8.9 %all-to-all-done.1.refs_0_.refs_1_.refs_2_.refs_3_ = bf16[16,128,512]{2,1,0:T(8,128)(2,1)S(1)} async-done(((bf16[16,128,512]{2,1,0:T(8,128)(2,1)}), bf16[16,128,512]{2,1,0:T(8,128)(2,1)S(1)}, u32[]{:S(2)}, u32[]{:S(2)}) %all-to-all-start.1) | async-done | bytes 2097184 | tf_op jit(solution)/shard_map/token_scatter/all_to_all | solution.py:380
  103.7 0.5 sum_pieces.1.mine_ref
  104.2 2.2 %collective-permute-start.14 = (bf16[128,512]{1,0:T(8,128)(2,1)S(1)}, bf16[128,512]{1,0:T(8,128)(2,1)S(1)}, u32[]{:S(2)}, u32[]{:S(2)}) collective-permute-start(bf16[128,512]{1,0:T(8,128)(2,1)S(1)} %sum_pieces.1.mine_ref), channel_id=1, source_target_pairs={{0,64},{4,68},{8,72},{12,76},{16,80},{20,84},{24,88},{28,92},{32,9... | collective-permute-start | bytes 393224 | tf_op jit(solution)/shard_map/token_sums/ppermute | solution.py:36
  106.4 3.8 %collective-permute-done.14.other_ref = bf16[128,512]{1,0:T(8,128)(2,1)S(1)} collective-permute-done((bf16[128,512]{1,0:T(8,128)(2,1)S(1)}, bf16[128,512]{1,0:T(8,128)(2,1)S(1)}, u32[]{:S(2)}, u32[]{:S(2)}) %collective-permute-start.14) | collective-permute-done | bytes 131104 | tf_op jit(solution)/shard_map/token_sums/ppermute | solution.py:36
  110.3 1.5 %finish_pieces.1 = bf16[16,128,512]{2,1,0:T(8,128)(2,1)} custom-call(bf16[128,512]{1,0:T(8,128)(2,1)S(1)} %sum_pieces.1.mine_ref, bf16[128,512]{1,0:T(8,128)(2,1)S(1)} %collective-permute-done.14.other_ref, f32[1,128]{1,0:T(1,128)S(1)} %constant_dynamic-slice_fusion.total_ref), custom_call_target="tpu_custom_call" | custom-call | tf_op jit(solution)/shard_map/token_gather/finish_pieces/pallas_call | solution.py:420
  111.8 3.6 %collective-permute-start.15 = (bf16[1024,512]{1,0:T(8,128)(2,1)S(1)}, bf16[1024,512]{1,0:T(8,128)(2,1)S(1)}, u32[]{:S(2)}, u32[]{:S(2)}) collective-permute-start(bf16[1024,512]{1,0:T(8,128)(2,1)S(1)} %add_convert_fusion.mine_ref), channel_id=1, source_target_pairs={{0,2},{1,3},{2,0},{3,1},{4,6},{5,7},{6,4},{7,5},{8,10},{9,11},{10,... | collective-permute-start | bytes 3145736 | tf_op jit(solution)/shard_map/token_gather/ppermute | solution.py:28
  115.4 4.4 %all-to-all-start.2 = ((bf16[16,128,512]{2,1,0:T(8,128)(2,1)}), bf16[16,128,512]{2,1,0:T(8,128)(2,1)}, u32[]{:S(2)}, u32[]{:S(2)}) async-start(bf16[16,128,512]{2,1,0:T(8,128)(2,1)} %finish_pieces.1), calls=%async_computation.2 | async-start | bytes 4194304 | tf_op jit(solution)/shard_map/token_gather/all_to_all | solution.py:431
  120.0 1.3 slice_reduce_fusion.1
  121.3 0.7 maximum_multiply_fusion
  122.0 0.6 div.8
  122.6 10.6 %collective-permute-done.15.other_ref = bf16[1024,512]{1,0:T(8,128)(2,1)S(1)} collective-permute-done((bf16[1024,512]{1,0:T(8,128)(2,1)S(1)}, bf16[1024,512]{1,0:T(8,128)(2,1)S(1)}, u32[]{:S(2)}, u32[]{:S(2)}) %collective-permute-start.15) | collective-permute-done | bytes 1048608 | tf_op jit(solution)/shard_map/token_gather/ppermute | solution.py:28
  133.2 1.3 finish_frames.1
  134.6 2.6 %collective-permute-done.17.theirs_ref = bf16[1024,512]{1,0:T(8,128)(2,1)S(1)} collective-permute-done((bf16[1024,512]{1,0:T(8,128)(2,1)S(1)}, bf16[1024,512]{1,0:T(8,128)(2,1)S(1)}, u32[]{:S(2)}, u32[]{:S(2)}) %collective-permute-start.17) | collective-permute-done | bytes 1048608 | tf_op jit(solution)/shard_map/frame_out/ppermute | solution.py:28
  137.2 1.0 copy-done.5
  138.2 2.2 %place_frames.1 = bf16[2048,512]{1,0:T(8,128)(2,1)} custom-call(s32[1]{0:T(128)} %bitcast.5.core_ref, bf16[1024,512]{1,0:T(8,128)(2,1)} %copy-done.5, bf16[2048,512]{1,0:T(8,128)(2,1)} %get-tuple-element.79.half_ref), custom_call_target="tpu_custom_call", output_to_operand_aliasing={{}: (2, {})} | custom-call | tf_op jit(solution)/shard_map/frame_out/place_frames/pallas_call | solution.py:448
  140.4 6.1 %all-to-all-done.2.pieces_ref = bf16[16,128,512]{2,1,0:T(8,128)(2,1)} async-done(((bf16[16,128,512]{2,1,0:T(8,128)(2,1)}), bf16[16,128,512]{2,1,0:T(8,128)(2,1)}, u32[]{:S(2)}, u32[]{:S(2)}) %all-to-all-start.2) | async-done | bytes 2097184 | tf_op jit(solution)/shard_map/token_gather/all_to_all | solution.py:431
  146.5 2.6 %place_tokens.1 = bf16[2048,512]{1,0:T(8,128)(2,1)} custom-call(bf16[16,128,512]{2,1,0:T(8,128)(2,1)} %all-to-all-done.2.pieces_ref), custom_call_target="tpu_custom_call" | custom-call | tf_op jit(solution)/shard_map/frame_out/place_tokens/pallas_call | solution.py:453
  (41 shorter events, 1.3 us)
Async XLA Ops:
  0.6 15.6 %copy-start.2 = (f32[2048]{0:T(1024)S(1)}, f32[2048]{0:T(1024)}, u32[]{:S(2)}) copy-start(f32[2048]{0:T(1024)} %param.6) | copy-start | bytes 24580
  9.2 1.3 collective-permute-start
  10.5 5.7 %collective-permute-start.1 = (f32[1,2048]{1,0:T(1,128)S(1)}, f32[1,2048]{1,0:T(1,128)S(1)}, u32[]{:S(2)}, u32[]{:S(2)}) collective-permute-start(f32[1,2048]{1,0:T(1,128)S(1)} %multiply_add_fusion.2), channel_id=1, source_target_pairs={{0,2},{1,3},{2,0},{3,1},{4,6},{5,7},{6,4},{7,5},{8,10},{9,11},{10,... | collective-permute-start | bytes 24584 | tf_op jit(solution)/shard_map/rows_one/ppermute | solution.py:28
  16.2 22.8 %copy-start.3 = (f32[2048]{0:T(1024)S(1)}, f32[2048]{0:T(1024)}, u32[]{:S(2)}) copy-start(f32[2048]{0:T(1024)} %param.7) | copy-start | bytes 24580
  38.4 0.7 copy-start.4
  39.1 8.9 %copy-start = (bf16[2048,512]{1,0:T(8,128)(2,1)S(1)}, bf16[2048,512]{1,0:T(8,128)(2,1)}, u32[]{:S(2)}) copy-start(bf16[2048,512]{1,0:T(8,128)(2,1)} %in_ref) | copy-start | bytes 6291460
  43.1 1.3 collective-permute-start.2
  44.3 5.8 %collective-permute-start.3 = (f32[1,2304]{1,0:T(1,128)S(1)}, f32[1,2304]{1,0:T(1,128)S(1)}, u32[]{:S(2)}, u32[]{:S(2)}) collective-permute-start(f32[1,2304]{1,0:T(1,128)S(1)} %add.69), channel_id=1, source_target_pairs={{0,2},{1,3},{2,0},{3,1},{4,6},{5,7},{6,4},{7,5},{8,10},{9,11},{10,... | collective-permute-start | bytes 27656 | tf_op jit(solution)/shard_map/rows_two/ppermute | solution.py:28
  50.2 2.2 %copy-start.1 = (bf16[2048,512]{1,0:T(8,128)(2,1)S(1)}, bf16[2048,512]{1,0:T(8,128)(2,1)}, u32[]{:S(2)}) copy-start(bf16[2048,512]{1,0:T(8,128)(2,1)} %f_ref.5) | copy-start | bytes 6291460
  52.1 3.7 %collective-permute-start.4 = (f32[1,2048]{1,0:T(1,128)S(1)}, f32[1,2048]{1,0:T(1,128)S(1)}, u32[]{:S(2)}, u32[]{:S(2)}) collective-permute-start(f32[1,2048]{1,0:T(1,128)S(1)} %get-tuple-element.53), channel_id=1, source_target_pairs={{0,64},{4,68},{8,72},{12,76},{16,80},{20,84},{24,88},{28,92},{32,9... | collective-permute-start | bytes 24584 | tf_op jit(solution)/shard_map/cols_two/ppermute | solution.py:36
  55.8 6.8 %collective-permute-start.7 = (f32[1,2048]{1,0:T(1,128)S(1)}, f32[1,2048]{1,0:T(1,128)S(1)}, u32[]{:S(2)}, u32[]{:S(2)}) collective-permute-start(f32[1,2048]{1,0:T(1,128)S(1)} %add.71), channel_id=1, source_target_pairs={{0,12},{4,0},{8,4},{12,8},{16,28},{20,16},{24,20},{28,24},{32,44},... | collective-permute-start | bytes 24584 | tf_op jit(solution)/shard_map/cols_two/ppermute | solution.py:36
  57.4 5.2 %collective-permute-start.6 = (f32[1,2048]{1,0:T(1,128)S(1)}, f32[1,2048]{1,0:T(1,128)S(1)}, u32[]{:S(2)}, u32[]{:S(2)}) collective-permute-start(f32[1,2048]{1,0:T(1,128)S(1)} %add.71), channel_id=1, source_target_pairs={{0,8},{4,12},{8,0},{12,4},{16,24},{20,28},{24,16},{28,20},{32,40},... | collective-permute-start | bytes 24584 | tf_op jit(solution)/shard_map/cols_two/ppermute | solution.py:36
  58.5 4.9 %collective-permute-start.5 = (f32[1,2048]{1,0:T(1,128)S(1)}, f32[1,2048]{1,0:T(1,128)S(1)}, u32[]{:S(2)}, u32[]{:S(2)}) collective-permute-start(f32[1,2048]{1,0:T(1,128)S(1)} %add.71), channel_id=1, source_target_pairs={{0,4},{4,8},{8,12},{12,0},{16,20},{20,24},{24,28},{28,16},{32,36},... | collective-permute-start | bytes 24584 | tf_op jit(solution)/shard_map/cols_two/ppermute | solution.py:36
  63.4 6.7 %collective-permute-start.10 = (f32[1,2048]{1,0:T(1,128)S(1)}, f32[1,2048]{1,0:T(1,128)S(1)}, u32[]{:S(2)}, u32[]{:S(2)}) collective-permute-start(f32[1,2048]{1,0:T(1,128)S(1)} %add_add_fusion.1), channel_id=1, source_target_pairs={{0,48},{4,52},{8,56},{12,60},{16,0},{20,4},{24,8},{28,12},{32,16},... | collective-permute-start | bytes 24584 | tf_op jit(solution)/shard_map/cols_two/ppermute | solution.py:36
  64.6 5.5 %collective-permute-start.9 = (f32[1,2048]{1,0:T(1,128)S(1)}, f32[1,2048]{1,0:T(1,128)S(1)}, u32[]{:S(2)}, u32[]{:S(2)}) collective-permute-start(f32[1,2048]{1,0:T(1,128)S(1)} %add_add_fusion.1), channel_id=1, source_target_pairs={{0,32},{4,36},{8,40},{12,44},{16,48},{20,52},{24,56},{28,60},{32,0... | collective-permute-start | bytes 24584 | tf_op jit(solution)/shard_map/cols_two/ppermute | solution.py:36
  65.8 4.9 %collective-permute-start.8 = (f32[1,2048]{1,0:T(1,128)S(1)}, f32[1,2048]{1,0:T(1,128)S(1)}, u32[]{:S(2)}, u32[]{:S(2)}) collective-permute-start(f32[1,2048]{1,0:T(1,128)S(1)} %add_add_fusion.1), channel_id=1, source_target_pairs={{0,16},{4,20},{8,24},{12,28},{16,32},{20,36},{24,40},{28,44},{32,4... | collective-permute-start | bytes 24584 | tf_op jit(solution)/shard_map/cols_two/ppermute | solution.py:36
  70.7 33.0 %all-to-all-start.1 = ((bf16[16,128,512]{2,1,0:T(8,128)(2,1)}), bf16[16,128,512]{2,1,0:T(8,128)(2,1)S(1)}, u32[]{:S(2)}, u32[]{:S(2)}) async-start(bf16[16,128,512]{2,1,0:T(8,128)(2,1)} %bitcast.15), calls=%async_computation.1 | async-start | bytes 4194304 | tf_op jit(solution)/shard_map/token_scatter/all_to_all | solution.py:380
  87.0 5.8 %collective-permute-start.11 = (bf16[1024,512]{1,0:T(8,128)(2,1)S(1)}, bf16[1024,512]{1,0:T(8,128)(2,1)S(1)}, u32[]{:S(2)}, u32[]{:S(2)}) collective-permute-start(bf16[1024,512]{1,0:T(8,128)(2,1)S(1)} %get-tuple-element.70), channel_id=1, source_target_pairs={{0,1},{1,0},{2,3},{3,2},{4,5},{5,4},{6,7},{7,6},{8,9},{9,8},{10,11... | collective-permute-start | bytes 3145736 | tf_op jit(solution)/shard_map/frame_rows/ppermute | solution.py:28
  87.1 2.6 %collective-permute-start.12 = (f32[1,1024]{1,0:T(1,128)S(1)}, f32[1,1024]{1,0:T(1,128)S(1)}, u32[]{:S(2)}, u32[]{:S(2)}) collective-permute-start(f32[1,1024]{1,0:T(1,128)S(1)} %slice.15), channel_id=1, source_target_pairs={{0,1},{1,0},{2,3},{3,2},{4,5},{5,4},{6,7},{7,6},{8,9},{9,8},{10,11... | collective-permute-start | bytes 12296 | tf_op jit(solution)/shard_map/frame_rows/ppermute | solution.py:28
  89.7 5.1 %collective-permute-start.13 = (f32[1,1024]{1,0:T(1,128)S(1)}, f32[1,1024]{1,0:T(1,128)S(1)}, u32[]{:S(2)}, u32[]{:S(2)}) collective-permute-start(f32[1,1024]{1,0:T(1,128)S(1)} %slice_add_fusion), channel_id=1, source_target_pairs={{0,2},{1,3},{2,0},{3,1},{4,6},{5,7},{6,4},{7,5},{8,10},{9,11},{10,... | collective-permute-start | bytes 12296 | tf_op jit(solution)/shard_map/frame_rows/ppermute | solution.py:28
  104.2 6.0 %collective-permute-start.14 = (bf16[128,512]{1,0:T(8,128)(2,1)S(1)}, bf16[128,512]{1,0:T(8,128)(2,1)S(1)}, u32[]{:S(2)}, u32[]{:S(2)}) collective-permute-start(bf16[128,512]{1,0:T(8,128)(2,1)S(1)} %sum_pieces.1.mine_ref), channel_id=1, source_target_pairs={{0,64},{4,68},{8,72},{12,76},{16,80},{20,84},{24,88},{28,92},{32,9... | collective-permute-start | bytes 393224 | tf_op jit(solution)/shard_map/token_sums/ppermute | solution.py:36
  111.8 21.4 %collective-permute-start.15 = (bf16[1024,512]{1,0:T(8,128)(2,1)S(1)}, bf16[1024,512]{1,0:T(8,128)(2,1)S(1)}, u32[]{:S(2)}, u32[]{:S(2)}) collective-permute-start(bf16[1024,512]{1,0:T(8,128)(2,1)S(1)} %add_convert_fusion.mine_ref), channel_id=1, source_target_pairs={{0,2},{1,3},{2,0},{3,1},{4,6},{5,7},{6,4},{7,5},{8,10},{9,11},{10,... | collective-permute-start | bytes 3145736 | tf_op jit(solution)/shard_map/token_gather/ppermute | solution.py:28
  115.4 31.2 %all-to-all-start.2 = ((bf16[16,128,512]{2,1,0:T(8,128)(2,1)}), bf16[16,128,512]{2,1,0:T(8,128)(2,1)}, u32[]{:S(2)}, u32[]{:S(2)}) async-start(bf16[16,128,512]{2,1,0:T(8,128)(2,1)} %finish_pieces.1), calls=%async_computation.2 | async-start | bytes 4194304 | tf_op jit(solution)/shard_map/token_gather/all_to_all | solution.py:431
  119.9 1.4 collective-permute-start.16
  134.5 2.7 %collective-permute-start.17 = (bf16[1024,512]{1,0:T(8,128)(2,1)S(1)}, bf16[1024,512]{1,0:T(8,128)(2,1)S(1)}, u32[]{:S(2)}, u32[]{:S(2)}) collective-permute-start(bf16[1024,512]{1,0:T(8,128)(2,1)S(1)} %get-tuple-element.78), channel_id=1, source_target_pairs={{0,1},{1,0},{2,3},{3,2},{4,5},{5,4},{6,7},{7,6},{8,9},{9,8},{10,11... | collective-permute-start | bytes 3145736 | tf_op jit(solution)/shard_map/frame_out/ppermute | solution.py:28
  137.2 1.0 copy-start.5

commit v5 on v4

--- a/solution.py
+++ b/solution.py
@@ -13,11 +13,11 @@
 TOK = 256
 CHUNK = 128
 SPLIT = 4
-SHARES = (2, 3, 3)
+STAGES = ((16, 2, 0, 2), (1, 4, 0, 1), (1, 4, 1, 2), (4, 4, 0, 1), (4, 4, 1, 2))
+EARLY = 4
 HELD = 4
 PAIR = 1
 EXTRA = 256
-ORDER = ((16, 2), (1, 4), (4, 4))
 VMEM_BYTES = 20 * 1024 * 1024
 VMEM = pl.BlockSpec(memory_space=pltpu.VMEM)
 SMEM = pl.BlockSpec(memory_space=pltpu.SMEM)
@@ -28,11 +28,12 @@
     return lax.ppermute(value, "tok", [(i, i ^ bit) for i in range(lax.axis_size("tok"))])
 
 
-def shift(value, stride, step, size):
+def meet(value, stride, size, later):
     pairs = []
     for i in range(lax.axis_size("ctx")):
         c = i // stride % size
-        pairs.append((i, i + ((c + step) % size - c) * stride))
+        other = c + 1 if c % 2 == later else c - 1
+        pairs.append((i, i + (other % size - c) * stride))
     return lax.ppermute(value, "ctx", pairs)
 
 
@@ -53,10 +54,6 @@
 def merge_lse(parts):
     highest = functools.reduce(jnp.maximum, parts)
     return highest + log2(sum(jnp.exp2(part - highest) for part in parts))
-
-
-def ring(value, stride, size):
-    return [value] + [shift(value, stride, step, size) for step in range(1, size)]
 
 
 def row_slice(i, size):
@@ -117,7 +114,33 @@
     lse_ref[...] = jnp.concatenate(found).T[0:1]
 
 
-def second_rows(s_ref, all_ref, tm_ref, u_ref, sum_ref, e_ref, col_ref):
+def store(e_ref, stored_ref, sems, slabs):
+    size = e_ref.shape[1] // SPLIT
+    return [
+        pltpu.make_async_copy(
+            e_ref.at[slab, pl.ds(k * size, size), :], stored_ref.at[slab, pl.ds(k * size, size), :], sems.at[n, k]
+        )
+        for n, slab in enumerate(slabs)
+        for k in range(SPLIT)
+    ]
+
+
+def during(copies):
+    @pl.when(pl.program_id(0) == 0)
+    def _():
+        for copy in copies:
+            copy.start()
+
+    def finish():
+        @pl.when(pl.program_id(0) == pl.num_programs(0) - 1)
+        def _():
+            for copy in copies:
+                copy.wait()
+
+    return finish
+
+
+def second_rows(s_ref, all_ref, tm_ref, u_ref, sum_ref, e_ref, stored_ref, col_ref, sems):
     i = pl.program_id(0)
     nt = s_ref.shape[1]
     nf = u_ref.shape[1]
@@ -135,11 +158,24 @@
         part = jnp.sum(e.reshape(CHUNK // 8, 8, W), axis=0)
         total = part if total is None else total + part
     sum_ref[:, row_slice(i, W)] = jnp.sum(total, axis=0, keepdims=True)
-
-
-def col_sums(e_ref, total_ref, fm_ref, sum_ref, alpha_ref, share_ref):
+    copies = store(e_ref, stored_ref, sems, range(EARLY))
+    for slab in range(EARLY):
+
+        @pl.when(i == slab)
+        def _(slab=slab):
+            for copy in copies[slab * SPLIT : (slab + 1) * SPLIT]:
+                copy.start()
+
+    @pl.when(i == pl.num_programs(0) - 1)
+    def _():
+        for copy in copies:
+            copy.wait()
+
+
+def col_sums(e_ref, total_ref, fm_ref, held_ref, sum_ref, alpha_ref, share_ref, stored_ref, sems):
     i = pl.program_id(0)
     nf = fm_ref.shape[1]
+    finish = during(store(e_ref, stored_ref, sems, range(EARLY, EARLY + 2)))
 
     @pl.when(i == 0)
     def _():
@@ -159,29 +195,20 @@
                 total = part if total is None else total + part
         found.append(total)
     sum_ref[...] = jnp.sum(jnp.concatenate(found).T, axis=0, keepdims=True)
-
-
-def token_parts(first, e_ref, alpha_ref, f_ref, *refs):
+    finish()
+
+
+def token_parts(first, slabs, e_ref, alpha_ref, f_ref, *refs):
     out_ref, stored_ref, sems = refs[-3:]
-    i = pl.program_id(0)
-
-    def store(step):
-        some = row_slice(first + step, TOK)
-        return pltpu.make_async_copy(e_ref.at[:, some, :], stored_ref.at[:, some, :], sems.at[step])
-
-    store(i).start()
-    rows = row_slice(first + i, TOK)
+    finish = during(store(e_ref, stored_ref, sems, slabs))
+    rows = row_slice(first + pl.program_id(0), TOK)
     acc = None
     for c in range(e_ref.shape[0]):
         p = (e_ref[c, rows, :] * alpha_ref[:, c * W : (c + 1) * W]).astype(BF16)
         part = jnp.dot(p, f_ref[c * W : (c + 1) * W, :], preferred_element_type=F32)
         acc = part if acc is None else acc + part
     out_ref[...] = acc.astype(BF16)
-
-    @pl.when(i == pl.num_programs(0) - 1)
-    def _():
-        for step in range(sems.shape[0]):
-            store(step).wait()
+    finish()
 
 
 def frame_parts(
@@ -339,9 +366,11 @@
         highest = jnp.max(parts[:, :nt], axis=0, keepdims=True)
         lse = highest + log2(jnp.sum(jnp.exp2(parts[:, :nt] - highest), axis=0, keepdims=True))
         frame_total = jnp.sum(parts[:, nt])
-    part, e = call(
-        second_rows, slabs, [VMEM, whole(1, nt), whole(1, nt), whole(1, nf)], [whole(1, nf + EXTRA), VMEM],
-        [f32(1, nf + EXTRA), kept], [pltpu.VMEM((nt, 128), F32)], input_output_aliases={0: 1}, name="second_rows",
+    part, e, stored = call(
+        second_rows, slabs, [VMEM, whole(1, nt), whole(1, nt), whole(1, nf)], [whole(1, nf + EXTRA), VMEM, hbm],
+        [f32(1, nf + EXTRA), kept, pltpu.HBM((slabs, nt, W), F32)],
+        [pltpu.VMEM((nt, 128), F32), pltpu.SemaphoreType.DMA((EARLY, SPLIT))],
+        input_output_aliases={0: 1}, name="second_rows",
     )(s, lse, tm, u)
     with jax.named_scope("rows_two"):
         part = part + swap_tok(part, 1)
@@ -352,33 +381,37 @@
         )(tokens_later)
         part = part + swap_tok(part, 2)
         part, turned = lax.optimization_barrier((part, turned))
-    part, alpha, share = call(
-        col_sums, steps, [VMEM, whole(1, nf + EXTRA), whole(1, nf)], [lanes(TOK), whole(1, nf), whole(1, nf)],
-        [f32(1, nt), f32(1, nf), f32(1, nf)], name="col_sums",
-    )(e, part, fm)
-
-    def some_token_parts(first, count, held):
+    part, alpha, share, stored = call(
+        col_sums, steps, [VMEM, whole(1, nf + EXTRA), whole(1, nf), hbm],
+        [lanes(TOK), whole(1, nf), whole(1, nf), hbm],
+        [f32(1, nt), f32(1, nf), f32(1, nf), pltpu.HBM((slabs, nt, W), F32)],
+        [pltpu.SemaphoreType.DMA((2, SPLIT))], input_output_aliases={3: 3}, name="col_sums",
+    )(e, part, fm, stored)
+
+    def some_token_parts(first, count, late, stored, held):
         return call(
-            functools.partial(token_parts, first), count, [VMEM, whole(1, nf), whole(nf, d)] + [hbm] * len(held),
+            functools.partial(token_parts, first, late), count, [VMEM, whole(1, nf), VMEM, hbm] + [hbm] * len(held),
             [pl.BlockSpec((TOK, d), lambda i: (first + i, 0)), hbm],
-            [pltpu.HBM((nt, d), BF16), pltpu.HBM((slabs, nt, W), F32)], [pltpu.SemaphoreType.DMA((count,))],
-            input_output_aliases={3 + k: k for k in range(len(held))}, name="token_parts",
-        )(e, alpha, frames, *held)
+            [pltpu.HBM((nt, d), BF16), pltpu.HBM((slabs, nt, W), F32)], [pltpu.SemaphoreType.DMA((1, SPLIT))],
+            input_output_aliases={3: 1} | {4 + k: 0 for k in range(len(held))}, name="token_parts",
+        )(e, alpha, frames, stored, *held)
 
     with jax.named_scope("cols_two"):
         held, first = [], 0
+        late = list(range(EARLY + 2, slabs))
         col_total = part
-        for (stride, size), count in zip(ORDER, SHARES):
-            held = list(some_token_parts(first, count, held))
+        for stride, size, later, count in STAGES:
+            which = [late.pop()] if late and count > 1 else []
+            token_part, stored = some_token_parts(first, count, which, stored, held)
             first += count
-            col_total = sum(ring(col_total, stride, size))
-            col_total, held[0] = lax.optimization_barrier((col_total, held[0]))
-        token_part, e = held
+            col_total = col_total + meet(col_total, stride, size, later)
+            col_total, token_part = lax.optimization_barrier((col_total, token_part))
+            held = [token_part]
     with jax.named_scope("token_scatter"):
         plane, own = 16, nt // 16
         planes = [list(range(z, z + plane)) for z in range(0, n_ctx, plane)]
         pieces = lax.all_to_all(token_part.reshape(plane, own, d), "ctx", 0, 0, axis_index_groups=planes)
-    e = pltpu.with_memory_space_constraint(e, pltpu.HBM)
+    e = pltpu.with_memory_space_constraint(stored, pltpu.HBM)
     half = slabs // 2
     base = ((1 - core) * half).reshape(1).astype(jnp.int32)
     with jax.named_scope("frame_rows"):
@@ -413,7 +446,9 @@
             [pl.BlockSpec((plane, deal, d), lambda i, k=k: (0, i * SPLIT + k, 0)) for k in range(SPLIT)],
             rows(own // 2, d), jax.ShapeDtypeStruct((own, d), BF16), name="sum_pieces",
         )(*[pieces] * SPLIT)
-        other_piece = shift(piece, 16, 1, 2)
+        other_piece = meet(piece, 16, 2, 0)
+        mine, other_piece = lax.optimization_barrier((mine, other_piece))
+        other = swap_tok(mine, 2)
 
     with jax.named_scope("token_gather"):
         col_mine = lax.dynamic_slice_in_dim(col_total, ctx % plane * own, own, axis=1)
@@ -426,8 +461,6 @@
             ],
             compiler_params=pltpu.CompilerParams(vmem_limit_bytes=VMEM_BYTES), name="finish_pieces",
         )(piece, other_piece, col_mine)
-        mine, pieces = lax.optimization_barrier((mine, pieces))
-        other = swap_tok(mine, 2)
         pieces = lax.all_to_all(pieces, "ctx", 0, 0, axis_index_groups=planes)
     with jax.named_scope("frame_sums"):
         my_sum = my_sum + other_sum

time: 150 us -> 146 us (0.973)
  starting transfers between devices: 34.1 us -> 27.9 us
    ppermute x8 -> x6, waiting for transfers between devices: 5.74 us -> 11.3 us  [meet(): return lax.ppermute(value, 'ctx', pairs)]
    ppermute x10, waiting for transfers between devices: 21.2 us -> 17.6 us  [swap_tok(): lax.ppermute(value, 'tok', [(i, i ^ bit) for i in range(lax.axis_size('to...]
    ppermute x8 -> x6, starting transfers between devices: 8.79 us -> 5.48 us  [meet(): return lax.ppermute(value, 'ctx', pairs)]
    all_to_all x1, starting transfers between devices: 5.72 us -> 3.85 us  [shards(): lax.all_to_all(token_part.reshape(plane, own, d), 'ctx', 0, 0, axis_index...]
    pallas_call x4 -> x6, Pallas kernels: 11.9 us -> 12.5 us  [the longest x5 10.3 us: some_token_parts(): call(functools.partial(token_parts, first, late), count, [VMEM, whole(1,...]
  transfers between devices with their start and end apart: 20 -> 18, of which waited for: 13 -> 15; matrix products, arithmetic and copies ran while one was open for 2% -> 2% of each run, Pallas kernels for 18% -> 20%
where the time goes in v5:
time: 146 us
  Pallas kernels  51.4 us (35%)
  waiting for transfers between devices  42.7 us (29%)
  starting transfers between devices  27.9 us (19%)
  blocking collectives  17.1 us (12%)
  other arithmetic  3.23 us (2%)
  local copies, waits for them, and re-layouts  2.25 us (2%)
    ppermute x10, waiting for transfers between devices, swap_tok(): lax.ppermute(value, 'tok', [(i, i ^ bit) for i in range(lax.axis_size('to...  17.6 us
    all_to_all x1, blocking collectives, shards(): lax.all_to_all(jnp.broadcast_to(lse[None], (n_ctx, 1, nt + 128)), 'ctx',...  17.1 us
    ppermute x10, starting transfers between devices, swap_tok(): lax.ppermute(value, 'tok', [(i, i ^ bit) for i in range(lax.axis_size('to...  14.1 us
    ppermute x6, waiting for transfers between devices, meet(): return lax.ppermute(value, 'ctx', pairs)  11.3 us
    pallas_call x1, Pallas kernels, shards(): pl.pallas_call(frame_parts, grid=(slabs,), in_specs=[SMEM, hbm, whole(1,...  11 us
    pallas_call x5, Pallas kernels, some_token_parts(): call(functools.partial(token_parts, first, late), count, [VMEM, whole(1,...  10.3 us
    pallas_call x1, Pallas kernels, shards(): call(functools.partial(first_rows, scale), slabs // PAIR, [pl.BlockSpec((...  8.55 us
    all_to_all x1, waiting for transfers between devices, shards(): lax.all_to_all(token_part.reshape(plane, own, d), 'ctx', 0, 0, axis_index...  7.41 us
  transfers between devices with their start and end apart: 18, of which 15 were waited for; matrix products, arithmetic and copies ran while one was open for 2% of the time, Pallas kernels for 20%

profile of v5, /device:TPU:0, one launch (start us, length us, event | category | flops | bytes accessed | tf_op | source)
XLA Modules:
  0.0 145.5 jit_solution(3398090930952573467)
XLA Ops:
  0.6 8.6 %first_rows.1 = (f32[1,2048]{1,0:T(1,128)S(1)}, f32[8,2048,256]{2,1,0:T(8,128)S(1)}) custom-call(bf16[2048,512]{1,0:T(8,128)(2,1)} %in_ref, bf16[2048,512]{1,0:T(8,128)(2,1)} %in_ref, bf16[2048,512]{1,0:T(8,128)(2,1)} %in_ref, bf16[2048,512]{1,0:T(8,128)(2,1)} %in_ref, bf16[2048,512]{1,0:T(8,128)(2,1)} %f_ref.9), custom_call_target="tpu_custom_call" | custom-call | tf_op jit(solution)/shard_map/first_rows/pallas_call | solution.py:351
  9.3 1.2 collective-permute-done
  10.5 4.0 %collective-permute-start.1 = (f32[1,2048]{1,0:T(1,128)S(1)}, f32[1,2048]{1,0:T(1,128)S(1)}, u32[]{:S(2)}, u32[]{:S(2)}) collective-permute-start(f32[1,2048]{1,0:T(1,128)S(1)} %multiply_add_fusion.2), channel_id=1, source_target_pairs={{0,2},{1,3},{2,0},{3,1},{4,6},{5,7},{6,4},{7,5},{8,10},{9,11},{10,... | collective-permute-start | bytes 24584 | tf_op jit(solution)/shard_map/rows_one/ppermute | solution.py:28
  14.5 1.6 %collective-permute-done.1 = f32[1,2048]{1,0:T(1,128)S(1)} collective-permute-done((f32[1,2048]{1,0:T(1,128)S(1)}, f32[1,2048]{1,0:T(1,128)S(1)}, u32[]{:S(2)}, u32[]{:S(2)}) %collective-permute-start.1) | collective-permute-done | bytes 8224 | tf_op jit(solution)/shard_map/rows_one/ppermute | solution.py:28
  16.2 4.8 %first_cols.1 = (f32[1,2048]{1,0:T(1,128)S(1)}, f32[1,2048]{1,0:T(1,128)S(1)}, f32[1,128]{1,0:T(1,128)S(1)}) custom-call(f32[8,2048,256]{2,1,0:T(8,128)S(1)} %get-tuple-element.53.s_ref, f32[1,2048]{1,0:T(1,128)S(1)} %multiply_add_fusion.1.all_ref, f32[1,2048]{1,0:T(1,128)S(1)} %bitcast.10), custom_call_target="tpu_custom_call" | custom-call | tf_op jit(solution)/shard_map/first_cols/pallas_call | solution.py:359
  21.2 17.1 %all_to_all.15 = f32[32,1,2176]{2,1,0:T(1,128)S(1)} all-to-all(f32[32,1,2176]{2,1,0:T(1,128)S(1)} %broadcast_in_dim.5), channel_id=1, replica_groups=mesh['ctx'=32,'tok'=4] {'ctx'}, dimensions={0} | all-to-all | bytes 557056 | tf_op jit(solution)/shard_map/cols_one/all_to_all | solution.py:365
  38.5 0.6 copy-done.4
  39.1 4.3 %second_rows.1 = (f32[1,2304]{1,0:T(1,128)S(1)}, f32[8,2048,256]{2,1,0:T(8,128)S(1)}, f32[8,2048,256]{2,1,0:T(8,128)}) custom-call(f32[8,2048,256]{2,1,0:T(8,128)S(1)} %get-tuple-element.53.s_ref, f32[1,2048]{1,0:T(1,128)S(1)} %bitcast.14, f32[1,2048]{1,0:T(1,128)S(1)} %bitcast.12, ...), custom_call_target="tpu_custom_call", output_to_operand_aliasing={{1}: (0, {})} | custom-call | tf_op jit(solution)/shard_map/second_rows/pallas_call | solution.py:369
  43.5 1.2 collective-permute-done.2
  44.6 3.7 %collective-permute-start.3 = (f32[1,2304]{1,0:T(1,128)S(1)}, f32[1,2304]{1,0:T(1,128)S(1)}, u32[]{:S(2)}, u32[]{:S(2)}) collective-permute-start(f32[1,2304]{1,0:T(1,128)S(1)} %add.63), channel_id=1, source_target_pairs={{0,2},{1,3},{2,0},{3,1},{4,6},{5,7},{6,4},{7,5},{8,10},{9,11},{10,... | collective-permute-start | bytes 27656 | tf_op jit(solution)/shard_map/rows_two/ppermute | solution.py:28
  48.3 2.2 %turn.1.turned_ref = bf16[512,2048]{1,0:T(8,128)(2,1)} custom-call(bf16[2048,512]{1,0:T(8,128)(2,1)S(1)} %copy-done.1), custom_call_target="tpu_custom_call" | custom-call | tf_op jit(solution)/shard_map/rows_two/turn/pallas_call | solution.py:378
  50.5 2.2 %col_sums.1 = (f32[1,2048]{1,0:T(1,128)S(1)}, f32[1,2048]{1,0:T(1,128)S(1)}, f32[1,2048]{1,0:T(1,128)S(1)}, f32[8,2048,256]{2,1,0:T(8,128)}) custom-call(f32[8,2048,256]{2,1,0:T(8,128)S(1)} %get-tuple-element.58.e_ref, f32[1,2304]{1,0:T(1,128)S(1)} %add.64.total_ref, f32[1,2048]{1,0:T(1,128)S(1)} %bitcast.11, ...), custom_call_target="tpu_custom_call", output_to_operand_aliasing={{3}: (3, {})} | custom-call | tf_op jit(solution)/shard_map/col_sums/pallas_call | solution.py:384
  53.0 0.5 copy-done
  53.5 2.6 %token_parts.5 = (bf16[2048,512]{1,0:T(8,128)(2,1)}, f32[8,2048,256]{2,1,0:T(8,128)}) custom-call(f32[8,2048,256]{2,1,0:T(8,128)S(1)} %get-tuple-element.58.e_ref, f32[1,2048]{1,0:T(1,128)S(1)} %get-tuple-element.65.alpha_ref, bf16[2048,512]{1,0:T(8,128)(2,1)S(1)} %copy-done, f32[8,2048,256]{2,1,0:T(8,128)} %get-tuple-element.66.refs_0_), custom_call_target="tpu_custom_call", output_to_operand_aliasing={{1}: (3, {})} | custom-call | tf_op jit(solution)/shard_map/cols_two/token_parts/pallas_call | solution.py:392
  56.4 0.6 collective-permute-start.5
  57.1 1.4 token_parts.6
  58.5 1.7 %collective-permute-done.5 = f32[1,2048]{1,0:T(1,128)S(1)} collective-permute-done((f32[1,2048]{1,0:T(1,128)S(1)}, f32[1,2048]{1,0:T(1,128)S(1)}, u32[]{:S(2)}, u32[]{:S(2)}) %collective-permute-start.5) | collective-permute-done | bytes 8224 | tf_op jit(solution)/shard_map/cols_two/ppermute | solution.py:37
  60.2 1.6 %collective-permute-start.6 = (f32[1,2048]{1,0:T(1,128)S(1)}, f32[1,2048]{1,0:T(1,128)S(1)}, u32[]{:S(2)}, u32[]{:S(2)}) collective-permute-start(f32[1,2048]{1,0:T(1,128)S(1)} %add.66), channel_id=1, source_target_pairs={{0,12},{4,8},{8,4},{12,0},{16,28},{20,24},{24,20},{28,16},{32,44},... | collective-permute-start | bytes 24584 | tf_op jit(solution)/shard_map/cols_two/ppermute | solution.py:37
  61.8 2.6 %token_parts.7 = (bf16[2048,512]{1,0:T(8,128)(2,1)}, f32[8,2048,256]{2,1,0:T(8,128)}) custom-call(f32[8,2048,256]{2,1,0:T(8,128)S(1)} %get-tuple-element.58.e_ref, f32[1,2048]{1,0:T(1,128)S(1)} %get-tuple-element.65.alpha_ref, bf16[2048,512]{1,0:T(8,128)(2,1)S(1)} %copy-done, ...), custom_call_target="tpu_custom_call", output_to_operand_aliasing={{1}: (3, {}), {0}: (4, {})} | custom-call | tf_op jit(solution)/shard_map/cols_two/token_parts/pallas_call | solution.py:392
  64.4 0.7 collective-permute-done.6
  65.6 1.4 token_parts.8
  67.1 1.8 %collective-permute-done.7 = f32[1,2048]{1,0:T(1,128)S(1)} collective-permute-done((f32[1,2048]{1,0:T(1,128)S(1)}, f32[1,2048]{1,0:T(1,128)S(1)}, u32[]{:S(2)}, u32[]{:S(2)}) %collective-permute-start.7) | collective-permute-done | bytes 8224 | tf_op jit(solution)/shard_map/cols_two/ppermute | solution.py:37
  68.9 1.4 collective-permute-start.8
  70.3 2.2 %token_parts.9 = (bf16[2048,512]{1,0:T(8,128)(2,1)}, f32[8,2048,256]{2,1,0:T(8,128)}) custom-call(f32[8,2048,256]{2,1,0:T(8,128)S(1)} %get-tuple-element.58.e_ref, f32[1,2048]{1,0:T(1,128)S(1)} %get-tuple-element.65.alpha_ref, bf16[2048,512]{1,0:T(8,128)(2,1)S(1)} %copy-done, ...), custom_call_target="tpu_custom_call", output_to_operand_aliasing={{1}: (3, {}), {0}: (4, {})} | custom-call | tf_op jit(solution)/shard_map/cols_two/token_parts/pallas_call | solution.py:392
  72.4 1.4 collective-permute-done.8
  73.8 3.9 %all-to-all-start.1 = ((bf16[16,128,512]{2,1,0:T(8,128)(2,1)}), bf16[16,128,512]{2,1,0:T(8,128)(2,1)S(1)}, u32[]{:S(2)}, u32[]{:S(2)}) async-start(bf16[16,128,512]{2,1,0:T(8,128)(2,1)} %bitcast.15), calls=%async_computation.1 | async-start | bytes 4194304 | tf_op jit(solution)/shard_map/token_scatter/all_to_all | solution.py:413
  77.7 11.0 %frame_parts.1 = (f32[1,2048]{1,0:T(1,128)S(1)}, bf16[1024,512]{1,0:T(8,128)(2,1)S(1)}, bf16[1024,512]{1,0:T(8,128)(2,1)S(1)}) custom-call(s32[1]{0:T(128)} %bitcast.4.base_ref, f32[8,2048,256]{2,1,0:T(8,128)} %get-tuple-element.85.e_ref, f32[1,2048]{1,0:T(1,128)S(1)} %add.69.total_ref, f32[1,2048]{1,0:T(1,128)S(1)} %bitcast.13, ...), custom_call_target="tpu_custom_call" | custom-call | tf_op jit(solution)/shard_map/frame_rows/frame_parts/pallas_call | solution.py:418
  88.8 0.5 collective-permute-start.10
  89.3 2.2 %collective-permute-done.10 = f32[1,1024]{1,0:T(1,128)S(1)} collective-permute-done((f32[1,1024]{1,0:T(1,128)S(1)}, f32[1,1024]{1,0:T(1,128)S(1)}, u32[]{:S(2)}, u32[]{:S(2)}) %collective-permute-start.10) | collective-permute-done | bytes 4128 | tf_op jit(solution)/shard_map/frame_rows/ppermute | solution.py:28
  91.5 3.0 %collective-permute-start.11 = (f32[1,1024]{1,0:T(1,128)S(1)}, f32[1,1024]{1,0:T(1,128)S(1)}, u32[]{:S(2)}, u32[]{:S(2)}) collective-permute-start(f32[1,1024]{1,0:T(1,128)S(1)} %slice_add_fusion), channel_id=1, source_target_pairs={{0,2},{1,3},{2,0},{3,1},{4,6},{5,7},{6,4},{7,5},{8,10},{9,11},{10,... | collective-permute-start | bytes 12296 | tf_op jit(solution)/shard_map/frame_rows/ppermute | solution.py:28
  94.8 1.8 %collective-permute-done.11 = f32[1,1024]{1,0:T(1,128)S(1)} collective-permute-done((f32[1,1024]{1,0:T(1,128)S(1)}, f32[1,1024]{1,0:T(1,128)S(1)}, u32[]{:S(2)}, u32[]{:S(2)}) %collective-permute-start.11) | collective-permute-done | bytes 4128 | tf_op jit(solution)/shard_map/frame_rows/ppermute | solution.py:28
  96.6 7.4 %all-to-all-done.1.refs_0_.refs_1_.refs_2_.refs_3_ = bf16[16,128,512]{2,1,0:T(8,128)(2,1)S(1)} async-done(((bf16[16,128,512]{2,1,0:T(8,128)(2,1)}), bf16[16,128,512]{2,1,0:T(8,128)(2,1)S(1)}, u32[]{:S(2)}, u32[]{:S(2)}) %all-to-all-start.1) | async-done | bytes 2097184 | tf_op jit(solution)/shard_map/token_scatter/all_to_all | solution.py:413
  104.0 0.5 sum_pieces.1.mine_ref
  104.5 1.1 collective-permute-start.12
  105.6 5.4 %collective-permute-done.12.other_ref = bf16[128,512]{1,0:T(8,128)(2,1)S(1)} collective-permute-done((bf16[128,512]{1,0:T(8,128)(2,1)S(1)}, bf16[128,512]{1,0:T(8,128)(2,1)S(1)}, u32[]{:S(2)}, u32[]{:S(2)}) %collective-permute-start.12) | collective-permute-done | bytes 131104 | tf_op jit(solution)/shard_map/token_sums/ppermute | solution.py:37
  111.0 2.5 %collective-permute-start.13 = (bf16[1024,512]{1,0:T(8,128)(2,1)S(1)}, bf16[1024,512]{1,0:T(8,128)(2,1)S(1)}, u32[]{:S(2)}, u32[]{:S(2)}) collective-permute-start(bf16[1024,512]{1,0:T(8,128)(2,1)S(1)} %add_convert_fusion.mine_ref), channel_id=1, source_target_pairs={{0,2},{1,3},{2,0},{3,1},{4,6},{5,7},{6,4},{7,5},{8,10},{9,11},{10,... | collective-permute-start | bytes 3145736 | tf_op jit(solution)/shard_map/token_sums/ppermute | solution.py:28
  113.5 1.5 %finish_pieces.1 = bf16[16,128,512]{2,1,0:T(8,128)(2,1)} custom-call(bf16[128,512]{1,0:T(8,128)(2,1)S(1)} %sum_pieces.1.mine_ref, bf16[128,512]{1,0:T(8,128)(2,1)S(1)} %collective-permute-done.12.other_ref, f32[1,128]{1,0:T(1,128)S(1)} %constant_dynamic-slice_fusion.total_ref), custom_call_target="tpu_custom_call" | custom-call | tf_op jit(solution)/shard_map/token_gather/finish_pieces/pallas_call | solution.py:455
  115.1 4.5 %all-to-all-start.2 = ((bf16[16,128,512]{2,1,0:T(8,128)(2,1)}), bf16[16,128,512]{2,1,0:T(8,128)(2,1)}, u32[]{:S(2)}, u32[]{:S(2)}) async-start(bf16[16,128,512]{2,1,0:T(8,128)(2,1)} %finish_pieces.1), calls=%async_computation.2 | async-start | bytes 4194304 | tf_op jit(solution)/shard_map/token_gather/all_to_all | solution.py:464
  119.7 1.3 slice_reduce_fusion.1
  121.0 0.7 maximum_multiply_fusion
  121.7 0.6 div.8
  122.3 7.0 %collective-permute-done.13.other_ref = bf16[1024,512]{1,0:T(8,128)(2,1)S(1)} collective-permute-done((bf16[1024,512]{1,0:T(8,128)(2,1)S(1)}, bf16[1024,512]{1,0:T(8,128)(2,1)S(1)}, u32[]{:S(2)}, u32[]{:S(2)}) %collective-permute-start.13) | collective-permute-done | bytes 1048608 | tf_op jit(solution)/shard_map/token_sums/ppermute | solution.py:28
  129.3 1.3 finish_frames.1
  130.7 2.6 %collective-permute-done.15.theirs_ref = bf16[1024,512]{1,0:T(8,128)(2,1)S(1)} collective-permute-done((bf16[1024,512]{1,0:T(8,128)(2,1)S(1)}, bf16[1024,512]{1,0:T(8,128)(2,1)S(1)}, u32[]{:S(2)}, u32[]{:S(2)}) %collective-permute-start.15) | collective-permute-done | bytes 1048608 | tf_op jit(solution)/shard_map/frame_out/ppermute | solution.py:28
  133.3 1.0 copy-done.5
  134.3 2.2 %place_frames.1 = bf16[2048,512]{1,0:T(8,128)(2,1)} custom-call(s32[1]{0:T(128)} %bitcast.5.core_ref, bf16[1024,512]{1,0:T(8,128)(2,1)} %copy-done.5, bf16[2048,512]{1,0:T(8,128)(2,1)} %get-tuple-element.99.half_ref), custom_call_target="tpu_custom_call", output_to_operand_aliasing={{}: (2, {})} | custom-call | tf_op jit(solution)/shard_map/frame_out/place_frames/pallas_call | solution.py:481
  136.5 6.4 %all-to-all-done.2.pieces_ref = bf16[16,128,512]{2,1,0:T(8,128)(2,1)} async-done(((bf16[16,128,512]{2,1,0:T(8,128)(2,1)}), bf16[16,128,512]{2,1,0:T(8,128)(2,1)}, u32[]{:S(2)}, u32[]{:S(2)}) %all-to-all-start.2) | async-done | bytes 2097184 | tf_op jit(solution)/shard_map/token_gather/all_to_all | solution.py:464
  142.9 2.6 %place_tokens.1 = bf16[2048,512]{1,0:T(8,128)(2,1)} custom-call(bf16[16,128,512]{2,1,0:T(8,128)(2,1)} %all-to-all-done.2.pieces_ref), custom_call_target="tpu_custom_call" | custom-call | tf_op jit(solution)/shard_map/frame_out/place_tokens/pallas_call | solution.py:486
  (41 shorter events, 2.3 us)
Async XLA Ops:
  0.6 15.6 %copy-start.2 = (f32[2048]{0:T(1024)S(1)}, f32[2048]{0:T(1024)}, u32[]{:S(2)}) copy-start(f32[2048]{0:T(1024)} %param.6) | copy-start | bytes 24580
  9.2 1.3 collective-permute-start
  10.5 5.7 %collective-permute-start.1 = (f32[1,2048]{1,0:T(1,128)S(1)}, f32[1,2048]{1,0:T(1,128)S(1)}, u32[]{:S(2)}, u32[]{:S(2)}) collective-permute-start(f32[1,2048]{1,0:T(1,128)S(1)} %multiply_add_fusion.2), channel_id=1, source_target_pairs={{0,2},{1,3},{2,0},{3,1},{4,6},{5,7},{6,4},{7,5},{8,10},{9,11},{10,... | collective-permute-start | bytes 24584 | tf_op jit(solution)/shard_map/rows_one/ppermute | solution.py:28
  16.2 22.8 %copy-start.3 = (f32[2048]{0:T(1024)S(1)}, f32[2048]{0:T(1024)}, u32[]{:S(2)}) copy-start(f32[2048]{0:T(1024)} %param.7) | copy-start | bytes 24580
  38.4 0.7 copy-start.4
  39.1 9.2 %copy-start.1 = (bf16[2048,512]{1,0:T(8,128)(2,1)S(1)}, bf16[2048,512]{1,0:T(8,128)(2,1)}, u32[]{:S(2)}) copy-start(bf16[2048,512]{1,0:T(8,128)(2,1)} %in_ref) | copy-start | bytes 6291460
  43.4 1.3 collective-permute-start.2
  44.6 5.8 %collective-permute-start.3 = (f32[1,2304]{1,0:T(1,128)S(1)}, f32[1,2304]{1,0:T(1,128)S(1)}, u32[]{:S(2)}, u32[]{:S(2)}) collective-permute-start(f32[1,2304]{1,0:T(1,128)S(1)} %add.63), channel_id=1, source_target_pairs={{0,2},{1,3},{2,0},{3,1},{4,6},{5,7},{6,4},{7,5},{8,10},{9,11},{10,... | collective-permute-start | bytes 27656 | tf_op jit(solution)/shard_map/rows_two/ppermute | solution.py:28
  50.5 3.1 %copy-start = (bf16[2048,512]{1,0:T(8,128)(2,1)S(1)}, bf16[2048,512]{1,0:T(8,128)(2,1)}, u32[]{:S(2)}) copy-start(bf16[2048,512]{1,0:T(8,128)(2,1)} %f_ref.9) | copy-start | bytes 6291460
  52.7 3.7 %collective-permute-start.4 = (f32[1,2048]{1,0:T(1,128)S(1)}, f32[1,2048]{1,0:T(1,128)S(1)}, u32[]{:S(2)}, u32[]{:S(2)}) collective-permute-start(f32[1,2048]{1,0:T(1,128)S(1)} %get-tuple-element.64), channel_id=1, source_target_pairs={{0,64},{4,68},{8,72},{12,76},{16,80},{20,84},{24,88},{28,92},{32,9... | collective-permute-start | bytes 24584 | tf_op jit(solution)/shard_map/cols_two/ppermute | solution.py:37
  56.4 3.7 %collective-permute-start.5 = (f32[1,2048]{1,0:T(1,128)S(1)}, f32[1,2048]{1,0:T(1,128)S(1)}, u32[]{:S(2)}, u32[]{:S(2)}) collective-permute-start(f32[1,2048]{1,0:T(1,128)S(1)} %add.65), channel_id=1, source_target_pairs={{0,4},{4,0},{8,12},{12,8},{16,20},{20,16},{24,28},{28,24},{32,36},... | collective-permute-start | bytes 24584 | tf_op jit(solution)/shard_map/cols_two/ppermute | solution.py:37
  60.2 4.9 %collective-permute-start.6 = (f32[1,2048]{1,0:T(1,128)S(1)}, f32[1,2048]{1,0:T(1,128)S(1)}, u32[]{:S(2)}, u32[]{:S(2)}) collective-permute-start(f32[1,2048]{1,0:T(1,128)S(1)} %add.66), channel_id=1, source_target_pairs={{0,12},{4,8},{8,4},{12,0},{16,28},{20,24},{24,20},{28,16},{32,44},... | collective-permute-start | bytes 24584 | tf_op jit(solution)/shard_map/cols_two/ppermute | solution.py:37
  65.1 3.7 %collective-permute-start.7 = (f32[1,2048]{1,0:T(1,128)S(1)}, f32[1,2048]{1,0:T(1,128)S(1)}, u32[]{:S(2)}, u32[]{:S(2)}) collective-permute-start(f32[1,2048]{1,0:T(1,128)S(1)} %add.67), channel_id=1, source_target_pairs={{0,16},{4,20},{8,24},{12,28},{16,0},{20,4},{24,8},{28,12},{32,48},... | collective-permute-start | bytes 24584 | tf_op jit(solution)/shard_map/cols_two/ppermute | solution.py:37
  68.9 4.9 %collective-permute-start.8 = (f32[1,2048]{1,0:T(1,128)S(1)}, f32[1,2048]{1,0:T(1,128)S(1)}, u32[]{:S(2)}, u32[]{:S(2)}) collective-permute-start(f32[1,2048]{1,0:T(1,128)S(1)} %add.68), channel_id=1, source_target_pairs={{0,48},{4,52},{8,56},{12,60},{16,32},{20,36},{24,40},{28,44},{32,1... | collective-permute-start | bytes 24584 | tf_op jit(solution)/shard_map/cols_two/ppermute | solution.py:37
  73.8 30.2 %all-to-all-start.1 = ((bf16[16,128,512]{2,1,0:T(8,128)(2,1)}), bf16[16,128,512]{2,1,0:T(8,128)(2,1)S(1)}, u32[]{:S(2)}, u32[]{:S(2)}) async-start(bf16[16,128,512]{2,1,0:T(8,128)(2,1)} %bitcast.15), calls=%async_computation.1 | async-start | bytes 4194304 | tf_op jit(solution)/shard_map/token_scatter/all_to_all | solution.py:413
  88.7 5.8 %collective-permute-start.9 = (bf16[1024,512]{1,0:T(8,128)(2,1)S(1)}, bf16[1024,512]{1,0:T(8,128)(2,1)S(1)}, u32[]{:S(2)}, u32[]{:S(2)}) collective-permute-start(bf16[1024,512]{1,0:T(8,128)(2,1)S(1)} %get-tuple-element.90), channel_id=1, source_target_pairs={{0,1},{1,0},{2,3},{3,2},{4,5},{5,4},{6,7},{7,6},{8,9},{9,8},{10,11... | collective-permute-start | bytes 3145736 | tf_op jit(solution)/shard_map/frame_rows/ppermute | solution.py:28
  88.8 2.6 %collective-permute-start.10 = (f32[1,1024]{1,0:T(1,128)S(1)}, f32[1,1024]{1,0:T(1,128)S(1)}, u32[]{:S(2)}, u32[]{:S(2)}) collective-permute-start(f32[1,1024]{1,0:T(1,128)S(1)} %slice.15), channel_id=1, source_target_pairs={{0,1},{1,0},{2,3},{3,2},{4,5},{5,4},{6,7},{7,6},{8,9},{9,8},{10,11... | collective-permute-start | bytes 12296 | tf_op jit(solution)/shard_map/frame_rows/ppermute | solution.py:28
  91.5 5.1 %collective-permute-start.11 = (f32[1,1024]{1,0:T(1,128)S(1)}, f32[1,1024]{1,0:T(1,128)S(1)}, u32[]{:S(2)}, u32[]{:S(2)}) collective-permute-start(f32[1,1024]{1,0:T(1,128)S(1)} %slice_add_fusion), channel_id=1, source_target_pairs={{0,2},{1,3},{2,0},{3,1},{4,6},{5,7},{6,4},{7,5},{8,10},{9,11},{10,... | collective-permute-start | bytes 12296 | tf_op jit(solution)/shard_map/frame_rows/ppermute | solution.py:28
  104.5 6.5 %collective-permute-start.12 = (bf16[128,512]{1,0:T(8,128)(2,1)S(1)}, bf16[128,512]{1,0:T(8,128)(2,1)S(1)}, u32[]{:S(2)}, u32[]{:S(2)}) collective-permute-start(bf16[128,512]{1,0:T(8,128)(2,1)S(1)} %sum_pieces.1.mine_ref), channel_id=1, source_target_pairs={{0,64},{4,68},{8,72},{12,76},{16,80},{20,84},{24,88},{28,92},{32,9... | collective-permute-start | bytes 393224 | tf_op jit(solution)/shard_map/token_sums/ppermute | solution.py:37
  111.0 18.3 %collective-permute-start.13 = (bf16[1024,512]{1,0:T(8,128)(2,1)S(1)}, bf16[1024,512]{1,0:T(8,128)(2,1)S(1)}, u32[]{:S(2)}, u32[]{:S(2)}) collective-permute-start(bf16[1024,512]{1,0:T(8,128)(2,1)S(1)} %add_convert_fusion.mine_ref), channel_id=1, source_target_pairs={{0,2},{1,3},{2,0},{3,1},{4,6},{5,7},{6,4},{7,5},{8,10},{9,11},{10,... | collective-permute-start | bytes 3145736 | tf_op jit(solution)/shard_map/token_sums/ppermute | solution.py:28
  115.1 27.9 %all-to-all-start.2 = ((bf16[16,128,512]{2,1,0:T(8,128)(2,1)}), bf16[16,128,512]{2,1,0:T(8,128)(2,1)}, u32[]{:S(2)}, u32[]{:S(2)}) async-start(bf16[16,128,512]{2,1,0:T(8,128)(2,1)} %finish_pieces.1), calls=%async_computation.2 | async-start | bytes 4194304 | tf_op jit(solution)/shard_map/token_gather/all_to_all | solution.py:464
  119.6 1.4 collective-permute-start.14
  130.6 2.7 %collective-permute-start.15 = (bf16[1024,512]{1,0:T(8,128)(2,1)S(1)}, bf16[1024,512]{1,0:T(8,128)(2,1)S(1)}, u32[]{:S(2)}, u32[]{:S(2)}) collective-permute-start(bf16[1024,512]{1,0:T(8,128)(2,1)S(1)} %get-tuple-element.98), channel_id=1, source_target_pairs={{0,1},{1,0},{2,3},{3,2},{4,5},{5,4},{6,7},{7,6},{8,9},{9,8},{10,11... | collective-permute-start | bytes 3145736 | tf_op jit(solution)/shard_map/frame_out/ppermute | solution.py:28
  133.3 1.0 copy-start.5

commit v6 on v5

--- a/solution.py
+++ b/solution.py
@@ -252,21 +252,24 @@
 
 
 def sum_pieces(*refs):
-    out_ref = refs[-1]
-    rows = refs[0].shape[1]
-    for k, pieces_ref in enumerate(refs[:-1]):
+    total_ref, out_ref, col_ref = refs[-3:]
+    column(total_ref[...], col_ref)
+    rows, d = refs[0].shape[1:]
+    for k, pieces_ref in enumerate(refs[:-3]):
         acc = pieces_ref[0].astype(F32)
         for n in range(1, pieces_ref.shape[0]):
             acc = acc + pieces_ref[n].astype(F32)
-        out_ref[k * rows : (k + 1) * rows, :] = acc.astype(BF16)
-
-
-def finish_pieces(mine_ref, other_ref, total_ref, out_ref, col_ref, done_ref, sems):
-    column(total_ref[...], col_ref)
-    d = mine_ref.shape[1]
-    done = (mine_ref[...].astype(F32) + other_ref[...].astype(F32)) / wide(col_ref[...], d)
-    done_ref[...] = done.astype(BF16)
-    copies = [pltpu.make_async_copy(done_ref, out_ref.at[k], sems.at[k]) for k in range(out_ref.shape[0])]
+        some = slice(k * rows, (k + 1) * rows)
+        out_ref[some, :] = (acc / wide(col_ref[some, :], d)).astype(BF16)
+
+
+def deal_pieces(plane_ref, mine_ref, other_ref, out_ref, sems):
+    rows = mine_ref.shape[0]
+    copies = [
+        pltpu.make_async_copy(ref, out_ref.at[k, row_slice(which, rows), :], sems.at[k, n])
+        for k in range(out_ref.shape[0])
+        for n, (ref, which) in enumerate(((mine_ref, plane_ref[0]), (other_ref, 1 - plane_ref[0])))
+    ]
     for copy in copies:
         copy.start()
     for copy in copies:
@@ -276,15 +279,22 @@
 def place_tokens(pieces_ref, out_ref, held_ref, sems, out_sems):
     count, rows = pieces_ref.shape[0], pieces_ref.shape[1]
     ins = [pltpu.make_async_copy(pieces_ref.at[k], held_ref.at[k], sems.at[k]) for k in range(count)]
+    half, piece = out_ref.shape[0] // 2, rows // 2
     outs = [
-        pltpu.make_async_copy(held_ref.at[k], out_ref.at[k * rows : (k + 1) * rows, :], out_sems.at[k])
+        pltpu.make_async_copy(
+            held_ref.at[k, pl.ds(n * piece, piece), :],
+            out_ref.at[pl.ds(n * half + k * piece, piece), :],
+            out_sems.at[k, n],
+        )
         for k in range(count)
+        for n in range(2)
     ]
     for copy in ins:
         copy.start()
     for k in range(count):
         ins[k].wait()
-        outs[k].start()
+        outs[2 * k].start()
+        outs[2 * k + 1].start()
     for copy in outs:
         copy.wait()
 
@@ -297,13 +307,6 @@
         done = (mine_ref[some, :].astype(F32) + other_ref[some, :].astype(F32)) / wide(col_ref[some, :], d)
         out_ref[some, :] = done.astype(BF16)
     copy = pltpu.make_async_copy(out_ref, map_ref.at[row_slice(core_ref[0], rows), :], sem)
-    copy.start()
-    copy.wait()
-
-
-def place_frames(core_ref, theirs_ref, half_ref, map_ref, sem):
-    rows = theirs_ref.shape[0]
-    copy = pltpu.make_async_copy(theirs_ref, map_ref.at[row_slice(1 - core_ref[0], rows), :], sem)
     copy.start()
     copy.wait()
 
@@ -408,9 +411,10 @@
             col_total, token_part = lax.optimization_barrier((col_total, token_part))
             held = [token_part]
     with jax.named_scope("token_scatter"):
-        plane, own = 16, nt // 16
+        plane, own = 16, nt // n_ctx
         planes = [list(range(z, z + plane)) for z in range(0, n_ctx, plane)]
-        pieces = lax.all_to_all(token_part.reshape(plane, own, d), "ctx", 0, 0, axis_index_groups=planes)
+        pieces = lax.all_to_all(token_part.reshape(n_ctx, own, d), "ctx", 0, 0)
+
     e = pltpu.with_memory_space_constraint(stored, pltpu.HBM)
     half = slabs // 2
     base = ((1 - core) * half).reshape(1).astype(jnp.int32)
@@ -439,28 +443,23 @@
         other_sum = swap_tok(my_sum, 2)
         mine = (mine.astype(F32) + swap_tok(theirs, 1).astype(F32)).astype(BF16)
     with jax.named_scope("token_sums"):
-        pieces, mine, other_sum = lax.optimization_barrier((pieces, mine, other_sum))
-        deal = own // (2 * SPLIT)
+        pieces, mine = lax.optimization_barrier((pieces, mine))
+        col_mine = lax.dynamic_slice_in_dim(col_total, ctx * own, own, axis=1)
+        deal = own // SPLIT
         piece = call(
-            sum_pieces, 2,
-            [pl.BlockSpec((plane, deal, d), lambda i, k=k: (0, i * SPLIT + k, 0)) for k in range(SPLIT)],
-            rows(own // 2, d), jax.ShapeDtypeStruct((own, d), BF16), name="sum_pieces",
-        )(*[pieces] * SPLIT)
+            sum_pieces, 1,
+            [pl.BlockSpec((n_ctx, deal, d), lambda i, k=k: (0, k, 0)) for k in range(SPLIT)] + [whole(1, 128)],
+            rows(own, d), jax.ShapeDtypeStruct((own, d), BF16), [pltpu.VMEM((128, 128), F32)], name="sum_pieces",
+        )(*[pieces] * SPLIT, jnp.pad(col_mine, ((0, 0), (0, 128 - own)), constant_values=1.0))
         other_piece = meet(piece, 16, 2, 0)
         mine, other_piece = lax.optimization_barrier((mine, other_piece))
         other = swap_tok(mine, 2)
-
     with jax.named_scope("token_gather"):
-        col_mine = lax.dynamic_slice_in_dim(col_total, ctx % plane * own, own, axis=1)
         pieces = pl.pallas_call(
-            finish_pieces, in_specs=[VMEM] * 3, out_specs=hbm, out_shape=pltpu.HBM((plane, own, d), BF16),
-            scratch_shapes=[
-                pltpu.VMEM((own, 128), F32),
-                pltpu.VMEM((own, d), BF16),
-                pltpu.SemaphoreType.DMA((plane,)),
-            ],
-            compiler_params=pltpu.CompilerParams(vmem_limit_bytes=VMEM_BYTES), name="finish_pieces",
-        )(piece, other_piece, col_mine)
+            deal_pieces, in_specs=[SMEM] + [VMEM] * 2, out_specs=hbm, out_shape=pltpu.HBM((plane, 2 * own, d), BF16),
+            scratch_shapes=[pltpu.SemaphoreType.DMA((plane, 2))],
+            compiler_params=pltpu.CompilerParams(vmem_limit_bytes=VMEM_BYTES), name="deal_pieces",
+        )((ctx // plane).reshape(1).astype(jnp.int32), piece, other_piece)
         pieces = lax.all_to_all(pieces, "ctx", 0, 0, axis_index_groups=planes)
     with jax.named_scope("frame_sums"):
         my_sum = my_sum + other_sum
@@ -469,7 +468,6 @@
         high = jnp.where(core == 0, their_sum, my_sum)
         row_sum = jnp.concatenate([low, high], axis=1)[0]
         mass_ratio = row_sum / (frame_mass / frame_total)
-        other, mass_ratio = lax.optimization_barrier((other, mass_ratio))
     with jax.named_scope("frame_out"):
         which = core.reshape(1).astype(jnp.int32)
         mine, frame_map = pl.pallas_call(
@@ -478,17 +476,14 @@
             scratch_shapes=[pltpu.VMEM((nf // 2, 128), F32), pltpu.SemaphoreType.DMA],
             compiler_params=pltpu.CompilerParams(vmem_limit_bytes=VMEM_BYTES), name="finish_frames",
         )(which, mine, other, my_sum)
-        frame_map = pl.pallas_call(
-            place_frames, in_specs=[SMEM, VMEM, hbm], out_specs=hbm, out_shape=pltpu.HBM((nf, d), BF16),
-            scratch_shapes=[pltpu.SemaphoreType.DMA], input_output_aliases={2: 0}, name="place_frames",
-        )(which, swap_tok(mine, 1), frame_map)
+        frame_map = lax.dynamic_update_slice_in_dim(frame_map, swap_tok(mine, 1), (1 - core) * (nf // 2), 0)
         pieces, frame_map = lax.optimization_barrier((pieces, frame_map))
         token_map = pl.pallas_call(
             place_tokens, in_specs=[hbm], out_specs=hbm, out_shape=pltpu.HBM((nt, d), BF16),
             scratch_shapes=[
-                pltpu.VMEM((plane, own, d), BF16),
+                pltpu.VMEM((plane, 2 * own, d), BF16),
                 pltpu.SemaphoreType.DMA((plane,)),
-                pltpu.SemaphoreType.DMA((plane,)),
+                pltpu.SemaphoreType.DMA((plane, 2)),
             ],
             compiler_params=pltpu.CompilerParams(vmem_limit_bytes=VMEM_BYTES), name="place_tokens",
         )(pltpu.with_memory_space_constraint(pieces, pltpu.HBM))

time: 146 us -> 144 us (0.986)
  Pallas kernels: 51.4 us -> 49.1 us
    ppermute x10, waiting for transfers between devices: 17.6 us -> 20.7 us  [swap_tok(): lax.ppermute(value, 'tok', [(i, i ^ bit) for i in range(lax.axis_size('to...]
    pallas_call x3 -> x2, Pallas kernels: 4.25 us -> 1.84 us  [the longest x1 1.57 us: shards(): pl.pallas_call(deal_pieces, in_specs=[SMEM] + [VMEM] * 2, out_specs=hbm,...]
    ppermute x10, starting transfers between devices: 14.1 us -> 12 us  [swap_tok(): lax.ppermute(value, 'tok', [(i, i ^ bit) for i in range(lax.axis_size('to...]
    ppermute x6, waiting for transfers between devices: 11.3 us -> 9.29 us  [meet(): return lax.ppermute(value, 'ctx', pairs)]
    convert_element_type x1, other arithmetic: 0.3 us -> 1.82 us  [shards(): mine = (mine.astype(F32) + swap_tok(theirs, 1).astype(F32)).astype(BF16)]
  transfers between devices with their start and end apart: 18 -> 18, of which waited for: 15 -> 15; matrix products, arithmetic and copies ran while one was open for 2% -> 3% of each run, Pallas kernels for 20% -> 18%
where the time goes in v6:
time: 144 us
  Pallas kernels  49.1 us (34%)
  waiting for transfers between devices  42.8 us (30%)
  starting transfers between devices  27.1 us (19%)
  blocking collectives  17.1 us (12%)
  other arithmetic  4.03 us (3%)
  local copies, waits for them, and re-layouts  2.78 us (2%)
    ppermute x10, waiting for transfers between devices, swap_tok(): lax.ppermute(value, 'tok', [(i, i ^ bit) for i in range(lax.axis_size('to...  20.7 us
    all_to_all x1, blocking collectives, shards(): lax.all_to_all(jnp.broadcast_to(lse[None], (n_ctx, 1, nt + 128)), 'ctx',...  17.1 us
    ppermute x10, starting transfers between devices, swap_tok(): lax.ppermute(value, 'tok', [(i, i ^ bit) for i in range(lax.axis_size('to...  12 us
    pallas_call x1, Pallas kernels, shards(): pl.pallas_call(frame_parts, grid=(slabs,), in_specs=[SMEM, hbm, whole(1,...  11 us
    pallas_call x5, Pallas kernels, some_token_parts(): call(functools.partial(token_parts, first, late), count, [VMEM, whole(1,...  10.3 us
    ppermute x6, waiting for transfers between devices, meet(): return lax.ppermute(value, 'ctx', pairs)  9.29 us
    pallas_call x1, Pallas kernels, shards(): call(functools.partial(first_rows, scale), slabs // PAIR, [pl.BlockSpec((...  8.55 us
    all_to_all x1, waiting for transfers between devices, shards(): pieces = lax.all_to_all(token_part.reshape(n_ctx, own, d), 'ctx', 0, 0)  6.93 us
  transfers between devices with their start and end apart: 18, of which 15 were waited for; matrix products, arithmetic and copies ran while one was open for 3% of the time, Pallas kernels for 18%

profile of v6, /device:TPU:0, one launch (start us, length us, event | category | flops | bytes accessed | tf_op | source)
XLA Modules:
  0.0 143.8 jit_solution(15389819266964426897)
XLA Ops:
  0.6 8.6 %first_rows.1 = (f32[1,2048]{1,0:T(1,128)S(1)}, f32[8,2048,256]{2,1,0:T(8,128)S(1)}) custom-call(bf16[2048,512]{1,0:T(8,128)(2,1)} %in_ref, bf16[2048,512]{1,0:T(8,128)(2,1)} %in_ref, bf16[2048,512]{1,0:T(8,128)(2,1)} %in_ref, bf16[2048,512]{1,0:T(8,128)(2,1)} %in_ref, bf16[2048,512]{1,0:T(8,128)(2,1)} %f_ref.9), custom_call_target="tpu_custom_call" | custom-call | tf_op jit(solution)/shard_map/first_rows/pallas_call | solution.py:354
  9.3 1.2 collective-permute-done
  10.5 4.0 %collective-permute-start.1 = (f32[1,2048]{1,0:T(1,128)S(1)}, f32[1,2048]{1,0:T(1,128)S(1)}, u32[]{:S(2)}, u32[]{:S(2)}) collective-permute-start(f32[1,2048]{1,0:T(1,128)S(1)} %multiply_add_fusion.2), channel_id=1, source_target_pairs={{0,2},{1,3},{2,0},{3,1},{4,6},{5,7},{6,4},{7,5},{8,10},{9,11},{10,... | collective-permute-start | bytes 24584 | tf_op jit(solution)/shard_map/rows_one/ppermute | solution.py:28
  14.5 1.6 %collective-permute-done.1 = f32[1,2048]{1,0:T(1,128)S(1)} collective-permute-done((f32[1,2048]{1,0:T(1,128)S(1)}, f32[1,2048]{1,0:T(1,128)S(1)}, u32[]{:S(2)}, u32[]{:S(2)}) %collective-permute-start.1) | collective-permute-done | bytes 8224 | tf_op jit(solution)/shard_map/rows_one/ppermute | solution.py:28
  16.2 4.8 %first_cols.1 = (f32[1,2048]{1,0:T(1,128)S(1)}, f32[1,2048]{1,0:T(1,128)S(1)}, f32[1,128]{1,0:T(1,128)S(1)}) custom-call(f32[8,2048,256]{2,1,0:T(8,128)S(1)} %get-tuple-element.50.s_ref, f32[1,2048]{1,0:T(1,128)S(1)} %multiply_add_fusion.1.all_ref, f32[1,2048]{1,0:T(1,128)S(1)} %bitcast.11), custom_call_target="tpu_custom_call" | custom-call | tf_op jit(solution)/shard_map/first_cols/pallas_call | solution.py:362
  21.2 17.1 %all_to_all.15 = f32[32,1,2176]{2,1,0:T(1,128)S(1)} all-to-all(f32[32,1,2176]{2,1,0:T(1,128)S(1)} %broadcast_in_dim.5), channel_id=1, replica_groups=mesh['ctx'=32,'tok'=4] {'ctx'}, dimensions={0} | all-to-all | bytes 557056 | tf_op jit(solution)/shard_map/cols_one/all_to_all | solution.py:368
  38.5 4.3 %second_rows.1 = (f32[1,2304]{1,0:T(1,128)S(1)}, f32[8,2048,256]{2,1,0:T(8,128)S(1)}, f32[8,2048,256]{2,1,0:T(8,128)}) custom-call(f32[8,2048,256]{2,1,0:T(8,128)S(1)} %get-tuple-element.50.s_ref, f32[1,2048]{1,0:T(1,128)S(1)} %bitcast.15, f32[1,2048]{1,0:T(1,128)S(1)} %bitcast.13, ...), custom_call_target="tpu_custom_call", output_to_operand_aliasing={{1}: (0, {})} | custom-call | tf_op jit(solution)/shard_map/second_rows/pallas_call | solution.py:372
  42.9 1.2 collective-permute-done.2
  44.1 3.7 %collective-permute-start.3 = (f32[1,2304]{1,0:T(1,128)S(1)}, f32[1,2304]{1,0:T(1,128)S(1)}, u32[]{:S(2)}, u32[]{:S(2)}) collective-permute-start(f32[1,2304]{1,0:T(1,128)S(1)} %add.66), channel_id=1, source_target_pairs={{0,2},{1,3},{2,0},{3,1},{4,6},{5,7},{6,4},{7,5},{8,10},{9,11},{10,... | collective-permute-start | bytes 27656 | tf_op jit(solution)/shard_map/rows_two/ppermute | solution.py:28
  47.7 2.2 %turn.1.turned_ref = bf16[512,2048]{1,0:T(8,128)(2,1)} custom-call(bf16[2048,512]{1,0:T(8,128)(2,1)S(1)} %copy-done.1), custom_call_target="tpu_custom_call" | custom-call | tf_op jit(solution)/shard_map/rows_two/turn/pallas_call | solution.py:381
  49.9 2.2 %col_sums.1 = (f32[1,2048]{1,0:T(1,128)S(1)}, f32[1,2048]{1,0:T(1,128)S(1)}, f32[1,2048]{1,0:T(1,128)S(1)}, f32[8,2048,256]{2,1,0:T(8,128)}) custom-call(f32[8,2048,256]{2,1,0:T(8,128)S(1)} %get-tuple-element.55.e_ref, f32[1,2304]{1,0:T(1,128)S(1)} %add.67.total_ref, f32[1,2048]{1,0:T(1,128)S(1)} %bitcast.12, ...), custom_call_target="tpu_custom_call", output_to_operand_aliasing={{3}: (3, {})} | custom-call | tf_op jit(solution)/shard_map/col_sums/pallas_call | solution.py:387
  52.5 0.5 copy-done
  53.0 2.6 %token_parts.5 = (bf16[2048,512]{1,0:T(8,128)(2,1)}, f32[8,2048,256]{2,1,0:T(8,128)}) custom-call(f32[8,2048,256]{2,1,0:T(8,128)S(1)} %get-tuple-element.55.e_ref, f32[1,2048]{1,0:T(1,128)S(1)} %get-tuple-element.62.alpha_ref, bf16[2048,512]{1,0:T(8,128)(2,1)S(1)} %copy-done, f32[8,2048,256]{2,1,0:T(8,128)} %get-tuple-element.63.refs_0_), custom_call_target="tpu_custom_call", output_to_operand_aliasing={{1}: (3, {})} | custom-call | tf_op jit(solution)/shard_map/cols_two/token_parts/pallas_call | solution.py:395
  55.9 0.6 collective-permute-start.5
  56.5 1.4 %token_parts.6 = (bf16[2048,512]{1,0:T(8,128)(2,1)}, f32[8,2048,256]{2,1,0:T(8,128)}) custom-call(f32[8,2048,256]{2,1,0:T(8,128)S(1)} %get-tuple-element.55.e_ref, f32[1,2048]{1,0:T(1,128)S(1)} %get-tuple-element.62.alpha_ref, bf16[2048,512]{1,0:T(8,128)(2,1)S(1)} %copy-done, ...), custom_call_target="tpu_custom_call", output_to_operand_aliasing={{1}: (3, {}), {0}: (4, {})} | custom-call | tf_op jit(solution)/shard_map/cols_two/token_parts/pallas_call | solution.py:395
  58.0 1.7 %collective-permute-done.5 = f32[1,2048]{1,0:T(1,128)S(1)} collective-permute-done((f32[1,2048]{1,0:T(1,128)S(1)}, f32[1,2048]{1,0:T(1,128)S(1)}, u32[]{:S(2)}, u32[]{:S(2)}) %collective-permute-start.5) | collective-permute-done | bytes 8224 | tf_op jit(solution)/shard_map/cols_two/ppermute | solution.py:37
  59.6 1.6 %collective-permute-start.6 = (f32[1,2048]{1,0:T(1,128)S(1)}, f32[1,2048]{1,0:T(1,128)S(1)}, u32[]{:S(2)}, u32[]{:S(2)}) collective-permute-start(f32[1,2048]{1,0:T(1,128)S(1)} %add.69), channel_id=1, source_target_pairs={{0,12},{4,8},{8,4},{12,0},{16,28},{20,24},{24,20},{28,16},{32,44},... | collective-permute-start | bytes 24584 | tf_op jit(solution)/shard_map/cols_two/ppermute | solution.py:37
  61.2 2.6 %token_parts.7 = (bf16[2048,512]{1,0:T(8,128)(2,1)}, f32[8,2048,256]{2,1,0:T(8,128)}) custom-call(f32[8,2048,256]{2,1,0:T(8,128)S(1)} %get-tuple-element.55.e_ref, f32[1,2048]{1,0:T(1,128)S(1)} %get-tuple-element.62.alpha_ref, bf16[2048,512]{1,0:T(8,128)(2,1)S(1)} %copy-done, ...), custom_call_target="tpu_custom_call", output_to_operand_aliasing={{1}: (3, {}), {0}: (4, {})} | custom-call | tf_op jit(solution)/shard_map/cols_two/token_parts/pallas_call | solution.py:395
  63.8 0.7 collective-permute-done.6
  64.6 0.5 collective-permute-start.7
  65.1 1.4 %token_parts.8 = (bf16[2048,512]{1,0:T(8,128)(2,1)}, f32[8,2048,256]{2,1,0:T(8,128)}) custom-call(f32[8,2048,256]{2,1,0:T(8,128)S(1)} %get-tuple-element.55.e_ref, f32[1,2048]{1,0:T(1,128)S(1)} %get-tuple-element.62.alpha_ref, bf16[2048,512]{1,0:T(8,128)(2,1)S(1)} %copy-done, ...), custom_call_target="tpu_custom_call", output_to_operand_aliasing={{1}: (3, {}), {0}: (4, {})} | custom-call | tf_op jit(solution)/shard_map/cols_two/token_parts/pallas_call | solution.py:395
  66.5 1.8 %collective-permute-done.7 = f32[1,2048]{1,0:T(1,128)S(1)} collective-permute-done((f32[1,2048]{1,0:T(1,128)S(1)}, f32[1,2048]{1,0:T(1,128)S(1)}, u32[]{:S(2)}, u32[]{:S(2)}) %collective-permute-start.7) | collective-permute-done | bytes 8224 | tf_op jit(solution)/shard_map/cols_two/ppermute | solution.py:37
  68.3 1.4 collective-permute-start.8
  69.7 2.2 %token_parts.9 = (bf16[2048,512]{1,0:T(8,128)(2,1)}, f32[8,2048,256]{2,1,0:T(8,128)}) custom-call(f32[8,2048,256]{2,1,0:T(8,128)S(1)} %get-tuple-element.55.e_ref, f32[1,2048]{1,0:T(1,128)S(1)} %get-tuple-element.62.alpha_ref, bf16[2048,512]{1,0:T(8,128)(2,1)S(1)} %copy-done, ...), custom_call_target="tpu_custom_call", output_to_operand_aliasing={{1}: (3, {}), {0}: (4, {})} | custom-call | tf_op jit(solution)/shard_map/cols_two/token_parts/pallas_call | solution.py:395
  71.9 1.4 collective-permute-done.8
  73.3 4.6 %all-to-all-start.1 = ((bf16[32,64,512]{2,1,0:T(8,128)(2,1)}), bf16[32,64,512]{2,1,0:T(8,128)(2,1)S(1)}, u32[]{:S(2)}, u32[]{:S(2)}) async-start(bf16[32,64,512]{2,1,0:T(8,128)(2,1)} %bitcast.16), calls=%async_computation.1 | async-start | bytes 4194304 | tf_op jit(solution)/shard_map/token_scatter/all_to_all | solution.py:416
  77.9 11.0 %frame_parts.1 = (f32[1,2048]{1,0:T(1,128)S(1)}, bf16[1024,512]{1,0:T(8,128)(2,1)S(1)}, bf16[1024,512]{1,0:T(8,128)(2,1)S(1)}) custom-call(s32[1]{0:T(128)} %bitcast.5.base_ref, f32[8,2048,256]{2,1,0:T(8,128)} %get-tuple-element.82.e_ref, f32[1,2048]{1,0:T(1,128)S(1)} %add.72.total_ref, f32[1,2048]{1,0:T(1,128)S(1)} %bitcast.14, ...), custom_call_target="tpu_custom_call" | custom-call | tf_op jit(solution)/shard_map/frame_rows/frame_parts/pallas_call | solution.py:422
  88.9 1.0 copy-done.2
  90.0 2.7 %collective-permute-done.9 = bf16[1024,512]{1,0:T(8,128)(2,1)} collective-permute-done((bf16[1024,512]{1,0:T(8,128)(2,1)S(1)}, bf16[1024,512]{1,0:T(8,128)(2,1)}, u32[]{:S(2)}, u32[]{:S(2)}) %collective-permute-start.9) | collective-permute-done | bytes 1048608 | tf_op jit(solution)/shard_map/frame_rows/ppermute | solution.py:28
  92.7 1.8 %add_convert_fusion.mine_ref = bf16[1024,512]{1,0:T(8,128)(2,1)S(1)} fusion(bf16[1024,512]{1,0:T(8,128)(2,1)} %collective-permute-done.9, bf16[1024,512]{1,0:T(8,128)(2,1)} %copy-done.2), kind=kLoop, calls=%fused_computation | loop fusion | flops 2097152 | bytes 3145728 | tf_op jit(solution)/shard_map/frame_rows/convert_element_type | solution.py:444
  94.5 6.9 %all-to-all-done.1.refs_0_.refs_1_.refs_2_.refs_3_ = bf16[32,64,512]{2,1,0:T(8,128)(2,1)S(1)} async-done(((bf16[32,64,512]{2,1,0:T(8,128)(2,1)}), bf16[32,64,512]{2,1,0:T(8,128)(2,1)S(1)}, u32[]{:S(2)}, u32[]{:S(2)}) %all-to-all-start.1) | async-done | bytes 2097184 | tf_op jit(solution)/shard_map/token_scatter/all_to_all | solution.py:416
  101.7 1.6 %collective-permute-start.10 = (bf16[64,512]{1,0:T(8,128)(2,1)S(1)}, bf16[64,512]{1,0:T(8,128)(2,1)S(1)}, u32[]{:S(2)}, u32[]{:S(2)}) collective-permute-start(bf16[64,512]{1,0:T(8,128)(2,1)S(1)} %sum_pieces.1.mine_ref), channel_id=1, source_target_pairs={{0,64},{4,68},{8,72},{12,76},{16,80},{20,84},{24,88},{28,92},{32,9... | collective-permute-start | bytes 196616 | tf_op jit(solution)/shard_map/token_sums/ppermute | solution.py:37
  103.3 3.4 %collective-permute-done.10.other_ref = bf16[64,512]{1,0:T(8,128)(2,1)S(1)} collective-permute-done((bf16[64,512]{1,0:T(8,128)(2,1)S(1)}, bf16[64,512]{1,0:T(8,128)(2,1)S(1)}, u32[]{:S(2)}, u32[]{:S(2)}) %collective-permute-start.10) | collective-permute-done | bytes 65568 | tf_op jit(solution)/shard_map/token_sums/ppermute | solution.py:37
  106.8 2.4 %collective-permute-start.11 = (bf16[1024,512]{1,0:T(8,128)(2,1)S(1)}, bf16[1024,512]{1,0:T(8,128)(2,1)S(1)}, u32[]{:S(2)}, u32[]{:S(2)}) collective-permute-start(bf16[1024,512]{1,0:T(8,128)(2,1)S(1)} %add_convert_fusion.mine_ref), channel_id=1, source_target_pairs={{0,2},{1,3},{2,0},{3,1},{4,6},{5,7},{6,4},{7,5},{8,10},{9,11},{10,... | collective-permute-start | bytes 3145736 | tf_op jit(solution)/shard_map/token_sums/ppermute | solution.py:28
  109.2 1.6 %deal_pieces.1 = bf16[16,128,512]{2,1,0:T(8,128)(2,1)} custom-call(s32[1]{0:T(128)} %bitcast.plane_ref, bf16[64,512]{1,0:T(8,128)(2,1)S(1)} %sum_pieces.1.mine_ref, bf16[64,512]{1,0:T(8,128)(2,1)S(1)} %collective-permute-done.10.other_ref), custom_call_target="tpu_custom_call" | custom-call | tf_op jit(solution)/shard_map/token_gather/deal_pieces/pallas_call | solution.py:458
  110.7 4.5 %all-to-all-start.2 = ((bf16[16,128,512]{2,1,0:T(8,128)(2,1)}), bf16[16,128,512]{2,1,0:T(8,128)(2,1)}, u32[]{:S(2)}, u32[]{:S(2)}) async-start(bf16[16,128,512]{2,1,0:T(8,128)(2,1)} %deal_pieces.1), calls=%async_computation.2 | async-start | bytes 4194304 | tf_op jit(solution)/shard_map/token_gather/all_to_all | solution.py:463
  115.3 1.2 collective-permute-done.12
  116.5 1.1 collective-permute-start.13
  117.6 11.3 %collective-permute-done.13 = f32[1,1024]{1,0:T(1,128)S(1)} collective-permute-done((f32[1,1024]{1,0:T(1,128)S(1)}, f32[1,1024]{1,0:T(1,128)S(1)}, u32[]{:S(2)}, u32[]{:S(2)}) %collective-permute-start.13) | collective-permute-done | bytes 4128 | tf_op jit(solution)/shard_map/frame_rows/ppermute | solution.py:28
  128.9 1.3 finish_frames.1
  130.4 0.5 collective-permute-start.15
  130.8 0.6 slice_reduce_fusion.1
  131.4 1.6 %collective-permute-done.15 = f32[1,1024]{1,0:T(1,128)S(1)} collective-permute-done((f32[1,1024]{1,0:T(1,128)S(1)}, f32[1,1024]{1,0:T(1,128)S(1)}, u32[]{:S(2)}, u32[]{:S(2)}) %collective-permute-start.15) | collective-permute-done | bytes 4128 | tf_op jit(solution)/shard_map/frame_sums/ppermute | solution.py:28
  133.0 0.7 maximum_multiply_fusion
  133.7 0.6 div.19
  134.3 1.0 constant_dynamic-update-slice_fusion
  135.3 5.8 %all-to-all-done.2.pieces_ref = bf16[16,128,512]{2,1,0:T(8,128)(2,1)} async-done(((bf16[16,128,512]{2,1,0:T(8,128)(2,1)}), bf16[16,128,512]{2,1,0:T(8,128)(2,1)}, u32[]{:S(2)}, u32[]{:S(2)}) %all-to-all-start.2) | async-done | bytes 2097184 | tf_op jit(solution)/shard_map/token_gather/all_to_all | solution.py:463
  141.1 2.7 %place_tokens.1 = bf16[2048,512]{1,0:T(8,128)(2,1)} custom-call(bf16[16,128,512]{2,1,0:T(8,128)(2,1)} %all-to-all-done.2.pieces_ref), custom_call_target="tpu_custom_call" | custom-call | tf_op jit(solution)/shard_map/frame_out/place_tokens/pallas_call | solution.py:481
  (40 shorter events, 1.8 us)
Async XLA Ops:
  0.6 15.6 %copy-start.3 = (f32[2048]{0:T(1024)S(1)}, f32[2048]{0:T(1024)}, u32[]{:S(2)}) copy-start(f32[2048]{0:T(1024)} %param.6) | copy-start | bytes 24580
  9.2 1.3 collective-permute-start
  10.5 5.7 %collective-permute-start.1 = (f32[1,2048]{1,0:T(1,128)S(1)}, f32[1,2048]{1,0:T(1,128)S(1)}, u32[]{:S(2)}, u32[]{:S(2)}) collective-permute-start(f32[1,2048]{1,0:T(1,128)S(1)} %multiply_add_fusion.2), channel_id=1, source_target_pairs={{0,2},{1,3},{2,0},{3,1},{4,6},{5,7},{6,4},{7,5},{8,10},{9,11},{10,... | collective-permute-start | bytes 24584 | tf_op jit(solution)/shard_map/rows_one/ppermute | solution.py:28
  16.2 22.3 %copy-start.4 = (f32[2048]{0:T(1024)S(1)}, f32[2048]{0:T(1024)}, u32[]{:S(2)}) copy-start(f32[2048]{0:T(1024)} %param.7) | copy-start | bytes 24580
  38.5 9.2 %copy-start.1 = (bf16[2048,512]{1,0:T(8,128)(2,1)S(1)}, bf16[2048,512]{1,0:T(8,128)(2,1)}, u32[]{:S(2)}) copy-start(bf16[2048,512]{1,0:T(8,128)(2,1)} %in_ref) | copy-start | bytes 6291460
  42.8 1.3 collective-permute-start.2
  44.1 5.8 %collective-permute-start.3 = (f32[1,2304]{1,0:T(1,128)S(1)}, f32[1,2304]{1,0:T(1,128)S(1)}, u32[]{:S(2)}, u32[]{:S(2)}) collective-permute-start(f32[1,2304]{1,0:T(1,128)S(1)} %add.66), channel_id=1, source_target_pairs={{0,2},{1,3},{2,0},{3,1},{4,6},{5,7},{6,4},{7,5},{8,10},{9,11},{10,... | collective-permute-start | bytes 27656 | tf_op jit(solution)/shard_map/rows_two/ppermute | solution.py:28
  49.9 3.1 %copy-start = (bf16[2048,512]{1,0:T(8,128)(2,1)S(1)}, bf16[2048,512]{1,0:T(8,128)(2,1)}, u32[]{:S(2)}) copy-start(bf16[2048,512]{1,0:T(8,128)(2,1)} %f_ref.9) | copy-start | bytes 6291460
  52.1 3.7 %collective-permute-start.4 = (f32[1,2048]{1,0:T(1,128)S(1)}, f32[1,2048]{1,0:T(1,128)S(1)}, u32[]{:S(2)}, u32[]{:S(2)}) collective-permute-start(f32[1,2048]{1,0:T(1,128)S(1)} %get-tuple-element.61), channel_id=1, source_target_pairs={{0,64},{4,68},{8,72},{12,76},{16,80},{20,84},{24,88},{28,92},{32,9... | collective-permute-start | bytes 24584 | tf_op jit(solution)/shard_map/cols_two/ppermute | solution.py:37
  55.9 3.7 %collective-permute-start.5 = (f32[1,2048]{1,0:T(1,128)S(1)}, f32[1,2048]{1,0:T(1,128)S(1)}, u32[]{:S(2)}, u32[]{:S(2)}) collective-permute-start(f32[1,2048]{1,0:T(1,128)S(1)} %add.68), channel_id=1, source_target_pairs={{0,4},{4,0},{8,12},{12,8},{16,20},{20,16},{24,28},{28,24},{32,36},... | collective-permute-start | bytes 24584 | tf_op jit(solution)/shard_map/cols_two/ppermute | solution.py:37
  59.6 4.9 %collective-permute-start.6 = (f32[1,2048]{1,0:T(1,128)S(1)}, f32[1,2048]{1,0:T(1,128)S(1)}, u32[]{:S(2)}, u32[]{:S(2)}) collective-permute-start(f32[1,2048]{1,0:T(1,128)S(1)} %add.69), channel_id=1, source_target_pairs={{0,12},{4,8},{8,4},{12,0},{16,28},{20,24},{24,20},{28,16},{32,44},... | collective-permute-start | bytes 24584 | tf_op jit(solution)/shard_map/cols_two/ppermute | solution.py:37
  64.6 3.7 %collective-permute-start.7 = (f32[1,2048]{1,0:T(1,128)S(1)}, f32[1,2048]{1,0:T(1,128)S(1)}, u32[]{:S(2)}, u32[]{:S(2)}) collective-permute-start(f32[1,2048]{1,0:T(1,128)S(1)} %add.70), channel_id=1, source_target_pairs={{0,16},{4,20},{8,24},{12,28},{16,0},{20,4},{24,8},{28,12},{32,48},... | collective-permute-start | bytes 24584 | tf_op jit(solution)/shard_map/cols_two/ppermute | solution.py:37
  68.3 4.9 %collective-permute-start.8 = (f32[1,2048]{1,0:T(1,128)S(1)}, f32[1,2048]{1,0:T(1,128)S(1)}, u32[]{:S(2)}, u32[]{:S(2)}) collective-permute-start(f32[1,2048]{1,0:T(1,128)S(1)} %add.71), channel_id=1, source_target_pairs={{0,48},{4,52},{8,56},{12,60},{16,32},{20,36},{24,40},{28,44},{32,1... | collective-permute-start | bytes 24584 | tf_op jit(solution)/shard_map/cols_two/ppermute | solution.py:37
  73.3 28.2 %all-to-all-start.1 = ((bf16[32,64,512]{2,1,0:T(8,128)(2,1)}), bf16[32,64,512]{2,1,0:T(8,128)(2,1)S(1)}, u32[]{:S(2)}, u32[]{:S(2)}) async-start(bf16[32,64,512]{2,1,0:T(8,128)(2,1)} %bitcast.16), calls=%async_computation.1 | async-start | bytes 4194304 | tf_op jit(solution)/shard_map/token_scatter/all_to_all | solution.py:416
  88.9 1.0 copy-start.2
  89.9 2.8 %collective-permute-start.9 = (bf16[1024,512]{1,0:T(8,128)(2,1)S(1)}, bf16[1024,512]{1,0:T(8,128)(2,1)}, u32[]{:S(2)}, u32[]{:S(2)}) collective-permute-start(bf16[1024,512]{1,0:T(8,128)(2,1)S(1)} %get-tuple-element.87), channel_id=1, source_target_pairs={{0,1},{1,0},{2,3},{3,2},{4,5},{5,4},{6,7},{7,6},{8,9},{9,8},{10,11... | collective-permute-start | bytes 3145736 | tf_op jit(solution)/shard_map/frame_rows/ppermute | solution.py:28
  101.7 5.0 %collective-permute-start.10 = (bf16[64,512]{1,0:T(8,128)(2,1)S(1)}, bf16[64,512]{1,0:T(8,128)(2,1)S(1)}, u32[]{:S(2)}, u32[]{:S(2)}) collective-permute-start(bf16[64,512]{1,0:T(8,128)(2,1)S(1)} %sum_pieces.1.mine_ref), channel_id=1, source_target_pairs={{0,64},{4,68},{8,72},{12,76},{16,80},{20,84},{24,88},{28,92},{32,9... | collective-permute-start | bytes 196616 | tf_op jit(solution)/shard_map/token_sums/ppermute | solution.py:37
  106.8 22.2 %collective-permute-start.11 = (bf16[1024,512]{1,0:T(8,128)(2,1)S(1)}, bf16[1024,512]{1,0:T(8,128)(2,1)S(1)}, u32[]{:S(2)}, u32[]{:S(2)}) collective-permute-start(bf16[1024,512]{1,0:T(8,128)(2,1)S(1)} %add_convert_fusion.mine_ref), channel_id=1, source_target_pairs={{0,2},{1,3},{2,0},{3,1},{4,6},{5,7},{6,4},{7,5},{8,10},{9,11},{10,... | collective-permute-start | bytes 3145736 | tf_op jit(solution)/shard_map/token_sums/ppermute | solution.py:28
  110.7 30.4 %all-to-all-start.2 = ((bf16[16,128,512]{2,1,0:T(8,128)(2,1)}), bf16[16,128,512]{2,1,0:T(8,128)(2,1)}, u32[]{:S(2)}, u32[]{:S(2)}) async-start(bf16[16,128,512]{2,1,0:T(8,128)(2,1)} %deal_pieces.1), calls=%async_computation.2 | async-start | bytes 4194304 | tf_op jit(solution)/shard_map/token_gather/all_to_all | solution.py:463
  115.2 1.2 collective-permute-start.12
  116.5 12.4 %collective-permute-start.13 = (f32[1,1024]{1,0:T(1,128)S(1)}, f32[1,1024]{1,0:T(1,128)S(1)}, u32[]{:S(2)}, u32[]{:S(2)}) collective-permute-start(f32[1,1024]{1,0:T(1,128)S(1)} %slice_add_fusion), channel_id=1, source_target_pairs={{0,2},{1,3},{2,0},{3,1},{4,6},{5,7},{6,4},{7,5},{8,10},{9,11},{10,... | collective-permute-start | bytes 12296 | tf_op jit(solution)/shard_map/frame_rows/ppermute | solution.py:28
  130.2 4.0 %collective-permute-start.14 = (bf16[1024,512]{1,0:T(8,128)(2,1)S(1)}, bf16[1024,512]{1,0:T(8,128)(2,1)S(1)}, u32[]{:S(2)}, u32[]{:S(2)}) collective-permute-start(bf16[1024,512]{1,0:T(8,128)(2,1)S(1)} %get-tuple-element.94), channel_id=1, source_target_pairs={{0,1},{1,0},{2,3},{3,2},{4,5},{5,4},{6,7},{7,6},{8,9},{9,8},{10,11... | collective-permute-start | bytes 3145736 | tf_op jit(solution)/shard_map/frame_out/ppermute | solution.py:28
  130.4 2.6 %collective-permute-start.15 = (f32[1,1024]{1,0:T(1,128)S(1)}, f32[1,1024]{1,0:T(1,128)S(1)}, u32[]{:S(2)}, u32[]{:S(2)}) collective-permute-start(f32[1,1024]{1,0:T(1,128)S(1)} %add.77.total_ref), channel_id=1, source_target_pairs={{0,1},{1,0},{2,3},{3,2},{4,5},{5,4},{6,7},{7,6},{8,9},{9,8},{10,11... | collective-permute-start | bytes 12296 | tf_op jit(solution)/shard_map/frame_sums/ppermute | solution.py:28

commit v7 on v6

--- a/solution.py
+++ b/solution.py
@@ -140,14 +140,18 @@
     return finish
 
 
-def second_rows(s_ref, all_ref, tm_ref, u_ref, sum_ref, e_ref, stored_ref, col_ref, sems):
+def second_rows(s_ref, parts_ref, tm_ref, u_ref, sum_ref, mass_ref, e_ref, stored_ref, col_ref, sems):
     i = pl.program_id(0)
     nt = s_ref.shape[1]
     nf = u_ref.shape[1]
 
     @pl.when(i == 0)
     def _():
-        column(log2(tm_ref[...]) - all_ref[...], col_ref)
+        parts = parts_ref[:, :nt]
+        highest = jnp.max(parts, axis=0, keepdims=True)
+        merged = highest + log2(jnp.sum(jnp.exp2(parts - highest), axis=0, keepdims=True))
+        column(log2(tm_ref[...]) - merged, col_ref)
+        mass_ref[...] = jnp.sum(parts_ref[:, nt:], axis=0, keepdims=True)
         sum_ref[:, nf:] = jnp.broadcast_to(jnp.sum(tm_ref[...]).reshape(1, 1), (1, EXTRA))
 
     u = u_ref[:, row_slice(i, W)]
@@ -366,15 +370,12 @@
     with jax.named_scope("cols_one"):
         lse = jnp.concatenate([lse, frame_total], axis=1)
         parts = lax.all_to_all(jnp.broadcast_to(lse[None], (n_ctx, 1, nt + 128)), "ctx", 0, 0)[:, 0]
-        highest = jnp.max(parts[:, :nt], axis=0, keepdims=True)
-        lse = highest + log2(jnp.sum(jnp.exp2(parts[:, :nt] - highest), axis=0, keepdims=True))
-        frame_total = jnp.sum(parts[:, nt])
-    part, e, stored = call(
-        second_rows, slabs, [VMEM, whole(1, nt), whole(1, nt), whole(1, nf)], [whole(1, nf + EXTRA), VMEM, hbm],
-        [f32(1, nf + EXTRA), kept, pltpu.HBM((slabs, nt, W), F32)],
+    part, frame_total, e, stored = call(
+        second_rows, slabs, [VMEM, whole(n_ctx, nt + 128), whole(1, nt), whole(1, nf)],
+        [whole(1, nf + EXTRA), whole(1, 128), VMEM, hbm], [f32(1, nf + EXTRA), f32(1, 128), kept, pltpu.HBM((slabs, nt, W), F32)],
         [pltpu.VMEM((nt, 128), F32), pltpu.SemaphoreType.DMA((EARLY, SPLIT))],
-        input_output_aliases={0: 1}, name="second_rows",
-    )(s, lse, tm, u)
+        input_output_aliases={0: 2}, name="second_rows",
+    )(s, parts, tm, u)
     with jax.named_scope("rows_two"):
         part = part + swap_tok(part, 1)
         tokens_later, part = lax.optimization_barrier((tokens, part))
@@ -467,7 +468,7 @@
         low = jnp.where(core == 0, my_sum, their_sum)
         high = jnp.where(core == 0, their_sum, my_sum)
         row_sum = jnp.concatenate([low, high], axis=1)[0]
-        mass_ratio = row_sum / (frame_mass / frame_total)
+        mass_ratio = row_sum / (frame_mass / frame_total[0, 0])
     with jax.named_scope("frame_out"):
         which = core.reshape(1).astype(jnp.int32)
         mine, frame_map = pl.pallas_call(

time: 144 us -> 144 us (level)
  no operation moved by 1% of the time
where the time goes in v7:
time: 144 us
  Pallas kernels  49.1 us (34%)
  waiting for transfers between devices  44 us (31%)
  starting transfers between devices  27.1 us (19%)
  blocking collectives  17.1 us (12%)
  local copies, waits for them, and re-layouts  2.78 us (2%)
  other arithmetic  2.71 us (2%)
    ppermute x10, waiting for transfers between devices, swap_tok(): lax.ppermute(value, 'tok', [(i, i ^ bit) for i in range(lax.axis_size('to...  21.3 us
    all_to_all x1, blocking collectives, shards(): lax.all_to_all(jnp.broadcast_to(lse[None], (n_ctx, 1, nt + 128)), 'ctx',...  17.1 us
    ppermute x10, starting transfers between devices, swap_tok(): lax.ppermute(value, 'tok', [(i, i ^ bit) for i in range(lax.axis_size('to...  12 us
    pallas_call x1, Pallas kernels, shards(): pl.pallas_call(frame_parts, grid=(slabs,), in_specs=[SMEM, hbm, whole(1,...  11 us
    pallas_call x5, Pallas kernels, some_token_parts(): call(functools.partial(token_parts, first, late), count, [VMEM, whole(1,...  10.3 us
    ppermute x6, waiting for transfers between devices, meet(): return lax.ppermute(value, 'ctx', pairs)  9.31 us
    pallas_call x1, Pallas kernels, shards(): call(functools.partial(first_rows, scale), slabs // PAIR, [pl.BlockSpec((...  8.55 us
    all_to_all x1, waiting for transfers between devices, shards(): pieces = lax.all_to_all(token_part.reshape(n_ctx, own, d), 'ctx', 0, 0)  6.91 us
  transfers between devices with their start and end apart: 18, of which 15 were waited for; matrix products, arithmetic and copies ran while one was open for 3% of the time, Pallas kernels for 18%

profile of v7, /device:TPU:0, one launch (start us, length us, event | category | flops | bytes accessed | tf_op | source)
XLA Modules:
  0.0 143.7 jit_solution(6813165196518661159)
XLA Ops:
  0.6 8.6 %first_rows.1 = (f32[1,2048]{1,0:T(1,128)S(1)}, f32[8,2048,256]{2,1,0:T(8,128)S(1)}) custom-call(bf16[2048,512]{1,0:T(8,128)(2,1)} %in_ref, bf16[2048,512]{1,0:T(8,128)(2,1)} %in_ref, bf16[2048,512]{1,0:T(8,128)(2,1)} %in_ref, bf16[2048,512]{1,0:T(8,128)(2,1)} %in_ref, bf16[2048,512]{1,0:T(8,128)(2,1)} %f_ref.9), custom_call_target="tpu_custom_call" | custom-call | tf_op jit(solution)/shard_map/first_rows/pallas_call | solution.py:358
  9.3 1.2 collective-permute-done
  10.5 4.0 %collective-permute-start.1 = (f32[1,2048]{1,0:T(1,128)S(1)}, f32[1,2048]{1,0:T(1,128)S(1)}, u32[]{:S(2)}, u32[]{:S(2)}) collective-permute-start(f32[1,2048]{1,0:T(1,128)S(1)} %multiply_add_fusion.1), channel_id=1, source_target_pairs={{0,2},{1,3},{2,0},{3,1},{4,6},{5,7},{6,4},{7,5},{8,10},{9,11},{10,... | collective-permute-start | bytes 24584 | tf_op jit(solution)/shard_map/rows_one/ppermute | solution.py:28
  14.5 1.6 %collective-permute-done.1 = f32[1,2048]{1,0:T(1,128)S(1)} collective-permute-done((f32[1,2048]{1,0:T(1,128)S(1)}, f32[1,2048]{1,0:T(1,128)S(1)}, u32[]{:S(2)}, u32[]{:S(2)}) %collective-permute-start.1) | collective-permute-done | bytes 8224 | tf_op jit(solution)/shard_map/rows_one/ppermute | solution.py:28
  16.2 4.8 %first_cols.1 = (f32[1,2048]{1,0:T(1,128)S(1)}, f32[1,2048]{1,0:T(1,128)S(1)}, f32[1,128]{1,0:T(1,128)S(1)}) custom-call(f32[8,2048,256]{2,1,0:T(8,128)S(1)} %get-tuple-element.51.s_ref, f32[1,2048]{1,0:T(1,128)S(1)} %multiply_add_fusion.all_ref, f32[1,2048]{1,0:T(1,128)S(1)} %bitcast.13), custom_call_target="tpu_custom_call" | custom-call | tf_op jit(solution)/shard_map/first_cols/pallas_call | solution.py:366
  21.2 17.1 %all_to_all.15 = f32[32,1,2176]{2,1,0:T(1,128)S(1)} all-to-all(f32[32,1,2176]{2,1,0:T(1,128)S(1)} %broadcast_in_dim.9), channel_id=1, replica_groups=mesh['ctx'=32,'tok'=4] {'ctx'}, dimensions={0} | all-to-all | bytes 557056 | tf_op jit(solution)/shard_map/cols_one/all_to_all | solution.py:372
  38.4 4.3 %second_rows.1 = (f32[1,2304]{1,0:T(1,128)S(1)}, f32[1,128]{1,0:T(1,128)S(1)}, f32[8,2048,256]{2,1,0:T(8,128)S(1)}, f32[8,2048,256]{2,1,0:T(8,128)}) custom-call(f32[8,2048,256]{2,1,0:T(8,128)S(1)} %get-tuple-element.51.s_ref, f32[32,2176]{1,0:T(8,128)S(1)} %bitcast.12, f32[1,2048]{1,0:T(1,128)S(1)} %bitcast.15, ...), custom_call_target="tpu_custom_call", output_to_operand_aliasing={{2}: (0, {})} | custom-call | tf_op jit(solution)/shard_map/second_rows/pallas_call | solution.py:373
  42.8 1.2 collective-permute-done.2
  44.0 3.7 %collective-permute-start.3 = (f32[1,2304]{1,0:T(1,128)S(1)}, f32[1,2304]{1,0:T(1,128)S(1)}, u32[]{:S(2)}, u32[]{:S(2)}) collective-permute-start(f32[1,2304]{1,0:T(1,128)S(1)} %add.59), channel_id=1, source_target_pairs={{0,2},{1,3},{2,0},{3,1},{4,6},{5,7},{6,4},{7,5},{8,10},{9,11},{10,... | collective-permute-start | bytes 27656 | tf_op jit(solution)/shard_map/rows_two/ppermute | solution.py:28
  47.6 2.2 %turn.1.turned_ref = bf16[512,2048]{1,0:T(8,128)(2,1)} custom-call(bf16[2048,512]{1,0:T(8,128)(2,1)S(1)} %copy-done.1), custom_call_target="tpu_custom_call" | custom-call | tf_op jit(solution)/shard_map/rows_two/turn/pallas_call | solution.py:382
  49.8 2.2 %col_sums.1 = (f32[1,2048]{1,0:T(1,128)S(1)}, f32[1,2048]{1,0:T(1,128)S(1)}, f32[1,2048]{1,0:T(1,128)S(1)}, f32[8,2048,256]{2,1,0:T(8,128)}) custom-call(f32[8,2048,256]{2,1,0:T(8,128)S(1)} %get-tuple-element.56.e_ref, f32[1,2304]{1,0:T(1,128)S(1)} %add.60.total_ref, f32[1,2048]{1,0:T(1,128)S(1)} %bitcast.14, ...), custom_call_target="tpu_custom_call", output_to_operand_aliasing={{3}: (3, {})} | custom-call | tf_op jit(solution)/shard_map/col_sums/pallas_call | solution.py:388
  52.0 0.3 collective-permute-start.4
  52.4 0.5 copy-done
  52.9 2.6 %token_parts.5 = (bf16[2048,512]{1,0:T(8,128)(2,1)}, f32[8,2048,256]{2,1,0:T(8,128)}) custom-call(f32[8,2048,256]{2,1,0:T(8,128)S(1)} %get-tuple-element.56.e_ref, f32[1,2048]{1,0:T(1,128)S(1)} %get-tuple-element.63.alpha_ref, bf16[2048,512]{1,0:T(8,128)(2,1)S(1)} %copy-done, f32[8,2048,256]{2,1,0:T(8,128)} %get-tuple-element.64.refs_0_), custom_call_target="tpu_custom_call", output_to_operand_aliasing={{1}: (3, {})} | custom-call | tf_op jit(solution)/shard_map/cols_two/token_parts/pallas_call | solution.py:396
  55.5 0.3 collective-permute-done.4
  55.8 0.6 collective-permute-start.5
  56.4 1.4 %token_parts.6 = (bf16[2048,512]{1,0:T(8,128)(2,1)}, f32[8,2048,256]{2,1,0:T(8,128)}) custom-call(f32[8,2048,256]{2,1,0:T(8,128)S(1)} %get-tuple-element.56.e_ref, f32[1,2048]{1,0:T(1,128)S(1)} %get-tuple-element.63.alpha_ref, bf16[2048,512]{1,0:T(8,128)(2,1)S(1)} %copy-done, ...), custom_call_target="tpu_custom_call", output_to_operand_aliasing={{1}: (3, {}), {0}: (4, {})} | custom-call | tf_op jit(solution)/shard_map/cols_two/token_parts/pallas_call | solution.py:396
  57.8 1.7 %collective-permute-done.5 = f32[1,2048]{1,0:T(1,128)S(1)} collective-permute-done((f32[1,2048]{1,0:T(1,128)S(1)}, f32[1,2048]{1,0:T(1,128)S(1)}, u32[]{:S(2)}, u32[]{:S(2)}) %collective-permute-start.5) | collective-permute-done | bytes 8224 | tf_op jit(solution)/shard_map/cols_two/ppermute | solution.py:37
  59.5 1.6 %collective-permute-start.6 = (f32[1,2048]{1,0:T(1,128)S(1)}, f32[1,2048]{1,0:T(1,128)S(1)}, u32[]{:S(2)}, u32[]{:S(2)}) collective-permute-start(f32[1,2048]{1,0:T(1,128)S(1)} %add.62), channel_id=1, source_target_pairs={{0,12},{4,8},{8,4},{12,0},{16,28},{20,24},{24,20},{28,16},{32,44},... | collective-permute-start | bytes 24584 | tf_op jit(solution)/shard_map/cols_two/ppermute | solution.py:37
  61.1 2.6 %token_parts.7 = (bf16[2048,512]{1,0:T(8,128)(2,1)}, f32[8,2048,256]{2,1,0:T(8,128)}) custom-call(f32[8,2048,256]{2,1,0:T(8,128)S(1)} %get-tuple-element.56.e_ref, f32[1,2048]{1,0:T(1,128)S(1)} %get-tuple-element.63.alpha_ref, bf16[2048,512]{1,0:T(8,128)(2,1)S(1)} %copy-done, ...), custom_call_target="tpu_custom_call", output_to_operand_aliasing={{1}: (3, {}), {0}: (4, {})} | custom-call | tf_op jit(solution)/shard_map/cols_two/token_parts/pallas_call | solution.py:396
  63.7 0.7 collective-permute-done.6
  64.5 0.5 collective-permute-start.7
  64.9 1.4 %token_parts.8 = (bf16[2048,512]{1,0:T(8,128)(2,1)}, f32[8,2048,256]{2,1,0:T(8,128)}) custom-call(f32[8,2048,256]{2,1,0:T(8,128)S(1)} %get-tuple-element.56.e_ref, f32[1,2048]{1,0:T(1,128)S(1)} %get-tuple-element.63.alpha_ref, bf16[2048,512]{1,0:T(8,128)(2,1)S(1)} %copy-done, ...), custom_call_target="tpu_custom_call", output_to_operand_aliasing={{1}: (3, {}), {0}: (4, {})} | custom-call | tf_op jit(solution)/shard_map/cols_two/token_parts/pallas_call | solution.py:396
  66.4 1.8 %collective-permute-done.7 = f32[1,2048]{1,0:T(1,128)S(1)} collective-permute-done((f32[1,2048]{1,0:T(1,128)S(1)}, f32[1,2048]{1,0:T(1,128)S(1)}, u32[]{:S(2)}, u32[]{:S(2)}) %collective-permute-start.7) | collective-permute-done | bytes 8224 | tf_op jit(solution)/shard_map/cols_two/ppermute | solution.py:37
  68.2 1.4 collective-permute-start.8
  69.6 2.2 %token_parts.9 = (bf16[2048,512]{1,0:T(8,128)(2,1)}, f32[8,2048,256]{2,1,0:T(8,128)}) custom-call(f32[8,2048,256]{2,1,0:T(8,128)S(1)} %get-tuple-element.56.e_ref, f32[1,2048]{1,0:T(1,128)S(1)} %get-tuple-element.63.alpha_ref, bf16[2048,512]{1,0:T(8,128)(2,1)S(1)} %copy-done, ...), custom_call_target="tpu_custom_call", output_to_operand_aliasing={{1}: (3, {}), {0}: (4, {})} | custom-call | tf_op jit(solution)/shard_map/cols_two/token_parts/pallas_call | solution.py:396
  71.8 1.4 collective-permute-done.8
  73.2 4.6 %all-to-all-start.1 = ((bf16[32,64,512]{2,1,0:T(8,128)(2,1)}), bf16[32,64,512]{2,1,0:T(8,128)(2,1)S(1)}, u32[]{:S(2)}, u32[]{:S(2)}) async-start(bf16[32,64,512]{2,1,0:T(8,128)(2,1)} %bitcast.18), calls=%async_computation.1 | async-start | bytes 4194304 | tf_op jit(solution)/shard_map/token_scatter/all_to_all | solution.py:417
  77.8 11.0 %frame_parts.1 = (f32[1,2048]{1,0:T(1,128)S(1)}, bf16[1024,512]{1,0:T(8,128)(2,1)S(1)}, bf16[1024,512]{1,0:T(8,128)(2,1)S(1)}) custom-call(s32[1]{0:T(128)} %bitcast.4.base_ref, f32[8,2048,256]{2,1,0:T(8,128)} %get-tuple-element.83.e_ref, f32[1,2048]{1,0:T(1,128)S(1)} %add.65.total_ref, f32[1,2048]{1,0:T(1,128)S(1)} %bitcast.16, ...), custom_call_target="tpu_custom_call" | custom-call | tf_op jit(solution)/shard_map/frame_rows/frame_parts/pallas_call | solution.py:423
  88.8 1.0 copy-done.2
  89.9 2.7 %collective-permute-done.9 = bf16[1024,512]{1,0:T(8,128)(2,1)} collective-permute-done((bf16[1024,512]{1,0:T(8,128)(2,1)S(1)}, bf16[1024,512]{1,0:T(8,128)(2,1)}, u32[]{:S(2)}, u32[]{:S(2)}) %collective-permute-start.9) | collective-permute-done | bytes 1048608 | tf_op jit(solution)/shard_map/frame_rows/ppermute | solution.py:28
  92.6 1.8 %add_convert_fusion.mine_ref = bf16[1024,512]{1,0:T(8,128)(2,1)S(1)} fusion(bf16[1024,512]{1,0:T(8,128)(2,1)} %collective-permute-done.9, bf16[1024,512]{1,0:T(8,128)(2,1)} %copy-done.2), kind=kLoop, calls=%fused_computation | loop fusion | flops 2097152 | bytes 3145728 | tf_op jit(solution)/shard_map/frame_rows/convert_element_type | solution.py:445
  94.4 6.9 %all-to-all-done.1.refs_0_.refs_1_.refs_2_.refs_3_ = bf16[32,64,512]{2,1,0:T(8,128)(2,1)S(1)} async-done(((bf16[32,64,512]{2,1,0:T(8,128)(2,1)}), bf16[32,64,512]{2,1,0:T(8,128)(2,1)S(1)}, u32[]{:S(2)}, u32[]{:S(2)}) %all-to-all-start.1) | async-done | bytes 2097184 | tf_op jit(solution)/shard_map/token_scatter/all_to_all | solution.py:417
  101.6 1.6 %collective-permute-start.10 = (bf16[64,512]{1,0:T(8,128)(2,1)S(1)}, bf16[64,512]{1,0:T(8,128)(2,1)S(1)}, u32[]{:S(2)}, u32[]{:S(2)}) collective-permute-start(bf16[64,512]{1,0:T(8,128)(2,1)S(1)} %sum_pieces.1.mine_ref), channel_id=1, source_target_pairs={{0,64},{4,68},{8,72},{12,76},{16,80},{20,84},{24,88},{28,92},{32,9... | collective-permute-start | bytes 196616 | tf_op jit(solution)/shard_map/token_sums/ppermute | solution.py:37
  103.2 3.4 %collective-permute-done.10.other_ref = bf16[64,512]{1,0:T(8,128)(2,1)S(1)} collective-permute-done((bf16[64,512]{1,0:T(8,128)(2,1)S(1)}, bf16[64,512]{1,0:T(8,128)(2,1)S(1)}, u32[]{:S(2)}, u32[]{:S(2)}) %collective-permute-start.10) | collective-permute-done | bytes 65568 | tf_op jit(solution)/shard_map/token_sums/ppermute | solution.py:37
  106.6 2.4 %collective-permute-start.11 = (bf16[1024,512]{1,0:T(8,128)(2,1)S(1)}, bf16[1024,512]{1,0:T(8,128)(2,1)S(1)}, u32[]{:S(2)}, u32[]{:S(2)}) collective-permute-start(bf16[1024,512]{1,0:T(8,128)(2,1)S(1)} %add_convert_fusion.mine_ref), channel_id=1, source_target_pairs={{0,2},{1,3},{2,0},{3,1},{4,6},{5,7},{6,4},{7,5},{8,10},{9,11},{10,... | collective-permute-start | bytes 3145736 | tf_op jit(solution)/shard_map/token_sums/ppermute | solution.py:28
  109.0 1.6 %deal_pieces.1 = bf16[16,128,512]{2,1,0:T(8,128)(2,1)} custom-call(s32[1]{0:T(128)} %bitcast.plane_ref, bf16[64,512]{1,0:T(8,128)(2,1)S(1)} %sum_pieces.1.mine_ref, bf16[64,512]{1,0:T(8,128)(2,1)S(1)} %collective-permute-done.10.other_ref), custom_call_target="tpu_custom_call" | custom-call | tf_op jit(solution)/shard_map/token_gather/deal_pieces/pallas_call | solution.py:459
  110.6 4.5 %all-to-all-start.2 = ((bf16[16,128,512]{2,1,0:T(8,128)(2,1)}), bf16[16,128,512]{2,1,0:T(8,128)(2,1)}, u32[]{:S(2)}, u32[]{:S(2)}) async-start(bf16[16,128,512]{2,1,0:T(8,128)(2,1)} %deal_pieces.1), calls=%async_computation.2 | async-start | bytes 4194304 | tf_op jit(solution)/shard_map/token_gather/all_to_all | solution.py:464
  115.2 1.2 collective-permute-done.12
  116.4 1.1 collective-permute-start.13
  117.4 11.3 %collective-permute-done.13 = f32[1,1024]{1,0:T(1,128)S(1)} collective-permute-done((f32[1,1024]{1,0:T(1,128)S(1)}, f32[1,1024]{1,0:T(1,128)S(1)}, u32[]{:S(2)}, u32[]{:S(2)}) %collective-permute-start.13) | collective-permute-done | bytes 4128 | tf_op jit(solution)/shard_map/frame_rows/ppermute | solution.py:28
  128.8 1.3 finish_frames.1
  130.2 0.5 collective-permute-start.15
  130.7 2.2 %collective-permute-done.15 = f32[1,1024]{1,0:T(1,128)S(1)} collective-permute-done((f32[1,1024]{1,0:T(1,128)S(1)}, f32[1,1024]{1,0:T(1,128)S(1)}, u32[]{:S(2)}, u32[]{:S(2)}) %collective-permute-start.15) | collective-permute-done | bytes 4128 | tf_op jit(solution)/shard_map/frame_sums/ppermute | solution.py:28
  132.9 0.6 div.19
  133.5 1.0 constant_dynamic-update-slice_fusion
  134.6 6.4 %all-to-all-done.2.pieces_ref = bf16[16,128,512]{2,1,0:T(8,128)(2,1)} async-done(((bf16[16,128,512]{2,1,0:T(8,128)(2,1)}), bf16[16,128,512]{2,1,0:T(8,128)(2,1)}, u32[]{:S(2)}, u32[]{:S(2)}) %all-to-all-start.2) | async-done | bytes 2097184 | tf_op jit(solution)/shard_map/token_gather/all_to_all | solution.py:464
  141.0 2.7 %place_tokens.1 = bf16[2048,512]{1,0:T(8,128)(2,1)} custom-call(bf16[16,128,512]{2,1,0:T(8,128)(2,1)} %all-to-all-done.2.pieces_ref), custom_call_target="tpu_custom_call" | custom-call | tf_op jit(solution)/shard_map/frame_out/place_tokens/pallas_call | solution.py:482
  (36 shorter events, 1.2 us)
Async XLA Ops:
  0.6 15.6 %copy-start.3 = (f32[2048]{0:T(1024)S(1)}, f32[2048]{0:T(1024)}, u32[]{:S(2)}) copy-start(f32[2048]{0:T(1024)} %param.6) | copy-start | bytes 24580
  9.2 1.3 collective-permute-start
  10.5 5.7 %collective-permute-start.1 = (f32[1,2048]{1,0:T(1,128)S(1)}, f32[1,2048]{1,0:T(1,128)S(1)}, u32[]{:S(2)}, u32[]{:S(2)}) collective-permute-start(f32[1,2048]{1,0:T(1,128)S(1)} %multiply_add_fusion.1), channel_id=1, source_target_pairs={{0,2},{1,3},{2,0},{3,1},{4,6},{5,7},{6,4},{7,5},{8,10},{9,11},{10,... | collective-permute-start | bytes 24584 | tf_op jit(solution)/shard_map/rows_one/ppermute | solution.py:28
  16.2 22.1 %copy-start.4 = (f32[2048]{0:T(1024)S(1)}, f32[2048]{0:T(1024)}, u32[]{:S(2)}) copy-start(f32[2048]{0:T(1024)} %param.7) | copy-start | bytes 24580
  38.4 9.2 %copy-start.1 = (bf16[2048,512]{1,0:T(8,128)(2,1)S(1)}, bf16[2048,512]{1,0:T(8,128)(2,1)}, u32[]{:S(2)}) copy-start(bf16[2048,512]{1,0:T(8,128)(2,1)} %in_ref) | copy-start | bytes 6291460
  42.7 1.3 collective-permute-start.2
  44.0 5.8 %collective-permute-start.3 = (f32[1,2304]{1,0:T(1,128)S(1)}, f32[1,2304]{1,0:T(1,128)S(1)}, u32[]{:S(2)}, u32[]{:S(2)}) collective-permute-start(f32[1,2304]{1,0:T(1,128)S(1)} %add.59), channel_id=1, source_target_pairs={{0,2},{1,3},{2,0},{3,1},{4,6},{5,7},{6,4},{7,5},{8,10},{9,11},{10,... | collective-permute-start | bytes 27656 | tf_op jit(solution)/shard_map/rows_two/ppermute | solution.py:28
  49.8 3.1 %copy-start = (bf16[2048,512]{1,0:T(8,128)(2,1)S(1)}, bf16[2048,512]{1,0:T(8,128)(2,1)}, u32[]{:S(2)}) copy-start(bf16[2048,512]{1,0:T(8,128)(2,1)} %f_ref.9) | copy-start | bytes 6291460
  52.0 3.7 %collective-permute-start.4 = (f32[1,2048]{1,0:T(1,128)S(1)}, f32[1,2048]{1,0:T(1,128)S(1)}, u32[]{:S(2)}, u32[]{:S(2)}) collective-permute-start(f32[1,2048]{1,0:T(1,128)S(1)} %get-tuple-element.62), channel_id=1, source_target_pairs={{0,64},{4,68},{8,72},{12,76},{16,80},{20,84},{24,88},{28,92},{32,9... | collective-permute-start | bytes 24584 | tf_op jit(solution)/shard_map/cols_two/ppermute | solution.py:37
  55.8 3.7 %collective-permute-start.5 = (f32[1,2048]{1,0:T(1,128)S(1)}, f32[1,2048]{1,0:T(1,128)S(1)}, u32[]{:S(2)}, u32[]{:S(2)}) collective-permute-start(f32[1,2048]{1,0:T(1,128)S(1)} %add.61), channel_id=1, source_target_pairs={{0,4},{4,0},{8,12},{12,8},{16,20},{20,16},{24,28},{28,24},{32,36},... | collective-permute-start | bytes 24584 | tf_op jit(solution)/shard_map/cols_two/ppermute | solution.py:37
  59.5 4.9 %collective-permute-start.6 = (f32[1,2048]{1,0:T(1,128)S(1)}, f32[1,2048]{1,0:T(1,128)S(1)}, u32[]{:S(2)}, u32[]{:S(2)}) collective-permute-start(f32[1,2048]{1,0:T(1,128)S(1)} %add.62), channel_id=1, source_target_pairs={{0,12},{4,8},{8,4},{12,0},{16,28},{20,24},{24,20},{28,16},{32,44},... | collective-permute-start | bytes 24584 | tf_op jit(solution)/shard_map/cols_two/ppermute | solution.py:37
  64.5 3.7 %collective-permute-start.7 = (f32[1,2048]{1,0:T(1,128)S(1)}, f32[1,2048]{1,0:T(1,128)S(1)}, u32[]{:S(2)}, u32[]{:S(2)}) collective-permute-start(f32[1,2048]{1,0:T(1,128)S(1)} %add.63), channel_id=1, source_target_pairs={{0,16},{4,20},{8,24},{12,28},{16,0},{20,4},{24,8},{28,12},{32,48},... | collective-permute-start | bytes 24584 | tf_op jit(solution)/shard_map/cols_two/ppermute | solution.py:37
  68.2 4.9 %collective-permute-start.8 = (f32[1,2048]{1,0:T(1,128)S(1)}, f32[1,2048]{1,0:T(1,128)S(1)}, u32[]{:S(2)}, u32[]{:S(2)}) collective-permute-start(f32[1,2048]{1,0:T(1,128)S(1)} %add.64), channel_id=1, source_target_pairs={{0,48},{4,52},{8,56},{12,60},{16,32},{20,36},{24,40},{28,44},{32,1... | collective-permute-start | bytes 24584 | tf_op jit(solution)/shard_map/cols_two/ppermute | solution.py:37
  73.2 28.1 %all-to-all-start.1 = ((bf16[32,64,512]{2,1,0:T(8,128)(2,1)}), bf16[32,64,512]{2,1,0:T(8,128)(2,1)S(1)}, u32[]{:S(2)}, u32[]{:S(2)}) async-start(bf16[32,64,512]{2,1,0:T(8,128)(2,1)} %bitcast.18), calls=%async_computation.1 | async-start | bytes 4194304 | tf_op jit(solution)/shard_map/token_scatter/all_to_all | solution.py:417
  88.8 1.0 copy-start.2
  89.8 2.8 %collective-permute-start.9 = (bf16[1024,512]{1,0:T(8,128)(2,1)S(1)}, bf16[1024,512]{1,0:T(8,128)(2,1)}, u32[]{:S(2)}, u32[]{:S(2)}) collective-permute-start(bf16[1024,512]{1,0:T(8,128)(2,1)S(1)} %get-tuple-element.88), channel_id=1, source_target_pairs={{0,1},{1,0},{2,3},{3,2},{4,5},{5,4},{6,7},{7,6},{8,9},{9,8},{10,11... | collective-permute-start | bytes 3145736 | tf_op jit(solution)/shard_map/frame_rows/ppermute | solution.py:28
  101.6 5.0 %collective-permute-start.10 = (bf16[64,512]{1,0:T(8,128)(2,1)S(1)}, bf16[64,512]{1,0:T(8,128)(2,1)S(1)}, u32[]{:S(2)}, u32[]{:S(2)}) collective-permute-start(bf16[64,512]{1,0:T(8,128)(2,1)S(1)} %sum_pieces.1.mine_ref), channel_id=1, source_target_pairs={{0,64},{4,68},{8,72},{12,76},{16,80},{20,84},{24,88},{28,92},{32,9... | collective-permute-start | bytes 196616 | tf_op jit(solution)/shard_map/token_sums/ppermute | solution.py:37
  106.6 22.2 %collective-permute-start.11 = (bf16[1024,512]{1,0:T(8,128)(2,1)S(1)}, bf16[1024,512]{1,0:T(8,128)(2,1)S(1)}, u32[]{:S(2)}, u32[]{:S(2)}) collective-permute-start(bf16[1024,512]{1,0:T(8,128)(2,1)S(1)} %add_convert_fusion.mine_ref), channel_id=1, source_target_pairs={{0,2},{1,3},{2,0},{3,1},{4,6},{5,7},{6,4},{7,5},{8,10},{9,11},{10,... | collective-permute-start | bytes 3145736 | tf_op jit(solution)/shard_map/token_sums/ppermute | solution.py:28
  110.6 30.4 %all-to-all-start.2 = ((bf16[16,128,512]{2,1,0:T(8,128)(2,1)}), bf16[16,128,512]{2,1,0:T(8,128)(2,1)}, u32[]{:S(2)}, u32[]{:S(2)}) async-start(bf16[16,128,512]{2,1,0:T(8,128)(2,1)} %deal_pieces.1), calls=%async_computation.2 | async-start | bytes 4194304 | tf_op jit(solution)/shard_map/token_gather/all_to_all | solution.py:464
  115.1 1.2 collective-permute-start.12
  116.4 12.4 %collective-permute-start.13 = (f32[1,1024]{1,0:T(1,128)S(1)}, f32[1,1024]{1,0:T(1,128)S(1)}, u32[]{:S(2)}, u32[]{:S(2)}) collective-permute-start(f32[1,1024]{1,0:T(1,128)S(1)} %slice_add_fusion), channel_id=1, source_target_pairs={{0,2},{1,3},{2,0},{3,1},{4,6},{5,7},{6,4},{7,5},{8,10},{9,11},{10,... | collective-permute-start | bytes 12296 | tf_op jit(solution)/shard_map/frame_rows/ppermute | solution.py:28
  130.1 3.4 %collective-permute-start.14 = (bf16[1024,512]{1,0:T(8,128)(2,1)S(1)}, bf16[1024,512]{1,0:T(8,128)(2,1)S(1)}, u32[]{:S(2)}, u32[]{:S(2)}) collective-permute-start(bf16[1024,512]{1,0:T(8,128)(2,1)S(1)} %get-tuple-element.95), channel_id=1, source_target_pairs={{0,1},{1,0},{2,3},{3,2},{4,5},{5,4},{6,7},{7,6},{8,9},{9,8},{10,11... | collective-permute-start | bytes 3145736 | tf_op jit(solution)/shard_map/frame_out/ppermute | solution.py:28
  130.2 2.7 %collective-permute-start.15 = (f32[1,1024]{1,0:T(1,128)S(1)}, f32[1,1024]{1,0:T(1,128)S(1)}, u32[]{:S(2)}, u32[]{:S(2)}) collective-permute-start(f32[1,1024]{1,0:T(1,128)S(1)} %add.70.total_ref), channel_id=1, source_target_pairs={{0,1},{1,0},{2,3},{3,2},{4,5},{5,4},{6,7},{7,6},{8,9},{9,8},{10,11... | collective-permute-start | bytes 12296 | tf_op jit(solution)/shard_map/frame_sums/ppermute | solution.py:28

commit v8 on v7

--- a/solution.py
+++ b/solution.py
@@ -89,13 +89,14 @@
         lse_ref[:, n * W : (n + 1) * W] = lse
 
 
-def first_cols(s_ref, all_ref, fm_ref, lse_ref, u_ref, mass_ref):
+def first_cols(s_ref, all_ref, fm_ref, lse_ref, u_ref):
     i = pl.program_id(0)
+    nt, count = s_ref.shape[1], lse_ref.shape[0]
 
     @pl.when(i == 0)
     def _():
         u_ref[...] = log2(fm_ref[...]) - all_ref[...]
-        mass_ref[...] = jnp.broadcast_to(jnp.sum(fm_ref[...]).reshape(1, 1), (1, 128))
+        lse_ref[:, :, nt:] = jnp.broadcast_to(jnp.sum(fm_ref[...]).reshape(1, 1, 1), (count, 1, 128))
 
     step = 16
     found = []
@@ -111,7 +112,8 @@
         top = jnp.max(highest, axis=1, keepdims=True)
         lse = top + log2(jnp.sum(total * jnp.exp2(highest - top), axis=1, keepdims=True))
         found.append(jnp.broadcast_to(lse, (step, 128)))
-    lse_ref[...] = jnp.concatenate(found).T[0:1]
+    row = jnp.concatenate(found).T[0:1]
+    lse_ref[:, :, row_slice(i, TOK)] = jnp.broadcast_to(row[None], (count, 1, TOK))
 
 
 def store(e_ref, stored_ref, sems, slabs):
@@ -363,13 +365,12 @@
     with jax.named_scope("rows_one"):
         lse = merge_lse([lse, swap_tok(lse, 1)])
         lse = merge_lse([lse, swap_tok(lse, 2)])
-    lse, u, frame_total = call(
-        first_cols, steps, [VMEM, whole(1, nf), whole(1, nf)], [lanes(TOK), whole(1, nf), whole(1, 128)],
-        [f32(1, nt), f32(1, nf), f32(1, 128)], name="first_cols",
+    lse, u = call(
+        first_cols, steps, [VMEM, whole(1, nf), whole(1, nf)], [whole(n_ctx, 1, nt + 128), whole(1, nf)],
+        [f32(n_ctx, 1, nt + 128), f32(1, nf)], name="first_cols",
     )(s, lse, fm)
     with jax.named_scope("cols_one"):
-        lse = jnp.concatenate([lse, frame_total], axis=1)
-        parts = lax.all_to_all(jnp.broadcast_to(lse[None], (n_ctx, 1, nt + 128)), "ctx", 0, 0)[:, 0]
+        parts = lax.all_to_all(lse, "ctx", 0, 0)[:, 0]
     part, frame_total, e, stored = call(
         second_rows, slabs, [VMEM, whole(n_ctx, nt + 128), whole(1, nt), whole(1, nf)],
         [whole(1, nf + EXTRA), whole(1, 128), VMEM, hbm], [f32(1, nf + EXTRA), f32(1, 128), kept, pltpu.HBM((slabs, nt, W), F32)],

time: 144 us -> 144 us (level)
  no operation moved by 1% of the time
where the time goes in v8:
time: 144 us
  Pallas kernels  49.3 us (34%)
  waiting for transfers between devices  44 us (31%)
  starting transfers between devices  27.1 us (19%)
  blocking collectives  17.1 us (12%)
  other arithmetic  2.66 us (2%)
  local copies, waits for them, and re-layouts  2.63 us (2%)
    ppermute x10, waiting for transfers between devices, swap_tok(): lax.ppermute(value, 'tok', [(i, i ^ bit) for i in range(lax.axis_size('to...  21.3 us
    all_to_all x1, blocking collectives, shards(): parts = lax.all_to_all(lse, 'ctx', 0, 0)[:, 0]  17.1 us
    ppermute x10, starting transfers between devices, swap_tok(): lax.ppermute(value, 'tok', [(i, i ^ bit) for i in range(lax.axis_size('to...  12 us
    pallas_call x1, Pallas kernels, shards(): pl.pallas_call(frame_parts, grid=(slabs,), in_specs=[SMEM, hbm, whole(1,...  11 us
    pallas_call x5, Pallas kernels, some_token_parts(): call(functools.partial(token_parts, first, late), count, [VMEM, whole(1,...  10.3 us
    ppermute x6, waiting for transfers between devices, meet(): return lax.ppermute(value, 'ctx', pairs)  9.3 us
    pallas_call x1, Pallas kernels, shards(): call(functools.partial(first_rows, scale), slabs // PAIR, [pl.BlockSpec((...  8.55 us
    all_to_all x1, waiting for transfers between devices, shards(): pieces = lax.all_to_all(token_part.reshape(n_ctx, own, d), 'ctx', 0, 0)  6.92 us
  transfers between devices with their start and end apart: 18, of which 15 were waited for; matrix products, arithmetic and copies ran while one was open for 3% of the time, Pallas kernels for 18%

profile of v8, /device:TPU:0, one launch (start us, length us, event | category | flops | bytes accessed | tf_op | source)
XLA Modules:
  0.0 143.7 jit_solution(17997647379937269474)
XLA Ops:
  0.6 8.6 %first_rows.1 = (f32[1,2048]{1,0:T(1,128)S(1)}, f32[8,2048,256]{2,1,0:T(8,128)S(1)}) custom-call(bf16[2048,512]{1,0:T(8,128)(2,1)} %in_ref, bf16[2048,512]{1,0:T(8,128)(2,1)} %in_ref, bf16[2048,512]{1,0:T(8,128)(2,1)} %in_ref, bf16[2048,512]{1,0:T(8,128)(2,1)} %in_ref, bf16[2048,512]{1,0:T(8,128)(2,1)} %f_ref.9), custom_call_target="tpu_custom_call" | custom-call | tf_op jit(solution)/shard_map/first_rows/pallas_call | solution.py:360
  9.3 1.2 collective-permute-done
  10.5 4.0 %collective-permute-start.1 = (f32[1,2048]{1,0:T(1,128)S(1)}, f32[1,2048]{1,0:T(1,128)S(1)}, u32[]{:S(2)}, u32[]{:S(2)}) collective-permute-start(f32[1,2048]{1,0:T(1,128)S(1)} %multiply_add_fusion.1), channel_id=1, source_target_pairs={{0,2},{1,3},{2,0},{3,1},{4,6},{5,7},{6,4},{7,5},{8,10},{9,11},{10,... | collective-permute-start | bytes 24584 | tf_op jit(solution)/shard_map/rows_one/ppermute | solution.py:28
  14.5 1.6 %collective-permute-done.1 = f32[1,2048]{1,0:T(1,128)S(1)} collective-permute-done((f32[1,2048]{1,0:T(1,128)S(1)}, f32[1,2048]{1,0:T(1,128)S(1)}, u32[]{:S(2)}, u32[]{:S(2)}) %collective-permute-start.1) | collective-permute-done | bytes 8224 | tf_op jit(solution)/shard_map/rows_one/ppermute | solution.py:28
  16.2 4.9 %first_cols.1 = (f32[32,1,2176]{2,1,0:T(1,128)S(1)}, f32[1,2048]{1,0:T(1,128)S(1)}) custom-call(f32[8,2048,256]{2,1,0:T(8,128)S(1)} %get-tuple-element.50.s_ref, f32[1,2048]{1,0:T(1,128)S(1)} %multiply_add_fusion.all_ref, f32[1,2048]{1,0:T(1,128)S(1)} %bitcast.13), custom_call_target="tpu_custom_call" | custom-call | tf_op jit(solution)/shard_map/first_cols/pallas_call | solution.py:368
  21.2 17.1 %all_to_all.15 = f32[32,1,2176]{2,1,0:T(1,128)S(1)} all-to-all(f32[32,1,2176]{2,1,0:T(1,128)S(1)} %get-tuple-element.52), channel_id=1, replica_groups=mesh['ctx'=32,'tok'=4] {'ctx'}, dimensions={0} | all-to-all | bytes 557056 | tf_op jit(solution)/shard_map/cols_one/all_to_all | solution.py:373
  38.3 4.3 %second_rows.1 = (f32[1,2304]{1,0:T(1,128)S(1)}, f32[1,128]{1,0:T(1,128)S(1)}, f32[8,2048,256]{2,1,0:T(8,128)S(1)}, f32[8,2048,256]{2,1,0:T(8,128)}) custom-call(f32[8,2048,256]{2,1,0:T(8,128)S(1)} %get-tuple-element.50.s_ref, f32[32,2176]{1,0:T(8,128)S(1)} %bitcast.12, f32[1,2048]{1,0:T(1,128)S(1)} %bitcast.15, ...), custom_call_target="tpu_custom_call", output_to_operand_aliasing={{2}: (0, {})} | custom-call | tf_op jit(solution)/shard_map/second_rows/pallas_call | solution.py:374
  42.7 1.2 collective-permute-done.2
  43.9 3.7 %collective-permute-start.3 = (f32[1,2304]{1,0:T(1,128)S(1)}, f32[1,2304]{1,0:T(1,128)S(1)}, u32[]{:S(2)}, u32[]{:S(2)}) collective-permute-start(f32[1,2304]{1,0:T(1,128)S(1)} %add.59), channel_id=1, source_target_pairs={{0,2},{1,3},{2,0},{3,1},{4,6},{5,7},{6,4},{7,5},{8,10},{9,11},{10,... | collective-permute-start | bytes 27656 | tf_op jit(solution)/shard_map/rows_two/ppermute | solution.py:28
  47.6 2.2 %turn.1.turned_ref = bf16[512,2048]{1,0:T(8,128)(2,1)} custom-call(bf16[2048,512]{1,0:T(8,128)(2,1)S(1)} %copy-done.1), custom_call_target="tpu_custom_call" | custom-call | tf_op jit(solution)/shard_map/rows_two/turn/pallas_call | solution.py:383
  49.8 2.2 %col_sums.1 = (f32[1,2048]{1,0:T(1,128)S(1)}, f32[1,2048]{1,0:T(1,128)S(1)}, f32[1,2048]{1,0:T(1,128)S(1)}, f32[8,2048,256]{2,1,0:T(8,128)}) custom-call(f32[8,2048,256]{2,1,0:T(8,128)S(1)} %get-tuple-element.54.e_ref, f32[1,2304]{1,0:T(1,128)S(1)} %add.60.total_ref, f32[1,2048]{1,0:T(1,128)S(1)} %bitcast.14, ...), custom_call_target="tpu_custom_call", output_to_operand_aliasing={{3}: (3, {})} | custom-call | tf_op jit(solution)/shard_map/col_sums/pallas_call | solution.py:389
  52.0 0.3 collective-permute-start.4
  52.3 0.5 copy-done
  52.8 2.6 %token_parts.5 = (bf16[2048,512]{1,0:T(8,128)(2,1)}, f32[8,2048,256]{2,1,0:T(8,128)}) custom-call(f32[8,2048,256]{2,1,0:T(8,128)S(1)} %get-tuple-element.54.e_ref, f32[1,2048]{1,0:T(1,128)S(1)} %get-tuple-element.61.alpha_ref, bf16[2048,512]{1,0:T(8,128)(2,1)S(1)} %copy-done, f32[8,2048,256]{2,1,0:T(8,128)} %get-tuple-element.62.refs_0_), custom_call_target="tpu_custom_call", output_to_operand_aliasing={{1}: (3, {})} | custom-call | tf_op jit(solution)/shard_map/cols_two/token_parts/pallas_call | solution.py:397
  55.4 0.3 collective-permute-done.4
  55.7 0.6 collective-permute-start.5
  56.4 1.4 %token_parts.6 = (bf16[2048,512]{1,0:T(8,128)(2,1)}, f32[8,2048,256]{2,1,0:T(8,128)}) custom-call(f32[8,2048,256]{2,1,0:T(8,128)S(1)} %get-tuple-element.54.e_ref, f32[1,2048]{1,0:T(1,128)S(1)} %get-tuple-element.61.alpha_ref, bf16[2048,512]{1,0:T(8,128)(2,1)S(1)} %copy-done, ...), custom_call_target="tpu_custom_call", output_to_operand_aliasing={{1}: (3, {}), {0}: (4, {})} | custom-call | tf_op jit(solution)/shard_map/cols_two/token_parts/pallas_call | solution.py:397
  57.8 1.7 %collective-permute-done.5 = f32[1,2048]{1,0:T(1,128)S(1)} collective-permute-done((f32[1,2048]{1,0:T(1,128)S(1)}, f32[1,2048]{1,0:T(1,128)S(1)}, u32[]{:S(2)}, u32[]{:S(2)}) %collective-permute-start.5) | collective-permute-done | bytes 8224 | tf_op jit(solution)/shard_map/cols_two/ppermute | solution.py:37
  59.5 1.6 %collective-permute-start.6 = (f32[1,2048]{1,0:T(1,128)S(1)}, f32[1,2048]{1,0:T(1,128)S(1)}, u32[]{:S(2)}, u32[]{:S(2)}) collective-permute-start(f32[1,2048]{1,0:T(1,128)S(1)} %add.62), channel_id=1, source_target_pairs={{0,12},{4,8},{8,4},{12,0},{16,28},{20,24},{24,20},{28,16},{32,44},... | collective-permute-start | bytes 24584 | tf_op jit(solution)/shard_map/cols_two/ppermute | solution.py:37
  61.1 2.6 %token_parts.7 = (bf16[2048,512]{1,0:T(8,128)(2,1)}, f32[8,2048,256]{2,1,0:T(8,128)}) custom-call(f32[8,2048,256]{2,1,0:T(8,128)S(1)} %get-tuple-element.54.e_ref, f32[1,2048]{1,0:T(1,128)S(1)} %get-tuple-element.61.alpha_ref, bf16[2048,512]{1,0:T(8,128)(2,1)S(1)} %copy-done, ...), custom_call_target="tpu_custom_call", output_to_operand_aliasing={{1}: (3, {}), {0}: (4, {})} | custom-call | tf_op jit(solution)/shard_map/cols_two/token_parts/pallas_call | solution.py:397
  63.7 0.7 collective-permute-done.6
  64.4 0.5 collective-permute-start.7
  64.9 1.4 %token_parts.8 = (bf16[2048,512]{1,0:T(8,128)(2,1)}, f32[8,2048,256]{2,1,0:T(8,128)}) custom-call(f32[8,2048,256]{2,1,0:T(8,128)S(1)} %get-tuple-element.54.e_ref, f32[1,2048]{1,0:T(1,128)S(1)} %get-tuple-element.61.alpha_ref, bf16[2048,512]{1,0:T(8,128)(2,1)S(1)} %copy-done, ...), custom_call_target="tpu_custom_call", output_to_operand_aliasing={{1}: (3, {}), {0}: (4, {})} | custom-call | tf_op jit(solution)/shard_map/cols_two/token_parts/pallas_call | solution.py:397
  66.3 1.8 %collective-permute-done.7 = f32[1,2048]{1,0:T(1,128)S(1)} collective-permute-done((f32[1,2048]{1,0:T(1,128)S(1)}, f32[1,2048]{1,0:T(1,128)S(1)}, u32[]{:S(2)}, u32[]{:S(2)}) %collective-permute-start.7) | collective-permute-done | bytes 8224 | tf_op jit(solution)/shard_map/cols_two/ppermute | solution.py:37
  68.2 1.4 collective-permute-start.8
  69.5 2.2 %token_parts.9 = (bf16[2048,512]{1,0:T(8,128)(2,1)}, f32[8,2048,256]{2,1,0:T(8,128)}) custom-call(f32[8,2048,256]{2,1,0:T(8,128)S(1)} %get-tuple-element.54.e_ref, f32[1,2048]{1,0:T(1,128)S(1)} %get-tuple-element.61.alpha_ref, bf16[2048,512]{1,0:T(8,128)(2,1)S(1)} %copy-done, ...), custom_call_target="tpu_custom_call", output_to_operand_aliasing={{1}: (3, {}), {0}: (4, {})} | custom-call | tf_op jit(solution)/shard_map/cols_two/token_parts/pallas_call | solution.py:397
  71.7 1.4 collective-permute-done.8
  73.1 4.6 %all-to-all-start.1 = ((bf16[32,64,512]{2,1,0:T(8,128)(2,1)}), bf16[32,64,512]{2,1,0:T(8,128)(2,1)S(1)}, u32[]{:S(2)}, u32[]{:S(2)}) async-start(bf16[32,64,512]{2,1,0:T(8,128)(2,1)} %bitcast.18), calls=%async_computation.1 | async-start | bytes 4194304 | tf_op jit(solution)/shard_map/token_scatter/all_to_all | solution.py:418
  77.7 11.0 %frame_parts.1 = (f32[1,2048]{1,0:T(1,128)S(1)}, bf16[1024,512]{1,0:T(8,128)(2,1)S(1)}, bf16[1024,512]{1,0:T(8,128)(2,1)S(1)}) custom-call(s32[1]{0:T(128)} %bitcast.4.base_ref, f32[8,2048,256]{2,1,0:T(8,128)} %get-tuple-element.81.e_ref, f32[1,2048]{1,0:T(1,128)S(1)} %add.65.total_ref, f32[1,2048]{1,0:T(1,128)S(1)} %bitcast.16, ...), custom_call_target="tpu_custom_call" | custom-call | tf_op jit(solution)/shard_map/frame_rows/frame_parts/pallas_call | solution.py:424
  88.8 1.0 copy-done.2
  89.8 2.7 %collective-permute-done.9 = bf16[1024,512]{1,0:T(8,128)(2,1)} collective-permute-done((bf16[1024,512]{1,0:T(8,128)(2,1)S(1)}, bf16[1024,512]{1,0:T(8,128)(2,1)}, u32[]{:S(2)}, u32[]{:S(2)}) %collective-permute-start.9) | collective-permute-done | bytes 1048608 | tf_op jit(solution)/shard_map/frame_rows/ppermute | solution.py:28
  92.5 1.8 %add_convert_fusion.mine_ref = bf16[1024,512]{1,0:T(8,128)(2,1)S(1)} fusion(bf16[1024,512]{1,0:T(8,128)(2,1)} %collective-permute-done.9, bf16[1024,512]{1,0:T(8,128)(2,1)} %copy-done.2), kind=kLoop, calls=%fused_computation | loop fusion | flops 2097152 | bytes 3145728 | tf_op jit(solution)/shard_map/frame_rows/convert_element_type | solution.py:446
  94.3 6.9 %all-to-all-done.1.refs_0_.refs_1_.refs_2_.refs_3_ = bf16[32,64,512]{2,1,0:T(8,128)(2,1)S(1)} async-done(((bf16[32,64,512]{2,1,0:T(8,128)(2,1)}), bf16[32,64,512]{2,1,0:T(8,128)(2,1)S(1)}, u32[]{:S(2)}, u32[]{:S(2)}) %all-to-all-start.1) | async-done | bytes 2097184 | tf_op jit(solution)/shard_map/token_scatter/all_to_all | solution.py:418
  101.5 1.6 %collective-permute-start.10 = (bf16[64,512]{1,0:T(8,128)(2,1)S(1)}, bf16[64,512]{1,0:T(8,128)(2,1)S(1)}, u32[]{:S(2)}, u32[]{:S(2)}) collective-permute-start(bf16[64,512]{1,0:T(8,128)(2,1)S(1)} %sum_pieces.1.mine_ref), channel_id=1, source_target_pairs={{0,64},{4,68},{8,72},{12,76},{16,80},{20,84},{24,88},{28,92},{32,9... | collective-permute-start | bytes 196616 | tf_op jit(solution)/shard_map/token_sums/ppermute | solution.py:37
  103.2 3.4 %collective-permute-done.10.other_ref = bf16[64,512]{1,0:T(8,128)(2,1)S(1)} collective-permute-done((bf16[64,512]{1,0:T(8,128)(2,1)S(1)}, bf16[64,512]{1,0:T(8,128)(2,1)S(1)}, u32[]{:S(2)}, u32[]{:S(2)}) %collective-permute-start.10) | collective-permute-done | bytes 65568 | tf_op jit(solution)/shard_map/token_sums/ppermute | solution.py:37
  106.6 2.4 %collective-permute-start.11 = (bf16[1024,512]{1,0:T(8,128)(2,1)S(1)}, bf16[1024,512]{1,0:T(8,128)(2,1)S(1)}, u32[]{:S(2)}, u32[]{:S(2)}) collective-permute-start(bf16[1024,512]{1,0:T(8,128)(2,1)S(1)} %add_convert_fusion.mine_ref), channel_id=1, source_target_pairs={{0,2},{1,3},{2,0},{3,1},{4,6},{5,7},{6,4},{7,5},{8,10},{9,11},{10,... | collective-permute-start | bytes 3145736 | tf_op jit(solution)/shard_map/token_sums/ppermute | solution.py:28
  109.0 1.6 %deal_pieces.1 = bf16[16,128,512]{2,1,0:T(8,128)(2,1)} custom-call(s32[1]{0:T(128)} %bitcast.plane_ref, bf16[64,512]{1,0:T(8,128)(2,1)S(1)} %sum_pieces.1.mine_ref, bf16[64,512]{1,0:T(8,128)(2,1)S(1)} %collective-permute-done.10.other_ref), custom_call_target="tpu_custom_call" | custom-call | tf_op jit(solution)/shard_map/token_gather/deal_pieces/pallas_call | solution.py:460
  110.6 4.5 %all-to-all-start.2 = ((bf16[16,128,512]{2,1,0:T(8,128)(2,1)}), bf16[16,128,512]{2,1,0:T(8,128)(2,1)}, u32[]{:S(2)}, u32[]{:S(2)}) async-start(bf16[16,128,512]{2,1,0:T(8,128)(2,1)} %deal_pieces.1), calls=%async_computation.2 | async-start | bytes 4194304 | tf_op jit(solution)/shard_map/token_gather/all_to_all | solution.py:465
  115.2 1.2 collective-permute-done.12
  116.3 1.1 collective-permute-start.13
  117.4 11.3 %collective-permute-done.13 = f32[1,1024]{1,0:T(1,128)S(1)} collective-permute-done((f32[1,1024]{1,0:T(1,128)S(1)}, f32[1,1024]{1,0:T(1,128)S(1)}, u32[]{:S(2)}, u32[]{:S(2)}) %collective-permute-start.13) | collective-permute-done | bytes 4128 | tf_op jit(solution)/shard_map/frame_rows/ppermute | solution.py:28
  128.8 1.3 finish_frames.1
  130.2 0.5 collective-permute-start.15
  130.7 2.2 %collective-permute-done.15 = f32[1,1024]{1,0:T(1,128)S(1)} collective-permute-done((f32[1,1024]{1,0:T(1,128)S(1)}, f32[1,1024]{1,0:T(1,128)S(1)}, u32[]{:S(2)}, u32[]{:S(2)}) %collective-permute-start.15) | collective-permute-done | bytes 4128 | tf_op jit(solution)/shard_map/frame_sums/ppermute | solution.py:28
  132.9 0.6 div.19
  133.5 1.0 constant_dynamic-update-slice_fusion
  134.5 6.4 %all-to-all-done.2.pieces_ref = bf16[16,128,512]{2,1,0:T(8,128)(2,1)} async-done(((bf16[16,128,512]{2,1,0:T(8,128)(2,1)}), bf16[16,128,512]{2,1,0:T(8,128)(2,1)}, u32[]{:S(2)}, u32[]{:S(2)}) %all-to-all-start.2) | async-done | bytes 2097184 | tf_op jit(solution)/shard_map/token_gather/all_to_all | solution.py:465
  141.0 2.7 %place_tokens.1 = bf16[2048,512]{1,0:T(8,128)(2,1)} custom-call(bf16[16,128,512]{2,1,0:T(8,128)(2,1)} %all-to-all-done.2.pieces_ref), custom_call_target="tpu_custom_call" | custom-call | tf_op jit(solution)/shard_map/frame_out/place_tokens/pallas_call | solution.py:483
  (34 shorter events, 1.0 us)
Async XLA Ops:
  0.6 15.6 %copy-start.3 = (f32[2048]{0:T(1024)S(1)}, f32[2048]{0:T(1024)}, u32[]{:S(2)}) copy-start(f32[2048]{0:T(1024)} %param.6) | copy-start | bytes 24580
  9.2 1.3 collective-permute-start
  10.5 5.7 %collective-permute-start.1 = (f32[1,2048]{1,0:T(1,128)S(1)}, f32[1,2048]{1,0:T(1,128)S(1)}, u32[]{:S(2)}, u32[]{:S(2)}) collective-permute-start(f32[1,2048]{1,0:T(1,128)S(1)} %multiply_add_fusion.1), channel_id=1, source_target_pairs={{0,2},{1,3},{2,0},{3,1},{4,6},{5,7},{6,4},{7,5},{8,10},{9,11},{10,... | collective-permute-start | bytes 24584 | tf_op jit(solution)/shard_map/rows_one/ppermute | solution.py:28
  16.2 22.1 %copy-start.4 = (f32[2048]{0:T(1024)S(1)}, f32[2048]{0:T(1024)}, u32[]{:S(2)}) copy-start(f32[2048]{0:T(1024)} %param.7) | copy-start | bytes 24580
  38.3 9.2 %copy-start.1 = (bf16[2048,512]{1,0:T(8,128)(2,1)S(1)}, bf16[2048,512]{1,0:T(8,128)(2,1)}, u32[]{:S(2)}) copy-start(bf16[2048,512]{1,0:T(8,128)(2,1)} %in_ref) | copy-start | bytes 6291460
  42.6 1.3 collective-permute-start.2
  43.9 5.8 %collective-permute-start.3 = (f32[1,2304]{1,0:T(1,128)S(1)}, f32[1,2304]{1,0:T(1,128)S(1)}, u32[]{:S(2)}, u32[]{:S(2)}) collective-permute-start(f32[1,2304]{1,0:T(1,128)S(1)} %add.59), channel_id=1, source_target_pairs={{0,2},{1,3},{2,0},{3,1},{4,6},{5,7},{6,4},{7,5},{8,10},{9,11},{10,... | collective-permute-start | bytes 27656 | tf_op jit(solution)/shard_map/rows_two/ppermute | solution.py:28
  49.8 3.1 %copy-start = (bf16[2048,512]{1,0:T(8,128)(2,1)S(1)}, bf16[2048,512]{1,0:T(8,128)(2,1)}, u32[]{:S(2)}) copy-start(bf16[2048,512]{1,0:T(8,128)(2,1)} %f_ref.9) | copy-start | bytes 6291460
  52.0 3.7 %collective-permute-start.4 = (f32[1,2048]{1,0:T(1,128)S(1)}, f32[1,2048]{1,0:T(1,128)S(1)}, u32[]{:S(2)}, u32[]{:S(2)}) collective-permute-start(f32[1,2048]{1,0:T(1,128)S(1)} %get-tuple-element.60), channel_id=1, source_target_pairs={{0,64},{4,68},{8,72},{12,76},{16,80},{20,84},{24,88},{28,92},{32,9... | collective-permute-start | bytes 24584 | tf_op jit(solution)/shard_map/cols_two/ppermute | solution.py:37
  55.7 3.7 %collective-permute-start.5 = (f32[1,2048]{1,0:T(1,128)S(1)}, f32[1,2048]{1,0:T(1,128)S(1)}, u32[]{:S(2)}, u32[]{:S(2)}) collective-permute-start(f32[1,2048]{1,0:T(1,128)S(1)} %add.61), channel_id=1, source_target_pairs={{0,4},{4,0},{8,12},{12,8},{16,20},{20,16},{24,28},{28,24},{32,36},... | collective-permute-start | bytes 24584 | tf_op jit(solution)/shard_map/cols_two/ppermute | solution.py:37
  59.5 4.9 %collective-permute-start.6 = (f32[1,2048]{1,0:T(1,128)S(1)}, f32[1,2048]{1,0:T(1,128)S(1)}, u32[]{:S(2)}, u32[]{:S(2)}) collective-permute-start(f32[1,2048]{1,0:T(1,128)S(1)} %add.62), channel_id=1, source_target_pairs={{0,12},{4,8},{8,4},{12,0},{16,28},{20,24},{24,20},{28,16},{32,44},... | collective-permute-start | bytes 24584 | tf_op jit(solution)/shard_map/cols_two/ppermute | solution.py:37
  64.4 3.7 %collective-permute-start.7 = (f32[1,2048]{1,0:T(1,128)S(1)}, f32[1,2048]{1,0:T(1,128)S(1)}, u32[]{:S(2)}, u32[]{:S(2)}) collective-permute-start(f32[1,2048]{1,0:T(1,128)S(1)} %add.63), channel_id=1, source_target_pairs={{0,16},{4,20},{8,24},{12,28},{16,0},{20,4},{24,8},{28,12},{32,48},... | collective-permute-start | bytes 24584 | tf_op jit(solution)/shard_map/cols_two/ppermute | solution.py:37
  68.2 4.9 %collective-permute-start.8 = (f32[1,2048]{1,0:T(1,128)S(1)}, f32[1,2048]{1,0:T(1,128)S(1)}, u32[]{:S(2)}, u32[]{:S(2)}) collective-permute-start(f32[1,2048]{1,0:T(1,128)S(1)} %add.64), channel_id=1, source_target_pairs={{0,48},{4,52},{8,56},{12,60},{16,32},{20,36},{24,40},{28,44},{32,1... | collective-permute-start | bytes 24584 | tf_op jit(solution)/shard_map/cols_two/ppermute | solution.py:37
  73.1 28.1 %all-to-all-start.1 = ((bf16[32,64,512]{2,1,0:T(8,128)(2,1)}), bf16[32,64,512]{2,1,0:T(8,128)(2,1)S(1)}, u32[]{:S(2)}, u32[]{:S(2)}) async-start(bf16[32,64,512]{2,1,0:T(8,128)(2,1)} %bitcast.18), calls=%async_computation.1 | async-start | bytes 4194304 | tf_op jit(solution)/shard_map/token_scatter/all_to_all | solution.py:418
  88.8 1.0 copy-start.2
  89.7 2.8 %collective-permute-start.9 = (bf16[1024,512]{1,0:T(8,128)(2,1)S(1)}, bf16[1024,512]{1,0:T(8,128)(2,1)}, u32[]{:S(2)}, u32[]{:S(2)}) collective-permute-start(bf16[1024,512]{1,0:T(8,128)(2,1)S(1)} %get-tuple-element.86), channel_id=1, source_target_pairs={{0,1},{1,0},{2,3},{3,2},{4,5},{5,4},{6,7},{7,6},{8,9},{9,8},{10,11... | collective-permute-start | bytes 3145736 | tf_op jit(solution)/shard_map/frame_rows/ppermute | solution.py:28
  101.5 5.0 %collective-permute-start.10 = (bf16[64,512]{1,0:T(8,128)(2,1)S(1)}, bf16[64,512]{1,0:T(8,128)(2,1)S(1)}, u32[]{:S(2)}, u32[]{:S(2)}) collective-permute-start(bf16[64,512]{1,0:T(8,128)(2,1)S(1)} %sum_pieces.1.mine_ref), channel_id=1, source_target_pairs={{0,64},{4,68},{8,72},{12,76},{16,80},{20,84},{24,88},{28,92},{32,9... | collective-permute-start | bytes 196616 | tf_op jit(solution)/shard_map/token_sums/ppermute | solution.py:37
  106.6 22.2 %collective-permute-start.11 = (bf16[1024,512]{1,0:T(8,128)(2,1)S(1)}, bf16[1024,512]{1,0:T(8,128)(2,1)S(1)}, u32[]{:S(2)}, u32[]{:S(2)}) collective-permute-start(bf16[1024,512]{1,0:T(8,128)(2,1)S(1)} %add_convert_fusion.mine_ref), channel_id=1, source_target_pairs={{0,2},{1,3},{2,0},{3,1},{4,6},{5,7},{6,4},{7,5},{8,10},{9,11},{10,... | collective-permute-start | bytes 3145736 | tf_op jit(solution)/shard_map/token_sums/ppermute | solution.py:28
  110.6 30.4 %all-to-all-start.2 = ((bf16[16,128,512]{2,1,0:T(8,128)(2,1)}), bf16[16,128,512]{2,1,0:T(8,128)(2,1)}, u32[]{:S(2)}, u32[]{:S(2)}) async-start(bf16[16,128,512]{2,1,0:T(8,128)(2,1)} %deal_pieces.1), calls=%async_computation.2 | async-start | bytes 4194304 | tf_op jit(solution)/shard_map/token_gather/all_to_all | solution.py:465
  115.1 1.2 collective-permute-start.12
  116.3 12.4 %collective-permute-start.13 = (f32[1,1024]{1,0:T(1,128)S(1)}, f32[1,1024]{1,0:T(1,128)S(1)}, u32[]{:S(2)}, u32[]{:S(2)}) collective-permute-start(f32[1,1024]{1,0:T(1,128)S(1)} %slice_add_fusion), channel_id=1, source_target_pairs={{0,2},{1,3},{2,0},{3,1},{4,6},{5,7},{6,4},{7,5},{8,10},{9,11},{10,... | collective-permute-start | bytes 12296 | tf_op jit(solution)/shard_map/frame_rows/ppermute | solution.py:28
  130.1 3.4 %collective-permute-start.14 = (bf16[1024,512]{1,0:T(8,128)(2,1)S(1)}, bf16[1024,512]{1,0:T(8,128)(2,1)S(1)}, u32[]{:S(2)}, u32[]{:S(2)}) collective-permute-start(bf16[1024,512]{1,0:T(8,128)(2,1)S(1)} %get-tuple-element.93), channel_id=1, source_target_pairs={{0,1},{1,0},{2,3},{3,2},{4,5},{5,4},{6,7},{7,6},{8,9},{9,8},{10,11... | collective-permute-start | bytes 3145736 | tf_op jit(solution)/shard_map/frame_out/ppermute | solution.py:28
  130.2 2.7 %collective-permute-start.15 = (f32[1,1024]{1,0:T(1,128)S(1)}, f32[1,1024]{1,0:T(1,128)S(1)}, u32[]{:S(2)}, u32[]{:S(2)}) collective-permute-start(f32[1,1024]{1,0:T(1,128)S(1)} %add.70.total_ref), channel_id=1, source_target_pairs={{0,1},{1,0},{2,3},{3,2},{4,5},{5,4},{6,7},{7,6},{8,9},{9,8},{10,11... | collective-permute-start | bytes 12296 | tf_op jit(solution)/shard_map/frame_sums/ppermute | solution.py:28
